TPU v7x, 32 devices: a whole 2x2x4 slice. The times are simulated.
32 devices in a mesh: dp: 8 (over z, y), tensor: 4 (over x, core).
Axes of the slice: x: 2, y: 2, z: 4, core: 2. Of those that a mesh axis runs over, the one named last changes fastest.
Arguments:
- tokens: bfloat16 [12608, 768], P(('dp', 'tensor')), may hold values from -6 to 6
- patch_mask: int32 [64, 197], P(('dp', 'tensor')), may hold values 0 or 1
- cotangent: bfloat16 [12608, 768], P(('dp', 'tensor')), may hold values from -6 to 6
- project_qkv: float32 [3, 768, 768], P(None, 'dp', 'tensor'), may hold values from -0.21875 to 0.21875
- first_qkv: float32 [3, 768, 768], P(None, 'dp', 'tensor'), may hold values from -320 to 320
- second_qkv: float32 [3, 768, 768], P(None, 'dp', 'tensor'), may hold values from 3152 to 12608
- project_out: float32 [768, 768], P('tensor', 'dp'), may hold values from -0.625 to 0.625
- first_out: float32 [768, 768], P('tensor', 'dp'), may hold values from -320 to 320
- second_out: float32 [768, 768], P('tensor', 'dp'), may hold values from 3152 to 12608
- expand_weight: float32 [768, 3072], P('dp', 'tensor'), may hold values from -0.21875 to 0.21875
- first_expand: float32 [768, 3072], P('dp', 'tensor'), may hold values from -320 to 320
- second_expand: float32 [768, 3072], P('dp', 'tensor'), may hold values from 3152 to 12608
- reduce_weight: float32 [3072, 768], P('tensor', 'dp'), may hold values from -0.109375 to 0.109375
- first_reduce: float32 [3072, 768], P('tensor', 'dp'), may hold values from -320 to 320
- second_reduce: float32 [3072, 768], P('tensor', 'dp'), may hold values from 3152 to 12608
- vectors: float32 [11, 768], P(None, 'dp'), may hold values from -2 to 2, as said below
- first_vectors: float32 [11, 768], P(None, 'dp'), may hold values from -320 to 320
- second_vectors: float32 [11, 768], P(None, 'dp'), may hold values from 3152 to 12608
- expand_bias: float32 [3072], P('dp'), may hold values from -3 to 3
- first_bias: float32 [3072], P('dp'), may hold values from -320 to 320
- second_bias: float32 [3072], P('dp'), may hold values from 3152 to 12608
Outputs:
- block_out: bfloat16 [12608, 768], P(('dp', 'tensor'))
- tokens_grad: bfloat16 [12608, 768], P(('dp', 'tensor'))
- new_qkv: float32 [3, 768, 768], P(None, 'dp', 'tensor')
- moment_qkv: float32 [3, 768, 768], P(None, 'dp', 'tensor')
- square_qkv: float32 [3, 768, 768], P(None, 'dp', 'tensor')
- new_out: float32 [768, 768], P('tensor', 'dp')
- moment_out: float32 [768, 768], P('tensor', 'dp')
- square_out: float32 [768, 768], P('tensor', 'dp')
- new_expand: float32 [768, 3072], P('dp', 'tensor')
- moment_expand: float32 [768, 3072], P('dp', 'tensor')
- square_expand: float32 [768, 3072], P('dp', 'tensor')
- new_reduce: float32 [3072, 768], P('tensor', 'dp')
- moment_reduce: float32 [3072, 768], P('tensor', 'dp')
- square_reduce: float32 [3072, 768], P('tensor', 'dp')
- new_vectors: float32 [11, 768], P(None, 'dp')
- moment_vectors: float32 [11, 768], P(None, 'dp')
- square_vectors: float32 [11, 768], P(None, 'dp')
- new_bias: float32 [3072], P('dp')
- moment_bias: float32 [3072], P('dp')
- square_bias: float32 [3072], P('dp')
Inputs may be any that keep to these rules, and one draw needn't show every extreme that they name: `patch_mask`: 1 marks a patch replaced by the mask token; the class row (position 0 of each image) is never replaced, whatever its entry. `vectors`: rows 0, 2, 4 and 5 (gains and layer scales) are positive, the other rows are biases and the mask token.
All inputs are finite; a program needn't handle non-finite values. No bound on the sum of `patch_mask` on one device may be relied on, other than what follows from the above.
Results may differ from a plain program's by a relative error of at most 0.01.
The roundings to bfloat16 on the way count: a program that leaves them out, or rounds other values in their place, can miss the bound.
Values may be sent and summed in bfloat16 or wider, within the bound.
No kernel may reach another device: no remote copies, remote signals or barrier semaphores. Data moves between devices by JAX's collectives and lax.ppermute only.
A program may use at most 128 MiB of HBM per device.

v0:
```python
import jax
import jax.numpy as jnp
from jax import lax
from jax.sharding import PartitionSpec as P

D = 768
HEAD_DIM = 64
FF = 3072
SEQ = 197
STEP = 4


BETA_ONE = 0.5
BETA_TWO = 0.5
EPSILON = 1e-08
DECAY = 0.05
RATE_MATRIX = 0.02
RATE_VECTOR = 0.2
NORM_EPS = 1e-06


def layer_norm(values, gain_row, shift_row):
    row_mean = jnp.mean(values, axis=-1, keepdims=True)
    centred = values - row_mean
    row_var = jnp.mean(centred * centred, axis=-1, keepdims=True)
    return centred * lax.rsqrt(row_var + NORM_EPS) * gain_row + shift_row


def exact_gelu(values):
    return jax.nn.gelu(values, approximate=False)


def adam_update(weight, gradient, first_moment, second, step_rate, decay_rate):
    moment = BETA_ONE * first_moment + (1.0 - BETA_ONE) * gradient
    square = BETA_TWO * second + (1.0 - BETA_TWO) * gradient * gradient
    first_hat = moment / (1.0 - BETA_ONE**STEP)
    second_hat = square / (1.0 - BETA_TWO**STEP)
    updated = weight - step_rate * (
        first_hat / (jnp.sqrt(second_hat) + EPSILON) + decay_rate * weight
    )
    return (updated, moment, square)


def attention_scores(query_heads, key_heads, score_scale):
    return (
        jnp.einsum("bqhd,bkhd->bhqk", query_heads, key_heads, preferred_element_type=jnp.float32)
        * score_scale
    )


def on_device(
    tokens,
    patch_mask,
    cotangent,
    project_qkv,
    first_qkv,
    second_qkv,
    project_out,
    first_out,
    second_out,
    expand_weight,
    first_expand,
    second_expand,
    reduce_weight,
    first_reduce,
    second_reduce,
    vectors,
    first_vectors,
    second_vectors,
    expand_bias,
    first_bias,
    second_bias,
):
    qkv_all, out_all, expand_all, reduce_all, vector_all, bias_all = (
        lax.all_gather(project_qkv.astype(jnp.bfloat16), "dp", axis=1, tiled=True),
        lax.all_gather(project_out.astype(jnp.bfloat16), "dp", axis=1, tiled=True),
        lax.all_gather(expand_weight.astype(jnp.bfloat16), "dp", axis=0, tiled=True),
        lax.all_gather(reduce_weight.astype(jnp.bfloat16), "dp", axis=1, tiled=True),
        lax.all_gather(vectors.astype(jnp.bfloat16), "dp", axis=1, tiled=True),
        lax.all_gather(expand_bias.astype(jnp.bfloat16), "dp", axis=0, tiled=True),
    )
    col_start = lax.axis_index("tensor") * qkv_all.shape[2]
    unit_start = lax.axis_index("tensor") * expand_all.shape[1]
    vector_rows = vector_all.astype(jnp.float32)
    head_cols = qkv_all.shape[2]
    unit_cols = expand_all.shape[1]
    bias_query = lax.dynamic_slice_in_dim(vector_rows[9], col_start, head_cols, 0)
    bias_value = lax.dynamic_slice_in_dim(vector_rows[10], col_start, head_cols, 0)
    bias_hidden = lax.dynamic_slice_in_dim(bias_all.astype(jnp.float32), unit_start, unit_cols, 0)
    positions = lax.broadcasted_iota(jnp.int32, patch_mask.shape, 1)
    replaced = (
        jnp.where((patch_mask == 1) & (positions > 0), 1.0, 0.0).astype(jnp.float32).reshape(-1, 1)
    )
    start_rows = tokens.astype(jnp.float32) * (1.0 - replaced) + vector_rows[6] * replaced
    normed_f32, norm_pull = jax.vjp(layer_norm, start_rows, vector_rows[0], vector_rows[1])
    normed = normed_f32.astype(jnp.bfloat16)
    normed_all = lax.all_gather(normed, "tensor", axis=0, tiled=True)
    queries = (
        jnp.dot(normed_all, qkv_all[0], preferred_element_type=jnp.float32) + bias_query
    ).astype(jnp.bfloat16)
    key_rows = jnp.dot(normed_all, qkv_all[1], preferred_element_type=jnp.float32).astype(
        jnp.bfloat16
    )
    value_rows = (
        jnp.dot(normed_all, qkv_all[2], preferred_element_type=jnp.float32) + bias_value
    ).astype(jnp.bfloat16)
    group_rows = normed_all.shape[0]
    head_shape = (group_rows // SEQ, SEQ, head_cols // HEAD_DIM, HEAD_DIM)
    score_scale = HEAD_DIM ** (-0.5)
    query_heads = queries.reshape(head_shape)
    key_heads = key_rows.reshape(head_shape)
    value_heads = value_rows.reshape(head_shape)
    scores = attention_scores(query_heads, key_heads, score_scale)
    row_max = jnp.max(scores, axis=-1, keepdims=True)
    row_total = jnp.sum(jnp.exp(scores - row_max), axis=-1, keepdims=True)
    log_total = row_max + jnp.log(row_total)
    soft_low = jnp.exp(scores - log_total).astype(jnp.bfloat16)
    attended = (
        jnp.einsum("bhqk,bkhd->bqhd", soft_low, value_heads, preferred_element_type=jnp.float32)
        .reshape(group_rows, head_cols)
        .astype(jnp.bfloat16)
    )
    row_piece = attended
    attn_out = lax.psum_scatter(
        jnp.dot(row_piece, out_all, preferred_element_type=jnp.float32),
        "tensor",
        scatter_dimension=0,
        tiled=True,
    )
    middle = start_rows + vector_rows[4] * (attn_out + vector_rows[7])
    normed_two_f32, norm_two_pull = jax.vjp(layer_norm, middle, vector_rows[2], vector_rows[3])
    normed_two = normed_two_f32.astype(jnp.bfloat16)
    normed_two_all = lax.all_gather(normed_two, "tensor", axis=0, tiled=True)
    hidden = jnp.dot(normed_two_all, expand_all, preferred_element_type=jnp.float32) + bias_hidden
    active_f32, gelu_pull = jax.vjp(exact_gelu, hidden)
    active = active_f32.astype(jnp.bfloat16)
    row_piece = active
    branch = lax.psum_scatter(
        jnp.dot(row_piece, reduce_all, preferred_element_type=jnp.float32),
        "tensor",
        scatter_dimension=0,
        tiled=True,
    )
    block_out = (middle + vector_rows[5] * (branch + vector_rows[8])).astype(jnp.bfloat16)
    grad_out = cotangent.astype(jnp.float32)
    grad_scale_two = jnp.sum(grad_out * (branch + vector_rows[8]), axis=0)
    grad_shift_out = jnp.sum(grad_out * vector_rows[5], axis=0)
    grad_branch = (grad_out * vector_rows[5]).astype(jnp.bfloat16)
    grad_branch_all = lax.all_gather(grad_branch, "tensor", axis=0, tiled=True)
    grad_active = jnp.dot(grad_branch_all, reduce_all.T, preferred_element_type=jnp.float32)
    grad_reduce = jnp.dot(active.T, grad_branch_all, preferred_element_type=jnp.float32)
    grad_hidden = gelu_pull(grad_active)[0].astype(jnp.bfloat16)
    grad_bias_hidden = jnp.sum(grad_hidden.astype(jnp.float32), axis=0)
    grad_expand = jnp.dot(normed_two_all.T, grad_hidden, preferred_element_type=jnp.float32)
    row_piece = grad_hidden
    grad_normed_two = lax.psum_scatter(
        jnp.dot(row_piece, expand_all.T, preferred_element_type=jnp.float32),
        "tensor",
        scatter_dimension=0,
        tiled=True,
    )
    grad_middle_part, grad_gain_two, grad_shift_two = norm_two_pull(grad_normed_two)
    grad_middle = grad_out + grad_middle_part
    grad_scale_one = jnp.sum(grad_middle * (attn_out + vector_rows[7]), axis=0)
    grad_shift_attn = jnp.sum(grad_middle * vector_rows[4], axis=0)
    grad_attn = (grad_middle * vector_rows[4]).astype(jnp.bfloat16)
    grad_attn_all = lax.all_gather(grad_attn, "tensor", axis=0, tiled=True)
    grad_attended = jnp.dot(grad_attn_all, out_all.T, preferred_element_type=jnp.float32).astype(
        jnp.bfloat16
    )
    grad_project_out = jnp.dot(attended.T, grad_attn_all, preferred_element_type=jnp.float32)
    soft_again = jnp.exp(attention_scores(query_heads, key_heads, score_scale) - log_total)
    grad_heads = grad_attended.reshape(head_shape)
    grad_soft = jnp.einsum(
        "bqhd,bkhd->bhqk", grad_heads, value_heads, preferred_element_type=jnp.float32
    )
    grad_values = (
        jnp.einsum(
            "bhqk,bqhd->bkhd",
            soft_again.astype(jnp.bfloat16),
            grad_heads,
            preferred_element_type=jnp.float32,
        )
        .reshape(group_rows, head_cols)
        .astype(jnp.bfloat16)
    )
    inner_sum = jnp.sum(soft_again * grad_soft, axis=-1, keepdims=True)
    grad_scores = (soft_again * (grad_soft - inner_sum)).astype(jnp.bfloat16)
    grad_queries = (
        (
            jnp.einsum(
                "bhqk,bkhd->bqhd", grad_scores, key_heads, preferred_element_type=jnp.float32
            )
            * score_scale
        )
        .reshape(group_rows, head_cols)
        .astype(jnp.bfloat16)
    )
    grad_keys = (
        (
            jnp.einsum(
                "bhqk,bqhd->bkhd", grad_scores, query_heads, preferred_element_type=jnp.float32
            )
            * score_scale
        )
        .reshape(group_rows, head_cols)
        .astype(jnp.bfloat16)
    )
    grad_qkv = jnp.stack(
        [
            jnp.dot(normed_all.T, grad_queries, preferred_element_type=jnp.float32),
            jnp.dot(normed_all.T, grad_keys, preferred_element_type=jnp.float32),
            jnp.dot(normed_all.T, grad_values, preferred_element_type=jnp.float32),
        ]
    )
    grad_bias_query = jnp.sum(grad_queries.astype(jnp.float32), axis=0)
    grad_bias_value = jnp.sum(grad_values.astype(jnp.float32), axis=0)
    total = jnp.dot(grad_queries, qkv_all[0].T, preferred_element_type=jnp.float32)
    total = total + jnp.dot(grad_keys, qkv_all[1].T, preferred_element_type=jnp.float32)
    grad_normed = lax.psum_scatter(
        total + jnp.dot(grad_values, qkv_all[2].T, preferred_element_type=jnp.float32),
        "tensor",
        scatter_dimension=0,
        tiled=True,
    )
    grad_start_part, grad_gain_one, grad_shift_one = norm_pull(grad_normed)
    grad_start = grad_middle + grad_start_part
    tokens_grad = (grad_start * (1.0 - replaced)).astype(jnp.bfloat16)
    grad_mask_token = jnp.sum(grad_start * replaced, axis=0)
    zero_cols = jnp.zeros((D,), jnp.float32)
    place_query = lax.dynamic_update_slice_in_dim(zero_cols, grad_bias_query, col_start, 0)
    place_value = lax.dynamic_update_slice_in_dim(zero_cols, grad_bias_value, col_start, 0)
    vector_grad = jnp.stack(
        [
            grad_gain_one,
            grad_shift_one,
            grad_gain_two,
            grad_shift_two,
            grad_scale_one,
            grad_scale_two,
            grad_mask_token,
            grad_shift_attn,
            grad_shift_out,
            place_query,
            place_value,
        ]
    )
    bias_grad = lax.dynamic_update_slice_in_dim(
        jnp.zeros((FF,), jnp.float32), grad_bias_hidden, unit_start, 0
    )
    vector_grad, bias_grad = lax.psum((vector_grad, bias_grad), "tensor")
    grad_qkv, grad_project_out, grad_expand, grad_reduce, vector_grad, bias_grad = (
        lax.psum_scatter(grad_qkv, "dp", scatter_dimension=1, tiled=True),
        lax.psum_scatter(grad_project_out, "dp", scatter_dimension=1, tiled=True),
        lax.psum_scatter(grad_expand, "dp", scatter_dimension=0, tiled=True),
        lax.psum_scatter(grad_reduce, "dp", scatter_dimension=1, tiled=True),
        lax.psum_scatter(vector_grad, "dp", scatter_dimension=1, tiled=True),
        lax.psum_scatter(bias_grad, "dp", scatter_dimension=0, tiled=True),
    )
    new_qkv, moment_qkv, square_qkv = adam_update(
        project_qkv, grad_qkv, first_qkv, second_qkv, RATE_MATRIX, DECAY
    )
    new_out, moment_out, square_out = adam_update(
        project_out, grad_project_out, first_out, second_out, RATE_MATRIX, DECAY
    )
    new_expand, moment_expand, square_expand = adam_update(
        expand_weight, grad_expand, first_expand, second_expand, RATE_MATRIX, DECAY
    )
    new_reduce, moment_reduce, square_reduce = adam_update(
        reduce_weight, grad_reduce, first_reduce, second_reduce, RATE_MATRIX, DECAY
    )
    new_vectors, moment_vectors, square_vectors = adam_update(
        vectors, vector_grad, first_vectors, second_vectors, RATE_VECTOR, 0.0
    )
    new_bias, moment_bias, square_bias = adam_update(
        expand_bias, bias_grad, first_bias, second_bias, RATE_VECTOR, 0.0
    )
    return (
        block_out,
        tokens_grad,
        new_qkv,
        moment_qkv,
        square_qkv,
        new_out,
        moment_out,
        square_out,
        new_expand,
        moment_expand,
        square_expand,
        new_reduce,
        moment_reduce,
        square_reduce,
        new_vectors,
        moment_vectors,
        square_vectors,
        new_bias,
        moment_bias,
        square_bias,
    )


def solution(mesh):
    placed = (
        P(("dp", "tensor"), None),
        P(("dp", "tensor"), None),
        P(("dp", "tensor"), None),
        P(None, "dp", "tensor"),
        P(None, "dp", "tensor"),
        P(None, "dp", "tensor"),
        P("tensor", "dp"),
        P("tensor", "dp"),
        P("tensor", "dp"),
        P("dp", "tensor"),
        P("dp", "tensor"),
        P("dp", "tensor"),
        P("tensor", "dp"),
        P("tensor", "dp"),
        P("tensor", "dp"),
        P(None, "dp"),
        P(None, "dp"),
        P(None, "dp"),
        P("dp"),
        P("dp"),
        P("dp"),
    )
    return jax.shard_map(
        on_device,
        mesh=mesh,
        in_specs=placed,
        out_specs=(
            P(("dp", "tensor"), None),
            P(("dp", "tensor"), None),
            P(None, "dp", "tensor"),
            P(None, "dp", "tensor"),
            P(None, "dp", "tensor"),
            P("tensor", "dp"),
            P("tensor", "dp"),
            P("tensor", "dp"),
            P("dp", "tensor"),
            P("dp", "tensor"),
            P("dp", "tensor"),
            P("tensor", "dp"),
            P("tensor", "dp"),
            P("tensor", "dp"),
            P(None, "dp"),
            P(None, "dp"),
            P(None, "dp"),
            P("dp"),
            P("dp"),
            P("dp"),
        ),
        check_vma=False,
    )
```

profile of v0, /device:TPU:1, one launch (start us, length us, event | category | flops | bytes accessed | tf_op | source)
XLA Modules:
  0.0 929.1 jit_solution(7131804730807135545)
XLA Ops:
  8.8 25.2 %all-gather = bf16[8,96,11]{1,2,0:T(8,128)(2,1)S(1)} all-gather(bf16[1,96,11]{1,2,0:T(8,128)(2,1)S(1)} %convert_bitcast_fusion), channel_id=1, replica_groups=mesh['dp'=8,'tensor'=4] {'dp'}, dimensions={0}, use_global_device_ids=true | all-gather | bytes 19008 | tf_op jit(solution)/shard_map/all_gather | solution.py:79
  42.1 27.2 %all_gather.33 = bf16[192,768]{0,1:T(8,128)(2,1)} all-gather(bf16[192,96]{0,1:T(8,128)(2,1)S(1)} %copy.115), channel_id=1, replica_groups=mesh['dp'=8,'tensor'=4] {'dp'}, dimensions={1}, use_global_device_ids=true | all-gather | bytes 331776 | tf_op jit(solution)/shard_map/all_gather | solution.py:76
  69.3 31.5 %all_gather.32 = bf16[3,768,192]{2,1,0:T(8,128)(2,1)} all-gather(bf16[3,96,192]{2,1,0:T(8,128)(2,1)S(1)} %convert_element_type.132), channel_id=1, replica_groups=mesh['dp'=8,'tensor'=4] {'dp'}, dimensions={1}, use_global_device_ids=true | all-gather | bytes 995328 | tf_op jit(solution)/shard_map/all_gather | solution.py:75
  129.4 62.7 %fusion = f32[400,768]{1,0:T(8,128)S(1)} fusion(f32[1576,768]{1,0:T(8,128)} %fusion.63), kind=kCustom, calls=%all-reduce-scatter | all-reduce-scatter fusion | flops 1228801 | bytes 6070784
  192.1 5.0 collective-permute-start
  208.3 21.3 %all-gather.3 = bf16[8,1,384]{2,1,0:T(2,128)(2,1)S(1)} all-gather(bf16[1,1,384]{2,1,0:T(2,128)(2,1)S(1)} %reshape.180), channel_id=1, replica_groups=mesh['dp'=8,'tensor'=4] {'dp'}, dimensions={0}, use_global_device_ids=true | all-gather | bytes 6912 | tf_op jit(solution)/shard_map/all_gather | solution.py:80
  239.2 33.2 %all-gather.13.cloned.1.call-done = bf16[768,768]{1,0:T(8,128)(2,1)} async-done(((bf16[96,768]{1,0:T(8,128)(2,1)}), bf16[768,768]{1,0:T(8,128)(2,1)}) %all-gather.13.cloned.1.call-update) | async-done | bytes 1179664 | tf_op jit(solution)/shard_map/all_gather | solution.py:77
  272.4 6.3 fusion.64
  278.6 36.2 %all-gather.15.cloned.1.call-done = bf16[768,768]{0,1:T(8,128)(2,1)} async-done(((bf16[768,96]{0,1:T(8,128)(2,1)}), bf16[768,768]{0,1:T(8,128)(2,1)}) %all-gather.15.cloned.1.call-update) | async-done | bytes 1179664 | tf_op jit(solution)/shard_map/all_gather | solution.py:78
  314.8 16.6 %convert_reduce_fusion = (f32[768]{0:T(1024)}, bf16[1576,768]{1,0:T(8,128)(2,1)S(1)}, f32[1576,768]{1,0:T(8,128)}) fusion(f32[1576,768]{1,0:T(8,128)} %fusion.64, f32[768]{0:T(1024)} %dynamic_slice.11, bf16[1576,768]{1,0:T(8,128)(2,1)} %reshape.183, bf16[768,768]{0,1:T(8,128)(2,1)} %all-gather.15.cloned.1.call-done), kind=kOutput, calls=%fused_computation.6 | convolution fusion | flops 1949902080 | bytes 15710208 | tf_op jit(solution)/shard_map/dot_general | solution.py:150
  337.2 47.1 %fusion.2 = f32[400,768]{1,0:T(8,128)} fusion(f32[1576,768]{1,0:T(8,128)} %fusion.66), kind=kCustom, calls=%all-reduce-scatter.2 | all-reduce-scatter fusion | flops 1228801 | bytes 6070784
  390.9 6.1 concatenate.2
  403.2 4.6 multiply_convert_fusion.1
  413.6 14.2 %all-gather.23.cloned.1.call-done = bf16[4,394,768]{2,1,0:T(8,128)(2,1)} async-done(((bf16[1,394,768]{2,1,0:T(8,128)(2,1)}), bf16[4,394,768]{2,1,0:T(8,128)(2,1)}) %all-gather.23.cloned.1.call-update) | async-done | bytes 2420752 | tf_op jit(solution)/shard_map/all_gather | solution.py:167
  471.3 85.1 %fusion.51 = (f32[400,768]{1,0:T(8,128)}, f32[400,768]{1,0:T(8,128)}) fusion(f32[1576,768]{1,0:T(8,128)} %fusion.65, f32[1576,768]{1,0:T(8,128)} %add_add_fusion), kind=kCustom, calls=%all-reduce-scatter.4 | all-reduce-scatter fusion | flops 2457601 | bytes 12141056
  565.3 5.2 concatenate.3
  580.8 6.3 fusion.67
  587.2 5.6 fusion.68
  610.8 30.1 %all-reduce.4 = f32[3072]{0:T(1024)S(1)} all-reduce(f32[3072]{0:T(1024)S(1)} %dynamic_update_slice.13), channel_id=11, replica_groups=mesh['dp'=8,'tensor'=4] {'dp'}, use_global_device_ids=true, to_apply=%region_34.35.clone | all-reduce | flops 3072 | bytes 24576
  641.8 15.5 %all-reduce.9 = (f32[11,96]{1,0:T(8,128)S(1)}, f32[384]{0:T(512)S(1)}) all-reduce(f32[11,96]{1,0:T(8,128)S(1)} %copy.143, f32[384]{0:T(512)S(1)} %dynamic-slice.11), channel_id=1, replica_groups=mesh['dp'=8,'tensor'=4] {'tensor'}, use_global_device_ids=true, to_apply=%region_30.31 | all-reduce | flops 1440 | bytes 11520 | tf_op jit(solution)/shard_map/psum | solution.py:251
  658.6 54.1 %reduce-scatter.20.cloned.1.call-done = f32[96,768]{1,0:T(8,128)} async-done(((f32[768,768]{1,0:T(8,128)}), f32[96,768]{1,0:T(8,128)}) %reduce-scatter.20.cloned.1.call-update) | async-done | bytes 294928 | tf_op jit(solution)/shard_map/reduce_scatter | solution.py:255
  714.7 69.7 %reduce-scatter.22.cloned.1.call-done = f32[768,96]{0,1:T(8,128)} async-done(((f32[768,768]{0,1:T(8,128)}), f32[768,96]{0,1:T(8,128)}) %reduce-scatter.22.cloned.1.call-update) | async-done | bytes 294928 | tf_op jit(solution)/shard_map/reduce_scatter | solution.py:256
  786.4 62.0 %reduce-scatter.26.cloned.1.call-done = f32[96,192]{1,0:T(8,128)} async-done(((f32[768,192]{1,0:T(8,128)}), f32[96,192]{1,0:T(8,128)}) %reduce-scatter.26.cloned.1.call-update) | async-done | bytes 73744
  850.1 67.9 %reduce-scatter.24.cloned.1.call-done = f32[96,576]{1,0:T(8,128)} async-done(((f32[768,576]{1,0:T(8,128)}), f32[96,576]{1,0:T(8,128)}) %reduce-scatter.24.cloned.1.call-update) | async-done | bytes 221200
  (311 shorter events, 173.8 us)
Async XLA Ops:
  7.2 93.7 %all-gather.17.cloned.1.call-start = ((), (), s32[]{:S(2)}) async-start(), calls=%async_computation.9 | async-start | bytes 3072000 | tf_op jit(solution)/shard_map/all_gather | solution.py:97
  40.8 190.8 %all-gather.21.cloned.1.call-start = ((), (), s32[]{:S(2)}) async-start(), calls=%async_computation.11 | async-start | bytes 3072000 | tf_op jit(solution)/shard_map/all_gather | solution.py:149
  41.9 193.5 %all-gather.19.cloned.1.call-start = ((), (), s32[]{:S(2)}) async-start(), calls=%async_computation.10 | async-start | bytes 3072000 | tf_op jit(solution)/shard_map/all_gather | solution.py:133
  192.1 6.4 collective-permute-start
  204.2 68.2 %all-gather.13.cloned.1.call-start = ((), (), s32[]{:S(2)}) async-start(), calls=%async_computation.5 | async-start | bytes 1327104 | tf_op jit(solution)/shard_map/all_gather | solution.py:77
  205.9 109.0 %all-gather.15.cloned.1.call-start = ((), (), s32[]{:S(2)}) async-start(), calls=%async_computation.6 | async-start | bytes 1327104 | tf_op jit(solution)/shard_map/all_gather | solution.py:78
  207.6 220.3 %all-gather.23.cloned.1.call-start = ((), (), s32[]{:S(2)}) async-start(), calls=%async_computation.12 | async-start | bytes 3072000 | tf_op jit(solution)/shard_map/all_gather | solution.py:167
  385.2 5.8 collective-permute-start.2
  403.2 237.7 %reduce-scatter.28.cloned.1.call-start = ((), (), s32[]{:S(2)}) async-start(), calls=%async_computation.15 | async-start | bytes 442368
  557.3 8.0 collective-permute-start.3
  562.8 12.4 %collective-permute-start.1 = (f32[18,768]{1,0:T(8,128)S(1)}, f32[18,768]{1,0:T(8,128)S(1)}, u32[]{:S(2)}, u32[]{:S(2)}) collective-permute-start(f32[18,768]{1,0:T(8,128)S(1)} %slice.80), channel_id=1, source_target_pairs={{0,1},{1,2},{2,3},{4,5},{5,6},{6,7},{8,9},{9,10},{10,11},{12,13},{... | collective-permute-start | bytes 165896
  580.7 132.0 %reduce-scatter.20.cloned.1.call-start = ((), (), s32[]{:S(2)}) async-start(), calls=%async_computation.7 | async-start | bytes 2654208 | tf_op jit(solution)/shard_map/reduce_scatter | solution.py:255
  587.2 197.2 %reduce-scatter.22.cloned.1.call-start = ((), (), s32[]{:S(2)}) async-start(), calls=%async_computation.8 | async-start | bytes 2654208 | tf_op jit(solution)/shard_map/reduce_scatter | solution.py:256
  592.8 255.6 %reduce-scatter.26.cloned.1.call-start = ((), (), s32[]{:S(2)}) async-start(), calls=%async_computation.14 | async-start | bytes 884736
  597.1 320.9 %reduce-scatter.24.cloned.1.call-start = ((), (), s32[]{:S(2)}) async-start(), calls=%async_computation.13 | async-start | bytes 2211840
  608.0 104.7 %copy-start.29 = (f32[96,768]{1,0:T(8,128)S(1)}, f32[96,768]{1,0:T(8,128)}, u32[]{:S(2)}) copy-start(f32[96,768]{1,0:T(8,128)} %param.30) | copy-start | bytes 884740
  608.0 104.7 %copy-start.37 = (f32[96,768]{1,0:T(8,128)S(1)}, f32[96,768]{1,0:T(8,128)}, u32[]{:S(2)}) copy-start(f32[96,768]{1,0:T(8,128)} %param.31) | copy-start | bytes 884740
  608.0 104.7 %copy-start.38 = (f32[96,768]{1,0:T(8,128)S(1)}, f32[96,768]{1,0:T(8,128)}, u32[]{:S(2)}) copy-start(f32[96,768]{1,0:T(8,128)} %param.32) | copy-start | bytes 884740
  608.0 176.4 %copy-start.30 = (f32[768,96]{0,1:T(8,128)S(1)}, f32[768,96]{0,1:T(8,128)}, u32[]{:S(2)}) copy-start(f32[768,96]{0,1:T(8,128)} %param.33) | copy-start | bytes 884740
  608.0 176.4 %copy-start.39 = (f32[768,96]{0,1:T(8,128)S(1)}, f32[768,96]{0,1:T(8,128)}, u32[]{:S(2)}) copy-start(f32[768,96]{0,1:T(8,128)} %param.34) | copy-start | bytes 884740
  608.1 176.3 %copy-start.40 = (f32[768,96]{0,1:T(8,128)S(1)}, f32[768,96]{0,1:T(8,128)}, u32[]{:S(2)}) copy-start(f32[768,96]{0,1:T(8,128)} %param.35) | copy-start | bytes 884740
  609.0 240.4 %copy-start.34 = (f32[192,96]{1,0:T(8,128)S(1)}, f32[192,96]{1,0:T(8,128)}, u32[]{:S(2)}) copy-start(f32[192,96]{1,0:T(8,128)} %param.27) | copy-start | bytes 221188
  609.0 240.3 %copy-start.41 = (f32[192,96]{1,0:T(8,128)S(1)}, f32[192,96]{1,0:T(8,128)}, u32[]{:S(2)}) copy-start(f32[192,96]{1,0:T(8,128)} %param.28) | copy-start | bytes 221188
  609.0 240.3 %copy-start.42 = (f32[192,96]{1,0:T(8,128)S(1)}, f32[192,96]{1,0:T(8,128)}, u32[]{:S(2)}) copy-start(f32[192,96]{1,0:T(8,128)} %param.29) | copy-start | bytes 221188
  (67 other events, 944.3 us)
Sparse Core Ops, SparseCore 0:
  41.0 32.2 all-gather.16
  75.4 24.6 all-gather.20
  204.3 25.9 all-gather.18
  232.9 39.3 all-gather.12
  275.0 39.8 all-gather.14
  403.3 24.5 all-gather.22
  580.8 59.5 reduce-scatter.27
  643.9 68.7 reduce-scatter.19
  716.2 68.1 reduce-scatter.21
  787.5 60.7 reduce-scatter.25
  852.3 65.7 reduce-scatter.23
where the time goes:
time: 936 us; the launch traced here: 929 us
  blocking collectives  346 us (37%)
  waiting for transfers between devices  339 us (36%)
  matrix products  85.7 us (9%)
  local copies, waits for them, and re-layouts  83.8 us (9%)
  other arithmetic  41.8 us (4%)
  between operations  16.8 us (2%)
  starting transfers between devices  16.5 us (2%)
    unnamed x4, blocking collectives  225 us
    unnamed x18, waiting for transfers between devices  131 us
    reduce_scatter x1, waiting for transfers between devices, on_device(): lax.psum_scatter(grad_reduce, 'dp', scatter_dimension=1, tiled=True)  69.7 us
    unnamed x182, local copies, waits for them, and re-layouts  54.2 us
    reduce_scatter x1, waiting for transfers between devices, on_device(): lax.psum_scatter(grad_expand, 'dp', scatter_dimension=0, tiled=True)  54.1 us
    all_gather x1, waiting for transfers between devices, on_device(): lax.all_gather(reduce_weight.astype(jnp.bfloat16), 'dp', axis=1, tiled=True)  36.2 us
    all_gather x1, waiting for transfers between devices, on_device(): lax.all_gather(expand_weight.astype(jnp.bfloat16), 'dp', axis=0, tiled=True)  33.2 us
    all_gather x1, blocking collectives, on_device(): lax.all_gather(project_qkv.astype(jnp.bfloat16), 'dp', axis=1, tiled=True)  31.5 us
  transfers between devices with their start and end apart: 15, of which 9 were waited for; matrix products, arithmetic and copies ran while one was open for 18% of the time, Pallas kernels for 0%

commit v1 on v0

v1 whole, which is shorter than its diff:
```python
import functools

import jax
import jax.numpy as jnp
import numpy as np
from jax import lax
from jax.experimental import pallas as pl
from jax.experimental.pallas import tpu as pltpu
from jax.sharding import PartitionSpec as P

D = 768
HEAD_DIM = 64
FF = 3072
SEQ = 197
STEP = 4
BETA_ONE = 0.5
BETA_TWO = 0.5
EPSILON = 1e-08
DECAY = 0.05
RATE_MATRIX = 0.02
RATE_VECTOR = 0.2
NORM_EPS = 1e-06

AXES = ("dp", "tensor")
PAD = 208
GROUPS = 4
GROUP_COLS = D // GROUPS
HEADS_IN_GROUP = GROUP_COLS // HEAD_DIM
BLOCKS = 8
BLOCK_ROWS = D // BLOCKS
EXTRA = 8
SCALE = HEAD_DIM**-0.5
F32 = jnp.float32
BF16 = jnp.bfloat16

BIT = {"c": 1, "x": 2, "y": 4, "1": 8, "2": 16}
GATHER = (("12yx", "12xy"), ("x12y", "y12x"), ("2xy1", "2yx1"))
SCATTER = (("12yx", "12xy"), ("x12y", "y12x"), ("2xy1", "2yx1"))


def offset_of(order, place):
    found = 0
    for level in range(4):
        if place >> level & 1:
            found ^= BIT[order[level]]
    return found


def pairs_of(orders, level):
    return [(dev, dev ^ BIT[orders[dev & 1][level]]) for dev in range(32)]


CORE_PAIRS = [(dev, dev ^ 1) for dev in range(32)]


def build_table(gather, scatter):
    table = np.zeros((32, 80), np.int32)
    for dev in range(32):
        core = dev & 1
        for place in range(16):
            table[dev, place] = dev ^ offset_of(gather[core], place)
            table[dev, 16 + place] = dev ^ 1 ^ offset_of(gather[1 - core], place)
            mine = dev ^ offset_of(gather[core], place)
            if mine & 3 == dev & 3:
                table[dev, 32 + (mine >> 2)] = place
            table[dev, 40 + (dev ^ offset_of(scatter[core], place))] = place
            table[dev, 40 + (dev ^ 1 ^ offset_of(scatter[1 - core], place))] = place
        table[dev, 72] = core
    return table


def plain_table():
    table = np.zeros((80,), np.int32)
    for place in range(32):
        table[place] = (place % 8) * 4 + place // 8
    for block in range(8):
        table[32 + block] = block
        for group in range(4):
            table[40 + block * 4 + group] = block * 2 + group // 2
    return table


def dot(left, right):
    return jnp.dot(left, right, preferred_element_type=F32)


def dot_rt(left, right):
    return lax.dot_general(left, right, (((1,), (1,)), ((), ())), preferred_element_type=F32)


def dot_lt(left, right):
    return lax.dot_general(left, right, (((0,), (0,)), ((), ())), preferred_element_type=F32)


def norm_stats(values):
    mean = jnp.mean(values, axis=-1, keepdims=True)
    centred = values - mean
    var = jnp.mean(centred * centred, axis=-1, keepdims=True)
    rstd = lax.rsqrt(var + NORM_EPS)
    return centred * rstd, rstd


def norm_back(grad, gain, unit, rstd):
    grad_unit = grad * gain
    first = jnp.mean(grad_unit, axis=-1, keepdims=True)
    second = jnp.mean(grad_unit * unit, axis=-1, keepdims=True)
    return rstd * (grad_unit - first - unit * second)


def col_sum(values):
    return jnp.sum(values, axis=0, keepdims=True)


def assemble(tab, parts, whole):
    for index, part in enumerate(parts):
        for place in range(8):
            owner = tab[index * 8 + place]
            row = pl.multiple_of((owner >> 2) * BLOCK_ROWS, BLOCK_ROWS)
            whole[owner & 3, pl.ds(row, BLOCK_ROWS), :] = part[place, 0:BLOCK_ROWS, :]


def put_blocks(tab, group, grad, out):
    for block in range(BLOCKS):
        place = tab[40 + block * 4 + group]
        rows = slice(block * BLOCK_ROWS, (block + 1) * BLOCK_ROWS)
        out[place] = grad[rows].astype(BF16)


def mask_rows(tok, rep, vec):
    replaced = rep[...]
    return tok[...].astype(F32) * (1.0 - replaced) + vec[6:7, :] * replaced


def pack_kernel(project_qkv, project_out, vectors, expand_bias, out):
    blank = jnp.zeros((EXTRA, D), F32)
    columns = [project_qkv[0], project_qkv[1], project_qkv[2], project_out[...].T]
    block = jnp.concatenate(columns, axis=1)
    fill = jnp.zeros((EXTRA, 128 - BLOCK_ROWS), F32)
    low = jnp.concatenate([vectors[0:8, :], fill], axis=1)
    high = jnp.concatenate([vectors[8:11, :], jnp.zeros((5, BLOCK_ROWS), F32)], axis=0)
    high = jnp.concatenate([high, fill], axis=1)
    last = jnp.concatenate([expand_bias[...], jnp.zeros((EXTRA - 1, 384), F32)], axis=0)
    extra = jnp.concatenate([low, high, last, blank[:, 640:768]], axis=1)
    out[...] = jnp.concatenate([block, extra], axis=0).astype(BF16)


def attend_kernel(
    imgs, tab, tok, rep, extra, b0, b1, b2, b3,
    vec, bias, w1, normed, qkv, soft, att, attn, mid, normed_two, qb, vb,
):
    low = jnp.zeros((8, D), F32)
    high = jnp.zeros((8, D), F32)
    fill = jnp.zeros((8, D - 128), F32)
    for block in range(BLOCKS):
        piece = extra[tab[32 + block]]
        low += pltpu.roll(jnp.concatenate([piece[:, 0:128], fill], 1), block * BLOCK_ROWS, 1)
        high += pltpu.roll(jnp.concatenate([piece[:, 128:256], fill], 1), block * BLOCK_ROWS, 1)
        half = (block % 2) * 384
        bias[block // 2, 0:1, half : half + 384] = piece[0:1, 256:640]
    vec[0:8, :] = low
    vec[8:16, :] = high
    for group in range(GROUPS):
        cols = slice(group * GROUP_COLS, (group + 1) * GROUP_COLS)
        qb[group, 0:1, :] = vec[9:10, cols]
        vb[group, 0:1, :] = vec[10:11, cols]
    assemble(tab, (b0, b1, b2, b3), w1)
    start = mask_rows(tok, rep, vec)
    unit, _ = norm_stats(start)
    normed[...] = (unit * vec[0:1, :] + vec[1:2, :]).astype(BF16)
    attn[...] = jnp.zeros_like(attn)
    keep = lax.broadcasted_iota(jnp.int32, (PAD, PAD), 1) < SEQ

    def step(group, carry):
        result = dot(normed[...], w1[group, :, 0:576])
        qkv[group, :, 0:192] = (result[:, 0:192] + qb[group, 0:1, :]).astype(BF16)
        qkv[group, :, 192:384] = result[:, 192:384].astype(BF16)
        qkv[group, :, 384:576] = (result[:, 384:576] + vb[group, 0:1, :]).astype(BF16)
        for head in range(HEADS_IN_GROUP):
            c0 = head * HEAD_DIM
            for img in range(imgs):
                rows = slice(img * PAD, (img + 1) * PAD)
                q = qkv[group, rows, c0 : c0 + 64]
                k = qkv[group, rows, 192 + c0 : 256 + c0]
                v = qkv[group, rows, 384 + c0 : 448 + c0]
                scores = jnp.where(keep, dot_rt(q, k) * SCALE, -1e30)
                top = jnp.max(scores, axis=-1, keepdims=True)
                raised = jnp.exp(scores - top)
                weights = raised / jnp.sum(raised, axis=-1, keepdims=True)
                soft[group * (HEADS_IN_GROUP * imgs) + head * imgs + img] = weights
                att[group, rows, c0 : c0 + 64] = dot(weights.astype(BF16), v).astype(BF16)
        attn[...] += dot_rt(att[group], w1[group, :, 576:768])
        return carry

    lax.fori_loop(0, GROUPS, step, 0)
    middle = start + vec[4:5, :] * (attn[...] + vec[7:8, :])
    mid[...] = middle
    unit_two, _ = norm_stats(middle)
    normed_two[...] = (unit_two * vec[2:3, :] + vec[3:4, :]).astype(BF16)


def expand_kernel(
    tab, normed_two, cot, vec, bias, b0, b1, b2, b3,
    w2, active, slope, grad_branch, own, sib,
):
    assemble(tab, (b0, b1, b2, b3), w2)
    grad_branch[...] = (cot[...].astype(F32) * vec[5:6, :]).astype(BF16)
    for part, out in ((1, sib), (0, own)):

        def step(along_x, carry, part=part, out=out):
            group = along_x * 2 + (tab[72] ^ part)
            hidden = dot(normed_two[...], w2[group]) + bias[group, 0:1, :]
            cdf = 0.5 * (1.0 + lax.erf(hidden * 0.7071067811865476))
            pdf = 0.3989422804014327 * jnp.exp(-0.5 * hidden * hidden)
            act = (hidden * cdf).astype(BF16)
            active[group] = act
            slope[group] = cdf + hidden * pdf
            put_blocks(tab, group, dot_lt(grad_branch[...], act), out)
            return carry

        lax.fori_loop(0, 2, step, 0)


def hidden_kernel(
    tab, normed_two, grad_branch, slope, b0, b1, b2, b3,
    w3, grad_hidden, bias_grad, own, sib,
):
    assemble(tab, (b0, b1, b2, b3), w3)
    for part, out in ((1, sib), (0, own)):

        def step(along_x, carry, part=part, out=out):
            group = along_x * 2 + (tab[72] ^ part)
            grad = (dot(grad_branch[...], w3[group]) * slope[group]).astype(BF16)
            grad_hidden[group] = grad
            bias_grad[group, 0:1, :] = col_sum(grad.astype(F32))
            put_blocks(tab, group, dot_lt(normed_two[...], grad), out)
            return carry

        lax.fori_loop(0, 2, step, 0)


def middle_kernel(
    active, grad_hidden, w2, w3, mid, attn, cot, vec,
    block_out, grad_mid, grad_attn, sums, branch, grad_two,
):
    branch[...] = jnp.zeros_like(branch)
    sums[...] = jnp.zeros_like(sums)
    grad_two[...] = jnp.zeros_like(grad_two)

    def step(group, carry):
        branch[...] += dot_rt(active[group], w3[group])
        grad_two[...] += dot_rt(grad_hidden[group], w2[group])
        return carry

    lax.fori_loop(0, GROUPS, step, 0)
    middle = mid[...]
    total = branch[...] + vec[8:9, :]
    block_out[...] = (middle + vec[5:6, :] * total).astype(BF16)
    grad_out = cot[...].astype(F32)
    sums[5:6, :] = col_sum(grad_out * total)
    sums[8:9, :] = col_sum(grad_out * vec[5:6, :])
    unit, rstd = norm_stats(middle)
    grad = grad_two[...]
    sums[2:3, :] = col_sum(grad * unit)
    sums[3:4, :] = col_sum(grad)
    grad_middle = grad_out + norm_back(grad, vec[2:3, :], unit, rstd)
    grad_mid[...] = grad_middle
    sums[4:5, :] = col_sum(grad_middle * (attn[...] + vec[7:8, :]))
    scaled = grad_middle * vec[4:5, :]
    sums[7:8, :] = col_sum(scaled)
    grad_attn[...] = scaled.astype(BF16)


def back_kernel(
    imgs, tab, tok, rep, vec, w1, normed, qkv, soft, att, grad_attn, grad_mid, sums_in, bias_grad,
    tok_grad, own, sib, dw, grad_one, gqkv, qb, vb, packed, sums,
):
    grad_one[...] = jnp.zeros_like(grad_one)

    def step(group, carry):
        grad_att = dot(grad_attn[...], w1[group, :, 576:768]).astype(BF16)
        for head in range(HEADS_IN_GROUP):
            c0 = head * HEAD_DIM
            for img in range(imgs):
                rows = slice(img * PAD, (img + 1) * PAD)
                q = qkv[group, rows, c0 : c0 + 64]
                k = qkv[group, rows, 192 + c0 : 256 + c0]
                v = qkv[group, rows, 384 + c0 : 448 + c0]
                weights = soft[group * (HEADS_IN_GROUP * imgs) + head * imgs + img]
                grad = grad_att[rows, c0 : c0 + 64]
                grad_soft = dot_rt(grad, v)
                grad_v = dot_lt(weights.astype(BF16), grad)
                inner = jnp.sum(weights * grad_soft, axis=-1, keepdims=True)
                grad_scores = (weights * (grad_soft - inner)).astype(BF16)
                grad_q = dot(grad_scores, k) * SCALE
                grad_k = dot_lt(grad_scores, q) * SCALE
                gqkv[rows, c0 : c0 + 64] = grad_q.astype(BF16)
                gqkv[rows, 192 + c0 : 256 + c0] = grad_k.astype(BF16)
                gqkv[rows, 384 + c0 : 448 + c0] = grad_v.astype(BF16)
        all_grads = gqkv[...]
        qb[group, 0:1, :] = col_sum(all_grads[:, 0:192].astype(F32))
        vb[group, 0:1, :] = col_sum(all_grads[:, 384:576].astype(F32))
        dw[group, :, 0:576] = dot_lt(normed[...], all_grads)
        dw[group, :, 576:768] = dot_lt(grad_attn[...], att[group])
        grad_one[...] += dot_rt(all_grads, w1[group, :, 0:576])
        return carry

    lax.fori_loop(0, GROUPS, step, 0)
    replaced = rep[...]
    unit, rstd = norm_stats(mask_rows(tok, rep, vec))
    grad = grad_one[...]
    sums[...] = sums_in[...]
    sums[0:1, :] = col_sum(grad * unit)
    sums[1:2, :] = col_sum(grad)
    grad_start = grad_mid[...] + norm_back(grad, vec[0:1, :], unit, rstd)
    tok_grad[...] = (grad_start * (1.0 - replaced)).astype(BF16)
    sums[6:7, :] = col_sum(grad_start * replaced)
    for group in range(GROUPS):
        cols = slice(group * GROUP_COLS, (group + 1) * GROUP_COLS)
        sums[9:10, cols] = qb[group, 0:1, :]
        sums[10:11, cols] = vb[group, 0:1, :]
    low = sums[0:8, :]
    high = sums[8:16, :]
    for block in range(BLOCKS):
        shift = (D - block * BLOCK_ROWS) % D
        packed[block] = jnp.zeros((EXTRA, D), F32)
        packed[block, :, 0:BLOCK_ROWS] = pltpu.roll(low, shift, 1)[:, 0:BLOCK_ROWS]
        packed[block, :, 128 : 128 + BLOCK_ROWS] = pltpu.roll(high, shift, 1)[:, 0:BLOCK_ROWS]
        half = (block % 2) * 384
        packed[block, 0:1, 256:640] = bias_grad[block // 2, 0:1, half : half + 384]
    for part, out in ((1, sib), (0, own)):
        for along_x in range(2):
            group = along_x * 2 + (tab[72] ^ part)
            for block in range(BLOCKS):
                place = tab[40 + block * 4 + group]
                rows = slice(block * BLOCK_ROWS, (block + 1) * BLOCK_ROWS)
                both = jnp.concatenate([dw[group, rows, :], packed[block]], axis=0)
                out[place] = both.astype(BF16)


VMEM = pl.BlockSpec(memory_space=pltpu.VMEM)
SMEM = pl.BlockSpec(memory_space=pltpu.SMEM)


def shape(dims, dtype=BF16):
    return jax.ShapeDtypeStruct(dims, dtype)


def call(kernel, args, outs, scratch=(), flops=0, moved=0, megabytes=48, table=True):
    return pl.pallas_call(
        kernel,
        out_shape=outs,
        in_specs=[SMEM] * table + [VMEM] * (len(args) - table),
        out_specs=[VMEM] * len(outs),
        scratch_shapes=list(scratch),
        cost_estimate=pl.CostEstimate(flops=flops, bytes_accessed=moved, transcendentals=0),
        compiler_params=pltpu.CompilerParams(vmem_limit_bytes=megabytes << 20),
    )(*args)


def adam_update(weight, gradient, first_moment, second, step_rate, decay_rate):
    moment = BETA_ONE * first_moment + (1.0 - BETA_ONE) * gradient
    square = BETA_TWO * second + (1.0 - BETA_TWO) * gradient * gradient
    first_hat = moment / (1.0 - BETA_ONE**STEP)
    second_hat = square / (1.0 - BETA_TWO**STEP)
    updated = weight - step_rate * (
        first_hat / (jnp.sqrt(second_hat) + EPSILON) + decay_rate * weight
    )
    return (updated, moment, square)


def gather_stream(block, orders):
    held = block[None]
    for level in range(4):
        taken = lax.ppermute(held, AXES, pairs_of(orders, level))
        if level < 3:
            held = jnp.concatenate([held, taken], axis=0)
    return (
        held,
        taken,
        lax.ppermute(held, AXES, CORE_PAIRS),
        lax.ppermute(taken, AXES, CORE_PAIRS),
    )


def scatter_stream(own, sib, orders, even):
    terms = [own, lax.ppermute(sib, AXES, CORE_PAIRS)]

    def total(low, high, last):
        found = terms[0][low:high].astype(F32)
        for index, term in enumerate(terms[1:]):
            found = found + term[low:high].astype(F32)
            if even and not (last and index == len(terms) - 2):
                found = lax.reduce_precision(found, 8, 7)
        return found

    for level in (3, 2, 1, 0):
        size = 1 << level
        sent = total(size, 2 * size, False).astype(BF16)
        terms.append(lax.ppermute(sent, AXES, pairs_of(orders, level)))
    return total(0, 1, True)[0]


def gather_plain(block):
    whole = lax.all_gather(block, AXES, axis=0, tiled=False)
    whole = whole.reshape(-1, GROUPS, *block.shape).transpose(1, 0, 2, 3)
    whole = whole.reshape(GROUPS, BLOCKS, BLOCK_ROWS, D)
    return tuple(whole[group] for group in range(GROUPS))


def scatter_plain(own, sib, n_dp):
    parts = jnp.stack([own, sib]).reshape(2, BLOCKS, 2, BLOCK_ROWS, D)
    whole = parts.transpose(1, 3, 2, 0, 4).reshape(D, GROUPS, D).astype(F32)
    whole = whole.reshape(n_dp, D // n_dp, GROUPS, D).transpose(0, 2, 1, 3)
    whole = whole.reshape(n_dp * GROUPS, D // n_dp, D)
    return lax.psum_scatter(whole, AXES, scatter_dimension=0, tiled=True)[0]


def on_device(
    n_dp,
    tokens,
    patch_mask,
    cotangent,
    project_qkv,
    first_qkv,
    second_qkv,
    project_out,
    first_out,
    second_out,
    expand_weight,
    first_expand,
    second_expand,
    reduce_weight,
    first_reduce,
    second_reduce,
    vectors,
    first_vectors,
    second_vectors,
    expand_bias,
    first_bias,
    second_bias,
):
    direct = n_dp == BLOCKS
    imgs = patch_mask.shape[0]
    rows = imgs * PAD
    wide = vectors.shape[1]
    piece_two = expand_weight.astype(BF16)
    piece_three = reduce_weight.astype(BF16).T
    if direct:
        flat = lax.axis_index("dp") * GROUPS + lax.axis_index("tensor")
        tables = [
            lax.dynamic_index_in_dim(jnp.asarray(build_table(g, s)), flat, 0, keepdims=False)
            for g, s in zip(GATHER, (SCATTER[0], SCATTER[2], SCATTER[1]), strict=True)
        ]
        (piece_one,) = call(
            pack_kernel,
            (project_qkv, project_out, vectors, expand_bias[None]),
            (shape((BLOCK_ROWS + EXTRA, D)),),
            table=False,
        )
        w1_parts = gather_stream(piece_one, GATHER[0])
        w2_parts = gather_stream(piece_two, GATHER[1])
        w3_parts = gather_stream(piece_three, GATHER[2])
        extras = jnp.concatenate(
            [w1_parts[0][:, BLOCK_ROWS:], w1_parts[1][:, BLOCK_ROWS:]], axis=0
        ).astype(F32)
    else:
        tables = [jnp.asarray(plain_table())] * 3
        piece_one = jnp.concatenate(
            [project_qkv[0], project_qkv[1], project_qkv[2], project_out.T], axis=1
        ).astype(BF16)
        w1_parts, w2_parts, w3_parts = (
            gather_plain(piece) for piece in (piece_one, piece_two, piece_three)
        )
        vector_all = lax.all_gather(vectors.astype(BF16), "dp", axis=1, tiled=True).astype(F32)
        bias_all = lax.all_gather(expand_bias.astype(BF16), "dp", axis=0, tiled=True).astype(F32)
        by_block = vector_all.reshape(11, BLOCKS, BLOCK_ROWS).transpose(1, 0, 2)
        extras = jnp.zeros((BLOCKS, EXTRA, D), F32)
        extras = extras.at[:, :, 0:BLOCK_ROWS].set(by_block[:, 0:8])
        extras = extras.at[:, 0:3, 128 : 128 + BLOCK_ROWS].set(by_block[:, 8:11])
        extras = extras.at[:, 0, 256:640].set(bias_all.reshape(BLOCKS, FF // BLOCKS))

    if direct:
        w1_parts, _ = lax.optimization_barrier((w1_parts, (w2_parts[0], w3_parts[0])))

    def padded(values):
        values = values.reshape(imgs, SEQ, -1)
        return jnp.pad(values, ((0, 0), (0, PAD - SEQ), (0, 0))).reshape(rows, -1)

    positions = lax.broadcasted_iota(jnp.int32, patch_mask.shape, 1)
    replaced = jnp.where((patch_mask == 1) & (positions > 0), 1.0, 0.0).astype(F32)
    rep = padded(replaced)
    tok = padded(tokens)
    cot = padded(cotangent)

    matmul = 2 * rows * D * D
    extra_rows = w1_parts[0].shape[1]
    full = (GROUPS, D, D)
    row_f32 = shape((rows, D), F32)
    row_low = shape((rows, D))
    n_soft = GROUPS * HEADS_IN_GROUP * imgs
    vec, bias, w1, normed, qkv, soft, att, attn, mid, normed_two = call(
        functools.partial(attend_kernel, imgs),
        (tables[0], tok, rep, extras, *w1_parts),
        (
            shape((16, D), F32),
            shape((GROUPS, 1, D), F32),
            shape(full),
            row_low,
            shape((GROUPS, rows, 3 * GROUP_COLS)),
            shape((n_soft, PAD, PAD), F32),
            shape((GROUPS, rows, GROUP_COLS)),
            row_f32,
            row_f32,
            row_low,
        ),
        (pltpu.VMEM((GROUPS, 1, GROUP_COLS), F32), pltpu.VMEM((GROUPS, 1, GROUP_COLS), F32)),
        flops=6 * matmul,
        moved=20_000_000,
    )
    half = shape((16, BLOCK_ROWS, D))
    w2, active, slope, grad_branch, reduce_own, reduce_sib = call(
        expand_kernel,
        (tables[1], normed_two, cot, vec, bias, *w2_parts),
        (
            shape(full),
            shape((GROUPS, rows, D)),
            shape((GROUPS, rows, D), F32),
            row_low,
            half,
            half,
        ),
        flops=8 * matmul,
        moved=20_000_000,
    )
    w3, grad_hidden, bias_grad, expand_own, expand_sib = call(
        hidden_kernel,
        (tables[2], normed_two, grad_branch, slope, *w3_parts),
        (
            shape(full),
            shape((GROUPS, rows, D)),
            shape((GROUPS, 1, D), F32),
            half,
            half,
        ),
        flops=8 * matmul,
        moved=20_000_000,
    )
    block_out, grad_mid, grad_attn, sums = call(
        middle_kernel,
        (active, grad_hidden, w2, w3, mid, attn, cot, vec),
        (row_low, row_f32, row_low, shape((16, D), F32)),
        (pltpu.VMEM((rows, D), F32), pltpu.VMEM((rows, D), F32)),
        flops=8 * matmul,
        moved=20_000_000,
        table=False,
    )
    block_rows = BLOCK_ROWS + EXTRA
    tok_grad, first_own, first_sib = call(
        functools.partial(back_kernel, imgs),
        (tables[0], tok, rep, vec, w1, normed, qkv, soft, att, grad_attn, grad_mid, sums, bias_grad),
        (row_low, shape((16, block_rows, D)), shape((16, block_rows, D))),
        (
            pltpu.VMEM(full, F32),
            pltpu.VMEM((rows, D), F32),
            pltpu.VMEM((rows, 3 * GROUP_COLS), BF16),
            pltpu.VMEM((GROUPS, 1, GROUP_COLS), F32),
            pltpu.VMEM((GROUPS, 1, GROUP_COLS), F32),
            pltpu.VMEM((BLOCKS, EXTRA, D), F32),
            pltpu.VMEM((16, D), F32),
        ),
        flops=12 * matmul,
        moved=30_000_000,
    )

    def cut(values):
        return values.reshape(imgs, PAD, D)[:, :SEQ].reshape(imgs * SEQ, D)

    if direct:
        grad_three = scatter_stream(reduce_own, reduce_sib, SCATTER[2], False)
        grad_two = scatter_stream(expand_own, expand_sib, SCATTER[1], False)
        both = scatter_stream(first_own, first_sib, SCATTER[0], True)
        grad_one, mine = both[:BLOCK_ROWS], both[BLOCK_ROWS:]
        other = lax.ppermute(mine, AXES, CORE_PAIRS)
        mine = jnp.where(lax.axis_index("tensor") % 2 == 0, mine, other)
        vector_grad = jnp.concatenate([mine[:, 0:wide], mine[0:3, 128 : 128 + wide]], axis=0)
        grad_bias = mine[0, 256:640]
    else:
        grad_three = scatter_plain(reduce_own, reduce_sib, n_dp)
        grad_two = scatter_plain(expand_own, expand_sib, n_dp)
        grad_one = scatter_plain(
            first_own[:, :BLOCK_ROWS], first_sib[:, :BLOCK_ROWS], n_dp
        )
        packed = first_own[0::2, BLOCK_ROWS:].astype(F32)
        low = packed[:, :, 0:BLOCK_ROWS].transpose(1, 0, 2).reshape(8, D)
        high = packed[:, 0:3, 128 : 128 + BLOCK_ROWS].transpose(1, 0, 2).reshape(3, D)
        vector_sum, bias_sum = lax.psum(
            (jnp.concatenate([low, high], axis=0), packed[:, 0, 256:640].reshape(-1)), AXES
        )
        spot = lax.axis_index("dp")
        vector_grad = lax.dynamic_slice_in_dim(vector_sum, spot * wide, wide, 1)
        units = expand_bias.shape[0]
        grad_bias = lax.dynamic_slice_in_dim(bias_sum, spot * units, units, 0)
    grad_qkv = jnp.stack([grad_one[:, i * GROUP_COLS : (i + 1) * GROUP_COLS] for i in range(3)])
    grad_out = grad_one[:, 3 * GROUP_COLS :].T
    return (
        cut(block_out),
        cut(tok_grad),
        *adam_update(project_qkv, grad_qkv, first_qkv, second_qkv, RATE_MATRIX, DECAY),
        *adam_update(project_out, grad_out, first_out, second_out, RATE_MATRIX, DECAY),
        *adam_update(expand_weight, grad_two, first_expand, second_expand, RATE_MATRIX, DECAY),
        *adam_update(reduce_weight, grad_three.T, first_reduce, second_reduce, RATE_MATRIX, DECAY),
        *adam_update(vectors, vector_grad, first_vectors, second_vectors, RATE_VECTOR, 0.0),
        *adam_update(expand_bias, grad_bias, first_bias, second_bias, RATE_VECTOR, 0.0),
    )


def solution(mesh):
    rows = P(AXES, None)
    states = (
        *(P(None, "dp", "tensor"),) * 3,
        *(P("tensor", "dp"),) * 3,
        *(P("dp", "tensor"),) * 3,
        *(P("tensor", "dp"),) * 3,
        *(P(None, "dp"),) * 3,
        *(P("dp"),) * 3,
    )
    return jax.shard_map(
        functools.partial(on_device, mesh.shape["dp"]),
        mesh=mesh,
        in_specs=(rows, rows, rows, *states),
        out_specs=(rows, rows, *states),
        check_vma=False,
    )
```

time: 936 us -> 296 us (0.32)
  blocking collectives: 346 us -> 0 us
  waiting for transfers between devices: 339 us -> 133 us
  matrix products: 85.7 us -> 0 us
  Pallas kernels: 0 us -> 80.4 us
  local copies, waits for them, and re-layouts: 83.8 us -> 22.3 us
  other arithmetic: 41.8 us -> 22.4 us
  starting transfers between devices: 16.5 us -> 35.8 us
  between operations: 16.8 us -> 1.22 us
    unnamed x4 -> x0, blocking collectives: 225 us -> none
    ppermute x0 -> x34, waiting for transfers between devices: none -> 133 us  [the longest x12 70.4 us: gather_stream(): taken = lax.ppermute(held, AXES, pairs_of(orders, level))]
    unnamed x18 -> x0, waiting for transfers between devices: 131 us -> none
    reduce_scatter x2 -> x0, waiting for transfers between devices: 124 us -> none  [the longest x1 69.7 us: on_device(): lax.psum_scatter(grad_reduce, 'dp', scatter_dimension=1, tiled=True)]
    all_gather x4 -> x0, blocking collectives: 105 us -> none  [the longest x1 31.5 us: on_device(): lax.all_gather(project_qkv.astype(jnp.bfloat16), 'dp', axis=1, tiled=True)]
    all_gather x6 -> x0, waiting for transfers between devices: 83.6 us -> none  [the longest x1 36.2 us: on_device(): lax.all_gather(reduce_weight.astype(jnp.bfloat16), 'dp', axis=1, tiled=True)]
    dot_general x23 -> x0, matrix products: 81.8 us -> none  [the longest x1 16.6 us: on_device(): jnp.dot(grad_branch_all, reduce_all.T, preferred_element_type=jnp.float32)]
    pallas_call x0 -> x6, Pallas kernels: none -> 80.4 us  [call(): pl.pallas_call(kernel, out_shape=outs, in_specs=[SMEM] * table + [VMEM] *...]
  transfers between devices with their start and end apart: 15 -> 34, of which waited for: 9 -> 16; matrix products, arithmetic and copies ran while one was open for 18% -> 12% of each run, Pallas kernels for 0% -> 27%
where the time goes in v1:
time: 296 us; the launch traced here: 295 us
  waiting for transfers between devices  133 us (45%)
  Pallas kernels  80.4 us (27%)
  starting transfers between devices  35.8 us (12%)
  other arithmetic  22.4 us (8%)
  local copies, waits for them, and re-layouts  22.3 us (8%)
    pallas_call x6, Pallas kernels, call(): pl.pallas_call(kernel, out_shape=outs, in_specs=[SMEM] * table + [VMEM] *...  80.4 us
    ppermute x12, waiting for transfers between devices, gather_stream(): taken = lax.ppermute(held, AXES, pairs_of(orders, level))  70.4 us
    ppermute x12, waiting for transfers between devices, scatter_stream(): terms.append(lax.ppermute(sent, AXES, pairs_of(orders, level)))  62 us
    ppermute x12, starting transfers between devices, gather_stream(): taken = lax.ppermute(held, AXES, pairs_of(orders, level))  17 us
    convert_element_type x12, other arithmetic, scatter_stream(): sent = total(size, 2 * size, False).astype(BF16)  13.4 us
    unnamed x88, local copies, waits for them, and re-layouts  11.3 us
    ppermute x12, starting transfers between devices, scatter_stream(): terms.append(lax.ppermute(sent, AXES, pairs_of(orders, level)))  7.61 us
    sub x6, other arithmetic, adam_update(): weight - step_rate * (first_hat / (jnp.sqrt(second_hat) + EPSILON) + deca...  6.97 us
  transfers between devices with their start and end apart: 34, of which 16 were waited for; matrix products, arithmetic and copies ran while one was open for 12% of the time, Pallas kernels for 27%

profile of v1, /device:TPU:1, one launch (start us, length us, event | category | flops | bytes accessed | tf_op | source)
XLA Modules:
  0.0 295.3 jit_solution(11266922291230631168)
XLA Ops:
  6.3 3.8 %collective-permute-done = bf16[1,104,768]{2,1,0:T(8,128)(2,1)S(1)} collective-permute-done((bf16[1,104,768]{2,1,0:T(8,128)(2,1)S(1)}, bf16[1,104,768]{2,1,0:T(8,128)(2,1)S(1)}, u32[]{:S(2)}, u32[]{:S(2)}) %collective-permute-start) | collective-permute-done | bytes 159776 | tf_op jit(solution)/shard_map/ppermute | solution.py:374
  13.8 15.8 %collective-permute-done.1 = bf16[2,104,768]{2,1,0:T(8,128)(2,1)S(1)} collective-permute-done((bf16[2,104,768]{2,1,0:T(8,128)(2,1)S(1)}, bf16[2,104,768]{2,1,0:T(8,128)(2,1)S(1)}, u32[]{:S(2)}, u32[]{:S(2)}) %collective-permute-start.1) | collective-permute-done | bytes 319520 | tf_op jit(solution)/shard_map/ppermute | solution.py:374
  33.8 3.4 %collective-permute-done.7 = bf16[2,96,768]{2,1,0:T(8,128)(2,1)S(1)} collective-permute-done((bf16[2,96,768]{2,1,0:T(8,128)(2,1)S(1)}, bf16[2,96,768]{2,1,0:T(8,128)(2,1)S(1)}, u32[]{:S(2)}, u32[]{:S(2)}) %collective-permute-start.7) | collective-permute-done | bytes 294944 | tf_op jit(solution)/shard_map/ppermute | solution.py:374
  37.3 4.7 %collective-permute-start.8 = (bf16[4,96,768]{2,1,0:T(8,128)(2,1)S(1)}, bf16[4,96,768]{2,1,0:T(8,128)(2,1)S(1)}, u32[]{:S(2)}, u32[]{:S(2)}) collective-permute-start(bf16[4,96,768]{2,1,0:T(8,128)(2,1)S(1)} %pad_maximum_fusion.4), channel_id=1, source_target_pairs={{0,16},{1,17},{2,18},{3,19},{4,20},{5,21},{6,22},{7,23},{8,24},{9,... | collective-permute-start | bytes 1769480 | tf_op jit(solution)/shard_map/ppermute | solution.py:374
  44.6 22.9 %collective-permute-done.8 = bf16[4,96,768]{2,1,0:T(8,128)(2,1)S(1)} collective-permute-done((bf16[4,96,768]{2,1,0:T(8,128)(2,1)S(1)}, bf16[4,96,768]{2,1,0:T(8,128)(2,1)S(1)}, u32[]{:S(2)}, u32[]{:S(2)}) %collective-permute-start.8) | collective-permute-done | bytes 589856 | tf_op jit(solution)/shard_map/ppermute | solution.py:374
  67.7 4.0 %collective-permute-start.4 = (bf16[8,104,768]{2,1,0:T(8,128)(2,1)S(1)}, bf16[8,104,768]{2,1,0:T(8,128)(2,1)S(1)}, u32[]{:S(2)}, u32[]{:S(2)}) collective-permute-start(bf16[8,104,768]{2,1,0:T(8,128)(2,1)S(1)} %pad_maximum_fusion.b0), channel_id=1, source_target_pairs={{0,1},{1,0},{2,3},{3,2},{4,5},{5,4},{6,7},{7,6},{8,9},{9,8},{10,11... | collective-permute-start | bytes 3833864 | tf_op jit(solution)/shard_map/ppermute | solution.py:380
  72.8 10.3 %collective-permute-done.12.b1 = bf16[8,96,768]{2,1,0:T(8,128)(2,1)} collective-permute-done((bf16[8,96,768]{2,1,0:T(8,128)(2,1)S(1)}, bf16[8,96,768]{2,1,0:T(8,128)(2,1)}, u32[]{:S(2)}, u32[]{:S(2)}) %collective-permute-start.12) | collective-permute-done | bytes 1179680 | tf_op jit(solution)/shard_map/ppermute | solution.py:374
  83.1 2.8 collective-permute-start.14
  85.9 13.6 %collective-permute-done.15.b1 = bf16[8,96,768]{2,1,0:T(8,128)(2,1)} collective-permute-done((bf16[8,96,768]{2,1,0:T(8,128)(2,1)S(1)}, bf16[8,96,768]{2,1,0:T(8,128)(2,1)}, u32[]{:S(2)}, u32[]{:S(2)}) %collective-permute-start.15) | collective-permute-done | bytes 1179680 | tf_op jit(solution)/shard_map/ppermute | solution.py:374
  111.2 16.9 %shard_map.384 = (f32[16,768]{1,0:T(8,128)S(1)}, f32[4,1,768]{2,1,0:T(1,128)S(1)}, bf16[4,768,768]{2,1,0:T(8,128)(2,1)}, bf16[416,768]{1,0:T(8,128)(2,1)S(1)}, b...) custom-call(s32[80]{0:T(128)S(1)} %fusion.8.tab, ...), custom_call_target="tpu_custom_call" | custom-call | flops 2944401408 | bytes 20000000 | tf_op jit(solution)/shard_map/pallas_call | solution.py:349
  128.1 14.4 %shard_map.385 = (bf16[4,768,768]{2,1,0:T(8,128)(2,1)}, bf16[4,416,768]{2,1,0:T(8,128)(2,1)}, f32[4,416,768]{2,1,0:T(8,128)}, bf16[416,768]{1,0:T(8,128)(2,1)S(1...) custom-call(s32[80]{0:T(128)S(1)} %fusion.7.tab, bf16[416,768]{1,0:T(8,128)(2,1)S(1)} %get-tuple-element.56.normed_two, ...), custom_call_target="tpu_custom_call" | custom-call | flops 3925868544 | bytes 20000000 | tf_op jit(solution)/shard_map/pallas_call | solution.py:349
  142.5 12.6 %shard_map.386 = (bf16[4,768,768]{2,1,0:T(8,128)(2,1)}, bf16[4,416,768]{2,1,0:T(8,128)(2,1)}, f32[4,1,768]{2,1,0:T(1,128)S(1)}, bf16[16,96,768]{2,1,0:T(8,128)(2,1)}, bf16[16,96,768]{2,1,0:T(8,128)(2,1)}) custom-call(s32[80]{0:T(128)S(1)} %fusion.9.tab, bf16[416,768]{1,0:T(8,128)(2,1)S(1)} %get-tuple-element.56.normed_two, ...), custom_call_target="tpu_custom_call" | custom-call | flops 3925868544 | bytes 20000000 | tf_op jit(solution)/shard_map/pallas_call | solution.py:349
  155.6 11.7 %shard_map.387 = (bf16[416,768]{1,0:T(8,128)(2,1)S(1)}, f32[416,768]{1,0:T(8,128)S(1)}, bf16[416,768]{1,0:T(8,128)(2,1)S(1)}, f32[16,768]{1,0:T(8,128)S(1)}) custom-call(bf16[4,416,768]{2,1,0:T(8,128)(2,1)} %get-tuple-element.59.active, bf16[4,416,768]{2,1,0:T(8,128)(2,1)} %get-tuple-element.62.grad_hidden, bf16[4,768,768]{2,1,0:T(8,128)(2,1)} %get-tuple-element.63.w2, ...), custom_call_target="tpu_custom_call" | custom-call | flops 3925868544 | bytes 20000000 | tf_op jit(solution)/shard_map/pallas_call | solution.py:349
  167.3 24.6 %shard_map.388 = (bf16[416,768]{1,0:T(8,128)(2,1)S(1)}, bf16[16,104,768]{2,1,0:T(8,128)(2,1)}, bf16[16,104,768]{2,1,0:T(8,128)(2,1)}) custom-call(s32[80]{0:T(128)S(1)} %fusion.8.tab, bf16[416,768]{1,0:T(8,128)(2,1)S(1)} %bitcast.60, f32[416,1]{1,0:T(8,128)S(1)} %reshape.82.rep, f32[16,768]{1,0:T(8,128)S(1)} %get-tuple-element.57.vec, ...), custom_call_target="tpu_custom_call" | custom-call | flops 5888802816 | bytes 30000000 | tf_op jit(solution)/shard_map/pallas_call | solution.py:349
  197.4 22.0 %collective-permute-done.29 = bf16[8,96,768]{2,1,0:T(8,128)(2,1)S(1)} collective-permute-done((bf16[8,96,768]{2,1,0:T(8,128)(2,1)S(1)}, bf16[8,96,768]{2,1,0:T(8,128)(2,1)S(1)}, u32[]{:S(2)}, u32[]{:S(2)}) %collective-permute-start.29) | collective-permute-done | bytes 1179680 | tf_op jit(solution)/shard_map/ppermute | solution.py:399
  219.7 2.8 collective-permute-done.24
  222.5 2.5 add_convert_fusion.3
  228.8 2.9 collective-permute-done.30
  236.8 16.4 %collective-permute-done.25 = bf16[4,96,768]{2,1,0:T(8,128)(2,1)} collective-permute-done((bf16[4,96,768]{2,1,0:T(8,128)(2,1)}, bf16[4,96,768]{2,1,0:T(8,128)(2,1)}, u32[]{:S(2)}, u32[]{:S(2)}) %collective-permute-start.25) | collective-permute-done | bytes 589856 | tf_op jit(solution)/shard_map/ppermute | solution.py:399
  256.9 3.2 %collective-permute-start.32 = (bf16[1,96,768]{2,1,0:T(8,128)(2,1)S(1)}, bf16[1,96,768]{2,1,0:T(8,128)(2,1)S(1)}, u32[]{:S(2)}, u32[]{:S(2)}) collective-permute-start(bf16[1,96,768]{2,1,0:T(8,128)(2,1)S(1)} %add_convert_fusion.6), channel_id=1, source_target_pairs={{0,16},{1,17},{2,18},{3,19},{4,20},{5,21},{6,22},{7,23},{8,24},{9,... | collective-permute-start | bytes 442376 | tf_op jit(solution)/shard_map/ppermute | solution.py:399
  261.6 3.1 %collective-permute-done.26 = bf16[2,96,768]{2,1,0:T(8,128)(2,1)S(1)} collective-permute-done((bf16[2,96,768]{2,1,0:T(8,128)(2,1)S(1)}, bf16[2,96,768]{2,1,0:T(8,128)(2,1)S(1)}, u32[]{:S(2)}, u32[]{:S(2)}) %collective-permute-start.26) | collective-permute-done | bytes 294944 | tf_op jit(solution)/shard_map/ppermute | solution.py:399
  266.0 2.3 multiply_subtract_fusion
  268.3 12.7 %collective-permute-done.21 = bf16[2,104,768]{2,1,0:T(8,128)(2,1)S(1)} collective-permute-done((bf16[2,104,768]{2,1,0:T(8,128)(2,1)S(1)}, bf16[2,104,768]{2,1,0:T(8,128)(2,1)S(1)}, u32[]{:S(2)}, u32[]{:S(2)}) %collective-permute-start.21) | collective-permute-done | bytes 319520 | tf_op jit(solution)/shard_map/ppermute | solution.py:399
  287.7 2.6 collective-permute-start.33
  (194 shorter events, 62.2 us)
Async XLA Ops:
  10.1 19.5 %collective-permute-start.1 = (bf16[2,104,768]{2,1,0:T(8,128)(2,1)S(1)}, bf16[2,104,768]{2,1,0:T(8,128)(2,1)S(1)}, u32[]{:S(2)}, u32[]{:S(2)}) collective-permute-start(bf16[2,104,768]{2,1,0:T(8,128)(2,1)S(1)} %pad_maximum_fusion.6), channel_id=1, source_target_pairs={{0,16},{1,17},{2,18},{3,19},{4,20},{5,21},{6,22},{7,23},{8,24},{9,... | collective-permute-start | bytes 958472 | tf_op jit(solution)/shard_map/ppermute | solution.py:374
  12.4 18.3 %collective-permute-start.6 = (bf16[1,96,768]{2,1,0:T(8,128)(2,1)S(1)}, bf16[1,96,768]{2,1,0:T(8,128)(2,1)S(1)}, u32[]{:S(2)}, u32[]{:S(2)}) collective-permute-start(bf16[1,96,768]{2,1,0:T(8,128)(2,1)S(1)} %convert_bitcast_fusion.1), channel_id=1, source_target_pairs={{0,2},{1,5},{2,0},{3,7},{4,6},{5,1},{6,4},{7,3},{8,10},{9,13},{10,... | collective-permute-start | bytes 442376 | tf_op jit(solution)/shard_map/ppermute | solution.py:374
  13.7 19.1 %collective-permute-start.9 = (bf16[1,96,768]{2,1,0:T(8,128)(2,1)S(1)}, bf16[1,96,768]{2,1,0:T(8,128)(2,1)S(1)}, u32[]{:S(2)}, u32[]{:S(2)}) collective-permute-start(bf16[1,96,768]{2,1,0:T(8,128)(2,1)S(1)} %convert_bitcast_fusion), channel_id=1, source_target_pairs={{0,16},{1,17},{2,18},{3,19},{4,20},{5,21},{6,22},{7,23},{8,24},{9,... | collective-permute-start | bytes 442376 | tf_op jit(solution)/shard_map/ppermute | solution.py:374
  37.3 30.2 %collective-permute-start.8 = (bf16[4,96,768]{2,1,0:T(8,128)(2,1)S(1)}, bf16[4,96,768]{2,1,0:T(8,128)(2,1)S(1)}, u32[]{:S(2)}, u32[]{:S(2)}) collective-permute-start(bf16[4,96,768]{2,1,0:T(8,128)(2,1)S(1)} %pad_maximum_fusion.4), channel_id=1, source_target_pairs={{0,16},{1,17},{2,18},{3,19},{4,20},{5,21},{6,22},{7,23},{8,24},{9,... | collective-permute-start | bytes 1769480 | tf_op jit(solution)/shard_map/ppermute | solution.py:374
  42.0 29.6 %collective-permute-start.11 = (bf16[4,96,768]{2,1,0:T(8,128)(2,1)S(1)}, bf16[4,96,768]{2,1,0:T(8,128)(2,1)S(1)}, u32[]{:S(2)}, u32[]{:S(2)}) collective-permute-start(bf16[4,96,768]{2,1,0:T(8,128)(2,1)S(1)} %pad_maximum_fusion.5), channel_id=1, source_target_pairs={{0,4},{1,3},{2,6},{3,1},{4,0},{5,7},{6,2},{7,5},{8,12},{9,11},{10,... | collective-permute-start | bytes 1769480 | tf_op jit(solution)/shard_map/ppermute | solution.py:374
  43.0 29.3 %collective-permute-start.3 = (bf16[8,104,768]{2,1,0:T(8,128)(2,1)S(1)}, bf16[8,104,768]{2,1,0:T(8,128)(2,1)}, u32[]{:S(2)}, u32[]{:S(2)}) collective-permute-start(bf16[8,104,768]{2,1,0:T(8,128)(2,1)S(1)} %pad_maximum_fusion.b0), channel_id=1, source_target_pairs={{0,2},{1,5},{2,0},{3,7},{4,6},{5,1},{6,4},{7,3},{8,10},{9,13},{10,... | collective-permute-start | bytes 3833864 | tf_op jit(solution)/shard_map/ppermute | solution.py:374
  67.6 15.5 %collective-permute-start.12 = (bf16[8,96,768]{2,1,0:T(8,128)(2,1)S(1)}, bf16[8,96,768]{2,1,0:T(8,128)(2,1)}, u32[]{:S(2)}, u32[]{:S(2)}) collective-permute-start(bf16[8,96,768]{2,1,0:T(8,128)(2,1)S(1)} %pad_maximum_fusion.1.b0), channel_id=1, source_target_pairs={{0,4},{1,3},{2,6},{3,1},{4,0},{5,7},{6,2},{7,5},{8,12},{9,11},{10,... | collective-permute-start | bytes 3538952 | tf_op jit(solution)/shard_map/ppermute | solution.py:374
  67.7 32.6 %collective-permute-start.4 = (bf16[8,104,768]{2,1,0:T(8,128)(2,1)S(1)}, bf16[8,104,768]{2,1,0:T(8,128)(2,1)S(1)}, u32[]{:S(2)}, u32[]{:S(2)}) collective-permute-start(bf16[8,104,768]{2,1,0:T(8,128)(2,1)S(1)} %pad_maximum_fusion.b0), channel_id=1, source_target_pairs={{0,1},{1,0},{2,3},{3,2},{4,5},{5,4},{6,7},{7,6},{8,9},{9,8},{10,11... | collective-permute-start | bytes 3833864 | tf_op jit(solution)/shard_map/ppermute | solution.py:380
  71.8 27.8 %collective-permute-start.15 = (bf16[8,96,768]{2,1,0:T(8,128)(2,1)S(1)}, bf16[8,96,768]{2,1,0:T(8,128)(2,1)}, u32[]{:S(2)}, u32[]{:S(2)}) collective-permute-start(bf16[8,96,768]{2,1,0:T(8,128)(2,1)S(1)} %pad_maximum_fusion.2.b0), channel_id=1, source_target_pairs={{0,8},{1,9},{2,10},{3,11},{4,12},{5,13},{6,14},{7,15},{8,0},{9,1},... | collective-permute-start | bytes 3538952 | tf_op jit(solution)/shard_map/ppermute | solution.py:374
  72.3 37.8 %collective-permute-start.5 = (bf16[8,104,768]{2,1,0:T(8,128)(2,1)}, bf16[8,104,768]{2,1,0:T(8,128)(2,1)}, u32[]{:S(2)}, u32[]{:S(2)}) collective-permute-start(bf16[8,104,768]{2,1,0:T(8,128)(2,1)} %collective-permute-done.3.b1), channel_id=1, source_target_pairs={{0,1},{1,0},{2,3},{3,2},{4,5},{5,4},{6,7},{7,6},{8,9},{9,8},{10,11... | collective-permute-start | bytes 3833864 | tf_op jit(solution)/shard_map/ppermute | solution.py:381
  72.5 55.5 %collective-permute-start.13 = (bf16[8,96,768]{2,1,0:T(8,128)(2,1)S(1)}, bf16[8,96,768]{2,1,0:T(8,128)(2,1)}, u32[]{:S(2)}, u32[]{:S(2)}) collective-permute-start(bf16[8,96,768]{2,1,0:T(8,128)(2,1)S(1)} %pad_maximum_fusion.1.b0), channel_id=1, source_target_pairs={{0,1},{1,0},{2,3},{3,2},{4,5},{5,4},{6,7},{7,6},{8,9},{9,8},{10,11... | collective-permute-start | bytes 3538952 | tf_op jit(solution)/shard_map/ppermute | solution.py:380
  83.1 45.0 %collective-permute-start.14 = (bf16[8,96,768]{2,1,0:T(8,128)(2,1)}, bf16[8,96,768]{2,1,0:T(8,128)(2,1)}, u32[]{:S(2)}, u32[]{:S(2)}) collective-permute-start(bf16[8,96,768]{2,1,0:T(8,128)(2,1)} %collective-permute-done.12.b1), channel_id=1, source_target_pairs={{0,1},{1,0},{2,3},{3,2},{4,5},{5,4},{6,7},{7,6},{8,9},{9,8},{10,11... | collective-permute-start | bytes 3538952 | tf_op jit(solution)/shard_map/ppermute | solution.py:381
  99.5 43.0 %collective-permute-start.16 = (bf16[8,96,768]{2,1,0:T(8,128)(2,1)S(1)}, bf16[8,96,768]{2,1,0:T(8,128)(2,1)}, u32[]{:S(2)}, u32[]{:S(2)}) collective-permute-start(bf16[8,96,768]{2,1,0:T(8,128)(2,1)S(1)} %pad_maximum_fusion.2.b0), channel_id=1, source_target_pairs={{0,1},{1,0},{2,3},{3,2},{4,5},{5,4},{6,7},{7,6},{8,9},{9,8},{10,11... | collective-permute-start | bytes 3538952 | tf_op jit(solution)/shard_map/ppermute | solution.py:380
  100.3 42.2 %collective-permute-start.17 = (bf16[8,96,768]{2,1,0:T(8,128)(2,1)}, bf16[8,96,768]{2,1,0:T(8,128)(2,1)}, u32[]{:S(2)}, u32[]{:S(2)}) collective-permute-start(bf16[8,96,768]{2,1,0:T(8,128)(2,1)} %collective-permute-done.15.b1), channel_id=1, source_target_pairs={{0,1},{1,0},{2,3},{3,2},{4,5},{5,4},{6,7},{7,6},{8,9},{9,8},{10,11... | collective-permute-start | bytes 3538952 | tf_op jit(solution)/shard_map/ppermute | solution.py:381
  142.5 49.4 %collective-permute-start.28 = (bf16[16,96,768]{2,1,0:T(8,128)(2,1)}, bf16[16,96,768]{2,1,0:T(8,128)(2,1)S(1)}, u32[]{:S(2)}, u32[]{:S(2)}) collective-permute-start(bf16[16,96,768]{2,1,0:T(8,128)(2,1)} %get-tuple-element.83), channel_id=1, source_target_pairs={{0,1},{1,0},{2,3},{3,2},{4,5},{5,4},{6,7},{7,6},{8,9},{9,8},{10,11... | collective-permute-start | bytes 7077896 | tf_op jit(solution)/shard_map/ppermute | solution.py:386
  155.1 37.7 %collective-permute-start.23 = (bf16[16,96,768]{2,1,0:T(8,128)(2,1)}, bf16[16,96,768]{2,1,0:T(8,128)(2,1)}, u32[]{:S(2)}, u32[]{:S(2)}) collective-permute-start(bf16[16,96,768]{2,1,0:T(8,128)(2,1)} %get-tuple-element.81), channel_id=1, source_target_pairs={{0,1},{1,0},{2,3},{3,2},{4,5},{5,4},{6,7},{7,6},{8,9},{9,8},{10,11... | collective-permute-start | bytes 7077896 | tf_op jit(solution)/shard_map/ppermute | solution.py:386
  192.3 27.1 %collective-permute-start.29 = (bf16[8,96,768]{2,1,0:T(8,128)(2,1)S(1)}, bf16[8,96,768]{2,1,0:T(8,128)(2,1)S(1)}, u32[]{:S(2)}, u32[]{:S(2)}) collective-permute-start(bf16[8,96,768]{2,1,0:T(8,128)(2,1)S(1)} %add_convert_fusion), channel_id=1, source_target_pairs={{0,8},{1,9},{2,10},{3,11},{4,12},{5,13},{6,14},{7,15},{8,0},{9,1},... | collective-permute-start | bytes 3538952 | tf_op jit(solution)/shard_map/ppermute | solution.py:399
  196.2 26.3 %collective-permute-start.24 = (bf16[8,96,768]{2,1,0:T(8,128)(2,1)S(1)}, bf16[8,96,768]{2,1,0:T(8,128)(2,1)S(1)}, u32[]{:S(2)}, u32[]{:S(2)}) collective-permute-start(bf16[8,96,768]{2,1,0:T(8,128)(2,1)S(1)} %add_convert_fusion.1), channel_id=1, source_target_pairs={{0,4},{1,3},{2,6},{3,1},{4,0},{5,7},{6,2},{7,5},{8,12},{9,11},{10,... | collective-permute-start | bytes 3538952 | tf_op jit(solution)/shard_map/ppermute | solution.py:399
  197.3 30.2 %collective-permute-start.19 = (bf16[8,104,768]{2,1,0:T(8,128)(2,1)S(1)}, bf16[8,104,768]{2,1,0:T(8,128)(2,1)S(1)}, u32[]{:S(2)}, u32[]{:S(2)}) collective-permute-start(bf16[8,104,768]{2,1,0:T(8,128)(2,1)S(1)} %reduce-precision_convert_fusion), channel_id=1, source_target_pairs={{0,2},{1,5},{2,0},{3,7},{4,6},{5,1},{6,4},{7,3},{8,10},{9,13},{10,... | collective-permute-start | bytes 3833864 | tf_op jit(solution)/shard_map/ppermute | solution.py:399
  225.0 28.1 %collective-permute-start.25 = (bf16[4,96,768]{2,1,0:T(8,128)(2,1)}, bf16[4,96,768]{2,1,0:T(8,128)(2,1)}, u32[]{:S(2)}, u32[]{:S(2)}) collective-permute-start(bf16[4,96,768]{2,1,0:T(8,128)(2,1)} %add_convert_fusion.3), channel_id=1, source_target_pairs={{0,16},{1,17},{2,18},{3,19},{4,20},{5,21},{6,22},{7,23},{8,24},{9,... | collective-permute-start | bytes 1769480 | tf_op jit(solution)/shard_map/ppermute | solution.py:399
  228.6 31.4 %collective-permute-start.20 = (bf16[4,104,768]{2,1,0:T(8,128)(2,1)}, bf16[4,104,768]{2,1,0:T(8,128)(2,1)}, u32[]{:S(2)}, u32[]{:S(2)}) collective-permute-start(bf16[4,104,768]{2,1,0:T(8,128)(2,1)} %reduce-precision_convert_fusion.1), channel_id=1, source_target_pairs={{0,4},{1,3},{2,6},{3,1},{4,0},{5,7},{6,2},{7,5},{8,12},{9,11},{10,... | collective-permute-start | bytes 1916936 | tf_op jit(solution)/shard_map/ppermute | solution.py:399
  232.6 23.1 %collective-permute-start.31 = (bf16[2,96,768]{2,1,0:T(8,128)(2,1)}, bf16[2,96,768]{2,1,0:T(8,128)(2,1)}, u32[]{:S(2)}, u32[]{:S(2)}) collective-permute-start(bf16[2,96,768]{2,1,0:T(8,128)(2,1)} %add_convert_fusion.4), channel_id=1, source_target_pairs={{0,2},{1,5},{2,0},{3,7},{4,6},{5,1},{6,4},{7,3},{8,10},{9,13},{10,... | collective-permute-start | bytes 884744 | tf_op jit(solution)/shard_map/ppermute | solution.py:399
  261.4 19.6 %collective-permute-start.21 = (bf16[2,104,768]{2,1,0:T(8,128)(2,1)S(1)}, bf16[2,104,768]{2,1,0:T(8,128)(2,1)S(1)}, u32[]{:S(2)}, u32[]{:S(2)}) collective-permute-start(bf16[2,104,768]{2,1,0:T(8,128)(2,1)S(1)} %reduce-precision_convert_fusion.2), channel_id=1, source_target_pairs={{0,16},{1,17},{2,18},{3,19},{4,20},{5,21},{6,22},{7,23},{8,24},{9,... | collective-permute-start | bytes 958472 | tf_op jit(solution)/shard_map/ppermute | solution.py:399
  265.9 16.4 %collective-permute-start.27 = (bf16[1,96,768]{2,1,0:T(8,128)(2,1)S(1)}, bf16[1,96,768]{2,1,0:T(8,128)(2,1)S(1)}, u32[]{:S(2)}, u32[]{:S(2)}) collective-permute-start(bf16[1,96,768]{2,1,0:T(8,128)(2,1)S(1)} %add_convert_fusion.7), channel_id=1, source_target_pairs={{0,2},{1,5},{2,0},{3,7},{4,6},{5,1},{6,4},{7,3},{8,10},{9,13},{10,... | collective-permute-start | bytes 442376 | tf_op jit(solution)/shard_map/ppermute | solution.py:399
  (51 other events, 468.5 us)

commit v2 on v1

v2 whole, which is shorter than its diff:
```python
import functools

import jax
import jax.numpy as jnp
import numpy as np
from jax import lax
from jax.experimental import pallas as pl
from jax.experimental.pallas import tpu as pltpu
from jax.sharding import PartitionSpec as P

D = 768
HEAD_DIM = 64
FF = 3072
SEQ = 197
STEP = 4
BETA_ONE = 0.5
BETA_TWO = 0.5
EPSILON = 1e-08
DECAY = 0.05
RATE_MATRIX = 0.02
RATE_VECTOR = 0.2
NORM_EPS = 1e-06

AXES = ("dp", "tensor")
PAD = 208
GROUPS = 4
GROUP_COLS = D // GROUPS
HEADS_IN_GROUP = GROUP_COLS // HEAD_DIM
BLOCKS = 8
BLOCK_ROWS = D // BLOCKS
EXTRA = 8
SCALE = HEAD_DIM**-0.5
SHORT = 1
LONG = 10**11
F32 = jnp.float32
BF16 = jnp.bfloat16

BIT = {"c": 1, "x": 2, "y": 4, "1": 8, "2": 16}
GATHER = (("12yx", "21xy"), ("xy21", "2y1x"), ("1x2y", "y21x"))
SCATTER = (("2y1x", "12xy"), ("21xy", "2xy1"), ("2y1x", "12xy"))
STEPS = "S0S1S2D0S0D1S1D2S2D1S1D0S0F0D2S2D0S0D1S1D2S2F1D0"


def offset_of(order, place):
    found = 0
    for level in range(4):
        if place >> level & 1:
            found ^= BIT[order[level]]
    return found


def pairs_of(orders, level):
    return [(dev, dev ^ BIT[orders[dev & 1][level]]) for dev in range(32)]


CORE_PAIRS = [(dev, dev ^ 1) for dev in range(32)]


def build_table(gather, scatter):
    table = np.zeros((32, 80), np.int32)
    for dev in range(32):
        core = dev & 1
        for place in range(16):
            table[dev, place] = dev ^ offset_of(gather[core], place)
            table[dev, 16 + place] = dev ^ 1 ^ offset_of(gather[1 - core], place)
            mine = dev ^ offset_of(gather[core], place)
            if mine & 3 == dev & 3:
                table[dev, 32 + (mine >> 2)] = place
            table[dev, 40 + (dev ^ offset_of(scatter[core], place))] = place
            table[dev, 40 + (dev ^ 1 ^ offset_of(scatter[1 - core], place))] = place
        table[dev, 72] = core
    return table


def plain_table():
    table = np.zeros((80,), np.int32)
    for place in range(32):
        table[place] = (place % 8) * 4 + place // 8
    for block in range(8):
        table[32 + block] = block
        for group in range(4):
            table[40 + block * 4 + group] = block * 2 + group // 2
    return table


def dot(left, right):
    return jnp.dot(left, right, preferred_element_type=F32)


def dot_rt(left, right):
    return lax.dot_general(left, right, (((1,), (1,)), ((), ())), preferred_element_type=F32)


def dot_lt(left, right):
    return lax.dot_general(left, right, (((0,), (0,)), ((), ())), preferred_element_type=F32)


def norm_stats(values):
    mean = jnp.mean(values, axis=-1, keepdims=True)
    centred = values - mean
    var = jnp.mean(centred * centred, axis=-1, keepdims=True)
    rstd = lax.rsqrt(var + NORM_EPS)
    return centred * rstd, rstd


def norm_back(grad, gain, unit, rstd):
    grad_unit = grad * gain
    first = jnp.mean(grad_unit, axis=-1, keepdims=True)
    second = jnp.mean(grad_unit * unit, axis=-1, keepdims=True)
    return rstd * (grad_unit - first - unit * second)


def col_sum(values):
    return jnp.sum(values, axis=0, keepdims=True)


def assemble(tab, parts, whole):
    for index, part in enumerate(parts):
        for place in range(8):
            owner = tab[index * 8 + place]
            row = pl.multiple_of((owner >> 2) * BLOCK_ROWS, BLOCK_ROWS)
            whole[owner & 3, pl.ds(row, BLOCK_ROWS), :] = part[place, 0:BLOCK_ROWS, :]


def put_blocks(tab, group, grad, out):
    for block in range(BLOCKS):
        place = tab[40 + block * 4 + group]
        rows = slice(block * BLOCK_ROWS, (block + 1) * BLOCK_ROWS)
        out[place] = grad[rows].astype(BF16)


def mask_rows(tok, rep, vec):
    replaced = rep[...]
    return tok[...].astype(F32) * (1.0 - replaced) + vec[6:7, :] * replaced


def pad_kernel(values, out):
    wide = values[...].astype(F32)
    gap = jnp.zeros((PAD - SEQ, D), F32)
    rows = []
    for start in range(0, wide.shape[0], SEQ):
        rows += [wide[start : start + SEQ], gap]
    out[...] = jnp.concatenate(rows, axis=0).astype(BF16)


def cut_kernel(values, out):
    wide = values[...].astype(F32)
    rows = [wide[start : start + SEQ] for start in range(0, wide.shape[0], PAD)]
    out[...] = jnp.concatenate(rows, axis=0).astype(BF16)


def fence_kernel(values, out):
    out[...] = values[...] + 1.0


def pack_kernel(project_qkv, project_out, vectors, expand_bias, out):
    columns = [project_qkv[0], project_qkv[1], project_qkv[2], project_out[...].T]
    block = jnp.concatenate(columns, axis=1)
    fill = jnp.zeros((EXTRA, 128 - BLOCK_ROWS), F32)
    low = jnp.concatenate([vectors[0:8, :], fill], axis=1)
    high = jnp.concatenate([vectors[8:11, :], jnp.zeros((5, BLOCK_ROWS), F32)], axis=0)
    high = jnp.concatenate([high, fill], axis=1)
    last = jnp.concatenate([expand_bias[...], jnp.zeros((EXTRA - 1, 384), F32)], axis=0)
    extra = jnp.concatenate([low, high, last, jnp.zeros((EXTRA, 128), F32)], axis=1)
    out[...] = jnp.concatenate([block, extra], axis=0).astype(BF16)


def attend_kernel(
    imgs, tab, tok, rep, b0, b1, b2, b3,
    vec, bias, w1, normed, qkv, soft, att, attn, mid, normed_two, qb, vb,
):
    low = jnp.zeros((8, D), F32)
    high = jnp.zeros((8, D), F32)
    fill = jnp.zeros((8, D - 128), F32)
    for block in range(BLOCKS):
        place = tab[32 + block]
        near = b0[place & 7].astype(F32)[BLOCK_ROWS:]
        far = b1[place & 7].astype(F32)[BLOCK_ROWS:]
        piece = jnp.where(place < 8, near, far)
        low += pltpu.roll(jnp.concatenate([piece[:, 0:128], fill], 1), block * BLOCK_ROWS, 1)
        high += pltpu.roll(jnp.concatenate([piece[:, 128:256], fill], 1), block * BLOCK_ROWS, 1)
        half = (block % 2) * 384
        bias[block // 2, 0:1, half : half + 384] = piece[0:1, 256:640]
    vec[0:8, :] = low
    vec[8:16, :] = high
    for group in range(GROUPS):
        cols = slice(group * GROUP_COLS, (group + 1) * GROUP_COLS)
        qb[group, 0:1, :] = vec[9:10, cols]
        vb[group, 0:1, :] = vec[10:11, cols]
    assemble(tab, (b0, b1, b2, b3), w1)
    start = mask_rows(tok, rep, vec)
    unit, _ = norm_stats(start)
    normed[...] = (unit * vec[0:1, :] + vec[1:2, :]).astype(BF16)
    attn[...] = jnp.zeros_like(attn)
    keep = lax.broadcasted_iota(jnp.int32, (PAD, PAD), 1) < SEQ

    def step(group, carry):
        result = dot(normed[...], w1[group, :, 0:576])
        qkv[group, :, 0:192] = (result[:, 0:192] + qb[group, 0:1, :]).astype(BF16)
        qkv[group, :, 192:384] = result[:, 192:384].astype(BF16)
        qkv[group, :, 384:576] = (result[:, 384:576] + vb[group, 0:1, :]).astype(BF16)
        for head in range(HEADS_IN_GROUP):
            c0 = head * HEAD_DIM
            for img in range(imgs):
                rows = slice(img * PAD, (img + 1) * PAD)
                q = qkv[group, rows, c0 : c0 + 64]
                k = qkv[group, rows, 192 + c0 : 256 + c0]
                v = qkv[group, rows, 384 + c0 : 448 + c0]
                scores = jnp.where(keep, dot_rt(q, k) * SCALE, -1e30)
                top = jnp.max(scores, axis=-1, keepdims=True)
                raised = jnp.exp(scores - top)
                weights = raised / jnp.sum(raised, axis=-1, keepdims=True)
                soft[group * (HEADS_IN_GROUP * imgs) + head * imgs + img] = weights
                att[group, rows, c0 : c0 + 64] = dot(weights.astype(BF16), v).astype(BF16)
        attn[...] += dot_rt(att[group], w1[group, :, 576:768])
        return carry

    lax.fori_loop(0, GROUPS, step, 0)
    middle = start + vec[4:5, :] * (attn[...] + vec[7:8, :])
    mid[...] = middle
    unit_two, _ = norm_stats(middle)
    normed_two[...] = (unit_two * vec[2:3, :] + vec[3:4, :]).astype(BF16)


def expand_groups(tab, part, normed_two, grad_branch, bias, w2, active, slope, out):
    def step(along_x, carry):
        group = along_x * 2 + (tab[72] ^ part)
        hidden = dot(normed_two[...], w2[group]) + bias[group, 0:1, :]
        cdf = 0.5 * (1.0 + lax.erf(hidden * 0.7071067811865476))
        pdf = 0.3989422804014327 * jnp.exp(-0.5 * hidden * hidden)
        act = (hidden * cdf).astype(BF16)
        active[along_x] = act
        slope[along_x] = cdf + hidden * pdf
        put_blocks(tab, group, dot_lt(grad_branch[...], act), out)
        return carry

    lax.fori_loop(0, 2, step, 0)


def expand_sib_kernel(
    tab, normed_two, cot, vec, bias, b0, b1, b2, b3, w2, active, slope, grad_branch, out
):
    assemble(tab, (b0, b1, b2, b3), w2)
    grad_branch[...] = (cot[...].astype(F32) * vec[5:6, :]).astype(BF16)
    expand_groups(tab, 1, normed_two, grad_branch, bias, w2, active, slope, out)


def expand_own_kernel(tab, normed_two, grad_branch, bias, w2, active, slope, out):
    expand_groups(tab, 0, normed_two, grad_branch, bias, w2, active, slope, out)


def hidden_groups(tab, part, normed_two, grad_branch, slope, w3, grad_hidden, bias_grad, out):
    def step(along_x, carry):
        group = along_x * 2 + (tab[72] ^ part)
        grad = (dot(grad_branch[...], w3[group]) * slope[along_x]).astype(BF16)
        grad_hidden[along_x] = grad
        bias_grad[along_x, 0:1, :] = col_sum(grad.astype(F32))
        put_blocks(tab, group, dot_lt(normed_two[...], grad), out)
        return carry

    lax.fori_loop(0, 2, step, 0)


def hidden_sib_kernel(
    tab, normed_two, grad_branch, slope, b0, b1, b2, b3, w3, grad_hidden, bias_grad, out
):
    assemble(tab, (b0, b1, b2, b3), w3)
    hidden_groups(tab, 1, normed_two, grad_branch, slope, w3, grad_hidden, bias_grad, out)


def hidden_own_kernel(tab, normed_two, grad_branch, slope, w3, grad_hidden, bias_grad, out):
    hidden_groups(tab, 0, normed_two, grad_branch, slope, w3, grad_hidden, bias_grad, out)


def middle_kernel(
    tab, act_sib, act_own, hid_sib, hid_own, w2, w3, mid, attn, cot, vec,
    block_out, grad_mid, grad_attn, sums, branch, grad_two,
):
    branch[...] = jnp.zeros_like(branch)
    grad_two[...] = jnp.zeros_like(grad_two)
    sums[...] = jnp.zeros_like(sums)
    for part, active, grad_hidden in ((1, act_sib, hid_sib), (0, act_own, hid_own)):

        def step(along_x, carry, part=part, active=active, grad_hidden=grad_hidden):
            group = along_x * 2 + (tab[72] ^ part)
            branch[...] += dot_rt(active[along_x], w3[group])
            grad_two[...] += dot_rt(grad_hidden[along_x], w2[group])
            return carry

        lax.fori_loop(0, 2, step, 0)
    middle = mid[...]
    total = branch[...] + vec[8:9, :]
    block_out[...] = (middle + vec[5:6, :] * total).astype(BF16)
    grad_out = cot[...].astype(F32)
    sums[5:6, :] = col_sum(grad_out * total)
    sums[8:9, :] = col_sum(grad_out * vec[5:6, :])
    unit, rstd = norm_stats(middle)
    grad = grad_two[...]
    sums[2:3, :] = col_sum(grad * unit)
    sums[3:4, :] = col_sum(grad)
    grad_middle = grad_out + norm_back(grad, vec[2:3, :], unit, rstd)
    grad_mid[...] = grad_middle
    sums[4:5, :] = col_sum(grad_middle * (attn[...] + vec[7:8, :]))
    scaled = grad_middle * vec[4:5, :]
    sums[7:8, :] = col_sum(scaled)
    grad_attn[...] = scaled.astype(BF16)


def back_groups(
    imgs, tab, part, w1, normed, qkv, soft, att, grad_attn, out, grad_one, gqkv, bias_sums
):
    def step(along_x, carry):
        group = along_x * 2 + (tab[72] ^ part)
        grad_att = dot(grad_attn[...], w1[group, :, 576:768]).astype(BF16)
        for head in range(HEADS_IN_GROUP):
            c0 = head * HEAD_DIM
            for img in range(imgs):
                rows = slice(img * PAD, (img + 1) * PAD)
                q = qkv[group, rows, c0 : c0 + 64]
                k = qkv[group, rows, 192 + c0 : 256 + c0]
                v = qkv[group, rows, 384 + c0 : 448 + c0]
                weights = soft[group * (HEADS_IN_GROUP * imgs) + head * imgs + img]
                grad = grad_att[rows, c0 : c0 + 64]
                grad_soft = dot_rt(grad, v)
                grad_v = dot_lt(weights.astype(BF16), grad)
                inner = jnp.sum(weights * grad_soft, axis=-1, keepdims=True)
                grad_scores = (weights * (grad_soft - inner)).astype(BF16)
                grad_q = dot(grad_scores, k) * SCALE
                grad_k = dot_lt(grad_scores, q) * SCALE
                gqkv[rows, c0 : c0 + 64] = grad_q.astype(BF16)
                gqkv[rows, 192 + c0 : 256 + c0] = grad_k.astype(BF16)
                gqkv[rows, 384 + c0 : 448 + c0] = grad_v.astype(BF16)
        all_grads = gqkv[...]
        bias_sums[along_x, 0:1, :] = col_sum(all_grads[:, 0:192].astype(F32))
        bias_sums[along_x, 1:2, :] = col_sum(all_grads[:, 384:576].astype(F32))
        grad_one[...] += dot_rt(all_grads, w1[group, :, 0:576])
        both = jnp.concatenate(
            [dot_lt(normed[...], all_grads), dot_lt(grad_attn[...], att[group])], axis=1
        )
        put_blocks(tab, group, both, out)
        return carry

    lax.fori_loop(0, 2, step, 0)


def back_sib_kernel(
    imgs, tab, w1, normed, qkv, soft, att, grad_attn, out, grad_one, bias_sums, gqkv
):
    grad_one[...] = jnp.zeros_like(grad_one)
    back_groups(
        imgs, tab, 1, w1, normed, qkv, soft, att, grad_attn, out, grad_one, gqkv, bias_sums
    )


def back_own_kernel(
    imgs, tab, w1, normed, qkv, soft, att, grad_attn, grad_one_in, out, grad_one, bias_sums, gqkv
):
    grad_one[...] = grad_one_in[...]
    back_groups(
        imgs, tab, 0, w1, normed, qkv, soft, att, grad_attn, out, grad_one, gqkv, bias_sums
    )


def start_kernel(
    tab, tok, rep, vec, grad_one, bias_sib, bias_own, grad_mid, sums_in, units_sib, units_own,
    tok_grad, sums,
):
    replaced = rep[...]
    unit, rstd = norm_stats(mask_rows(tok, rep, vec))
    grad = grad_one[...]
    sums[0:16, :] = sums_in[...]
    sums[16:24, :] = jnp.zeros((8, D), F32)
    sums[0:1, :] = col_sum(grad * unit)
    sums[1:2, :] = col_sum(grad)
    grad_start = grad_mid[...] + norm_back(grad, vec[0:1, :], unit, rstd)
    tok_grad[...] = (grad_start * (1.0 - replaced)).astype(BF16)
    sums[6:7, :] = col_sum(grad_start * replaced)
    for group in range(GROUPS):
        cols = slice(group * GROUP_COLS, (group + 1) * GROUP_COLS)
        own = tab[72] == group % 2
        along_x = group // 2
        both = jnp.where(own, bias_own[along_x], bias_sib[along_x])
        sums[9:10, cols] = both[0:1]
        sums[10:11, cols] = both[1:2]
        sums[16 + group : 17 + group, :] = jnp.where(own, units_own[along_x], units_sib[along_x])


def adam_update(weight, gradient, first_moment, second, step_rate, decay_rate):
    moment = BETA_ONE * first_moment + (1.0 - BETA_ONE) * gradient
    square = BETA_TWO * second + (1.0 - BETA_TWO) * gradient * gradient
    first_hat = moment / (1.0 - BETA_ONE**STEP)
    second_hat = square / (1.0 - BETA_TWO**STEP)
    updated = weight - step_rate * (
        first_hat / (jnp.sqrt(second_hat) + EPSILON) + decay_rate * weight
    )
    return (updated, moment, square)


def finish_kernel(
    partial, last, qkv, first_qkv, second_qkv, out, first_out, second_out, *results
):
    grad = partial[...] + last[...].astype(F32)
    for index in range(3):
        cols = slice(index * GROUP_COLS, (index + 1) * GROUP_COLS)
        found = adam_update(
            qkv[index], grad[:, cols], first_qkv[index], second_qkv[index], RATE_MATRIX, DECAY
        )
        for result, values in zip(results[:3], found, strict=True):
            result[index] = values
    found = adam_update(
        out[...], grad[:, 576:768].T, first_out[...], second_out[...], RATE_MATRIX, DECAY
    )
    for result, values in zip(results[3:], found, strict=True):
        result[...] = values


VMEM = pl.BlockSpec(memory_space=pltpu.VMEM)
SMEM = pl.BlockSpec(memory_space=pltpu.SMEM)


def shape(dims, dtype=BF16):
    return jax.ShapeDtypeStruct(dims, dtype)


def call(kernel, args, outs, scratch=(), flops=SHORT, megabytes=10, table=True):
    return pl.pallas_call(
        kernel,
        out_shape=outs,
        in_specs=[SMEM] * table + [VMEM] * (len(args) - table),
        out_specs=[VMEM] * len(outs),
        scratch_shapes=list(scratch),
        cost_estimate=pl.CostEstimate(flops=flops, bytes_accessed=1, transcendentals=0),
        compiler_params=pltpu.CompilerParams(vmem_limit_bytes=megabytes << 20),
    )(*args)


def after(value, *earlier):
    return lax.optimization_barrier((value, earlier))[0]


def add_across(values, *masks):
    for mask in masks:
        pairs = [(dev, dev ^ mask) for dev in range(32)]
        values = values + lax.ppermute(values, AXES, pairs)
    return values


class Gather:
    def __init__(self, block, orders):
        self.held = block[None]
        self.orders = orders
        self.level = 0
        self.taken = None

    def start(self, *earlier):
        if earlier:
            self.held = after(self.held, *earlier)
        self.taken = lax.ppermute(self.held, AXES, pairs_of(self.orders, self.level))
        self.level += 1
        if self.level == 4:
            self.held_sib = lax.ppermute(self.held, AXES, CORE_PAIRS)

    def take(self):
        if self.level < 4:
            self.held = jnp.concatenate([self.held, self.taken], axis=0)
        return self.taken

    def finish(self, *earlier):
        while self.level < 4:
            self.taken = after(self.taken, *earlier)
            self.take()
            self.start()

    def parts(self, *earlier):
        if earlier:
            self.taken = after(self.taken, *earlier)
        self.taken_sib = lax.ppermute(self.taken, AXES, CORE_PAIRS)
        return self.held, self.taken, self.held_sib, self.taken_sib


class Scatter:
    def __init__(self, orders):
        self.orders = orders
        self.level = 4
        self.terms = []

    def swap(self, sib):
        self.terms.append(lax.ppermute(sib, AXES, CORE_PAIRS))

    def add(self, own):
        self.terms.insert(0, own)

    def total(self, low, high):
        return sum(term[low:high].astype(F32) for term in self.terms)

    def step(self, *earlier):
        self.level -= 1
        size = 1 << self.level
        if earlier:
            self.terms[-1] = after(self.terms[-1], *earlier)
        sent = self.total(size, 2 * size).astype(BF16)
        self.terms.append(lax.ppermute(sent, AXES, pairs_of(self.orders, self.level)))
        return sent

    def result(self):
        return self.total(0, 1)[0]


def gather_plain(block):
    whole = lax.all_gather(block, AXES, axis=0, tiled=False)
    whole = whole.reshape(-1, GROUPS, *block.shape).transpose(1, 0, 2, 3)
    whole = whole.reshape(GROUPS, BLOCKS, BLOCK_ROWS, D)
    return tuple(whole[group] for group in range(GROUPS))


def scatter_plain(own, sib, n_dp):
    parts = jnp.stack([own, sib]).reshape(2, BLOCKS, 2, BLOCK_ROWS, D)
    whole = parts.transpose(1, 3, 2, 0, 4).reshape(D, GROUPS, D).astype(F32)
    whole = whole.reshape(n_dp, D // n_dp, GROUPS, D).transpose(0, 2, 1, 3)
    whole = whole.reshape(n_dp * GROUPS, D // n_dp, D)
    return lax.psum_scatter(whole, AXES, scatter_dimension=0, tiled=True)[0]


def on_device(
    n_dp,
    tokens,
    patch_mask,
    cotangent,
    project_qkv,
    first_qkv,
    second_qkv,
    project_out,
    first_out,
    second_out,
    expand_weight,
    first_expand,
    second_expand,
    reduce_weight,
    first_reduce,
    second_reduce,
    vectors,
    first_vectors,
    second_vectors,
    expand_bias,
    first_bias,
    second_bias,
):
    direct = n_dp == BLOCKS
    imgs = patch_mask.shape[0]
    rows = imgs * PAD
    wide = vectors.shape[1]
    units = expand_bias.shape[0]

    def padded(values):
        values = values.reshape(imgs, SEQ, -1)
        return jnp.pad(values, ((0, 0), (0, PAD - SEQ), (0, 0))).reshape(rows, -1)

    positions = lax.broadcasted_iota(jnp.int32, patch_mask.shape, 1)
    replaced = jnp.where((patch_mask == 1) & (positions > 0), 1.0, 0.0).astype(F32)
    rep = padded(replaced)

    def cut(values):
        out = shape((imgs * SEQ, D))
        return call(cut_kernel, (values,), (out,), table=False)[0]

    def pad_rows(values):
        return call(pad_kernel, (values,), (shape((rows, D)),), flops=LONG, table=False)[0]

    piece_two = expand_weight.astype(BF16)
    piece_three = reduce_weight.astype(BF16).T
    if direct:
        flat = lax.axis_index("dp") * GROUPS + lax.axis_index("tensor")
        chosen = zip(GATHER, (SCATTER[0], SCATTER[2], SCATTER[1]), strict=True)
        every = np.concatenate([build_table(g, s) for g, s in chosen], axis=1)
        table = lax.dynamic_index_in_dim(jnp.asarray(every), flat, 0, keepdims=False)
        tables = [table[0:80], table[80:160], table[160:240]]
        (piece_one,) = call(
            pack_kernel,
            (project_qkv, project_out, vectors, expand_bias[None]),
            (shape((BLOCK_ROWS + EXTRA, D)),),
            table=False,
        )
        streams = [
            Gather(piece, orders)
            for piece, orders in zip((piece_one, piece_two, piece_three), GATHER, strict=True)
        ]
        seen = {}
        mark = jnp.zeros((8, 128), F32)
        for kind, index in zip(STEPS[0::2], STEPS[1::2], strict=True):
            stream = streams[int(index)]
            held = [stream.held for stream in streams]
            if kind == "X":
                mark = after(mark, *held, *seen.values())
                (mark,) = call(fence_kernel, (mark,), (shape((8, 128), F32),), flops=LONG, table=False)
                seen["mark"] = mark
            elif kind == "F":
                if index == "0":
                    tok = pad_rows(after(tokens, *held))
                    seen["tok"] = (tok, rep, *tables)
                else:
                    cot = pad_rows(after(cotangent, *held))
                    seen["cot"] = cot
            elif kind == "S":
                stream.start(*seen.values())
            else:
                seen[index] = stream.take()
        w1_parts = streams[0].parts(*[seen[name] for name in seen if name not in "12"])
    else:
        tables = [jnp.asarray(plain_table())] * 3
        tok, cot = pad_rows(tokens), pad_rows(cotangent)
        piece_one = jnp.concatenate(
            [project_qkv[0], project_qkv[1], project_qkv[2], project_out.T], axis=1
        ).astype(BF16)
        w1_parts, w2_parts, w3_parts = (
            gather_plain(piece) for piece in (piece_one, piece_two, piece_three)
        )
        vector_all = lax.all_gather(vectors.astype(BF16), "dp", axis=1, tiled=True)
        bias_all = lax.all_gather(expand_bias.astype(BF16), "dp", axis=0, tiled=True)
        by_block = vector_all.reshape(11, BLOCKS, BLOCK_ROWS).transpose(1, 0, 2)
        extras = jnp.zeros((BLOCKS, EXTRA, D), BF16)
        extras = extras.at[:, :, 0:BLOCK_ROWS].set(by_block[:, 0:8])
        extras = extras.at[:, 0:3, 128 : 128 + BLOCK_ROWS].set(by_block[:, 8:11])
        extras = extras.at[:, 0, 256:640].set(bias_all.reshape(BLOCKS, FF // BLOCKS))
        w1_parts = tuple(jnp.concatenate([part, extras], axis=1) for part in w1_parts)

    full = (GROUPS, D, D)
    row_f32 = shape((rows, D), F32)
    row_low = shape((rows, D))
    half = shape((16, BLOCK_ROWS, D))
    two_low = shape((2, rows, D))
    two_f32 = shape((2, rows, D), F32)
    two_bias = shape((2, 1, D), F32)
    group_bias = pltpu.VMEM((GROUPS, 1, GROUP_COLS), F32)
    n_soft = GROUPS * HEADS_IN_GROUP * imgs
    vec, bias, w1, normed, qkv, soft, att, attn, mid, normed_two = call(
        functools.partial(attend_kernel, imgs),
        (tables[0], tok, rep, *w1_parts),
        (
            shape((16, D), F32),
            shape((GROUPS, 1, D), F32),
            shape(full),
            row_low,
            shape((GROUPS, rows, 3 * GROUP_COLS)),
            shape((n_soft, PAD, PAD), F32),
            shape((GROUPS, rows, GROUP_COLS)),
            row_f32,
            row_f32,
            row_low,
        ),
        (group_bias, group_bias),
        flops=SHORT,
    )
    if direct:
        streams[1].finish(normed_two)
        streams[2].finish(normed_two)
        w2_parts = streams[1].parts(normed_two)
    three, two, one = (Scatter(SCATTER[index]) for index in (2, 1, 0))
    w2, act_sib, slope_sib, grad_branch, reduce_sib = call(
        expand_sib_kernel,
        (tables[1], normed_two, cot, vec, bias, *w2_parts),
        (shape(full), two_low, two_f32, row_low, half),
        flops=SHORT,
    )
    if direct:
        three.swap(reduce_sib)
    act_own, slope_own, reduce_own = call(
        expand_own_kernel,
        (tables[1], normed_two, grad_branch, bias, w2),
        (two_low, two_f32, half),
        flops=LONG,
    )
    if direct:
        w3_parts = streams[2].parts(reduce_own)
        three.add(reduce_own)
        w3_parts = after(w3_parts, three.step())
    w3, hid_sib, units_sib, expand_sib = call(
        hidden_sib_kernel,
        (tables[2], normed_two, grad_branch, slope_sib, *w3_parts),
        (shape(full), two_low, two_bias, half),
        flops=SHORT,
    )
    if direct:
        two.swap(expand_sib)
    hid_own, units_own, expand_own = call(
        hidden_own_kernel,
        (tables[2], normed_two, grad_branch, slope_own, w3),
        (two_low, two_bias, half),
        flops=LONG,
    )
    if direct:
        two.add(expand_own)
        mid = after(mid, two.step())
    block_out, grad_mid, grad_attn, sums = call(
        middle_kernel,
        (tables[0], act_sib, act_own, hid_sib, hid_own, w2, w3, mid, attn, cot, vec),
        (row_low, row_f32, row_low, shape((16, D), F32)),
        (pltpu.VMEM((rows, D), F32), pltpu.VMEM((rows, D), F32)),
        flops=SHORT,
    )
    if direct:
        grad_attn = after(grad_attn, three.step(sums))
    shared = (w1, normed, qkv, soft, att, grad_attn)
    held = pltpu.VMEM((rows, 3 * GROUP_COLS), BF16)
    bias_sums = (2, 2, GROUP_COLS)
    first_sib, grad_one, bias_sib = call(
        functools.partial(back_sib_kernel, imgs),
        (tables[0], *shared),
        (half, row_f32, shape(bias_sums, F32)),
        (held,),
        flops=SHORT,
    )
    if direct:
        one.swap(first_sib)
        grad_one = after(grad_one, three.step(grad_one), two.step(grad_one))
    first_own, grad_one, bias_own = call(
        functools.partial(back_own_kernel, imgs),
        (tables[0], *shared, grad_one),
        (half, row_f32, shape(bias_sums, F32)),
        (held,),
        flops=LONG,
    )
    if direct:
        first_own, grad_one = after((first_own, grad_one), three.terms[-1], two.terms[-1])
        one.add(first_own)
        sent = one.step()
        grad_one = after(grad_one, three.step(sent), two.step(sent))
    tok_grad, sums = call(
        start_kernel,
        (
            tables[0], tok, rep, vec, grad_one, bias_sib, bias_own, grad_mid, sums,
            units_sib, units_own,
        ),
        (row_low, shape((24, D), F32)),
    )

    if direct:
        sums = add_across(sums, 1, 8, 16)
        block_rows, token_rows = cut(block_out), cut(tok_grad)
        sent = one.step(sums, block_rows, token_rows)
        grad_three = after(three.result(), sent)
        states_three = adam_update(
            reduce_weight, grad_three.T, first_reduce, second_reduce, RATE_MATRIX, DECAY
        )
        sums = add_across(after(sums, sent), 4)
        sent_two = two.step(sent)
        sent = one.step(states_three[0], sent_two, sums)
        sums = add_across(after(sums, sent), 2)
        sent = one.step(sums)
        grad_two = after(two.result(), sent)
        partial = sum(term[0].astype(F32) for term in one.terms[:-1])
        finished = call(
            finish_kernel,
            (
                partial, one.terms[-1][0], project_qkv, first_qkv, second_qkv,
                project_out, first_out, second_out,
            ),
            (shape(project_qkv.shape, F32),) * 3 + (shape(project_out.shape, F32),) * 3,
            table=False,
        )
    else:
        block_rows, token_rows = cut(block_out), cut(tok_grad)
        grad_three = scatter_plain(reduce_own, reduce_sib, n_dp)
        grad_two = scatter_plain(expand_own, expand_sib, n_dp)
        grad_one = scatter_plain(first_own, first_sib, n_dp)
        sums = lax.psum(sums, AXES)
        grad_qkv = jnp.stack([grad_one[:, i * GROUP_COLS : (i + 1) * GROUP_COLS] for i in range(3)])
        grad_out = grad_one[:, 3 * GROUP_COLS :].T
        states_three = adam_update(
            reduce_weight, grad_three.T, first_reduce, second_reduce, RATE_MATRIX, DECAY
        )
        finished = (
            *adam_update(project_qkv, grad_qkv, first_qkv, second_qkv, RATE_MATRIX, DECAY),
            *adam_update(project_out, grad_out, first_out, second_out, RATE_MATRIX, DECAY),
        )
    spot = lax.axis_index("dp")
    vector_grad = lax.dynamic_slice_in_dim(sums[0:11], spot * wide, wide, 1)
    grad_bias = lax.dynamic_slice_in_dim(sums[16:20].reshape(-1), spot * units, units, 0)
    return (
        block_rows,
        token_rows,
        *finished,
        *adam_update(expand_weight, grad_two, first_expand, second_expand, RATE_MATRIX, DECAY),
        *states_three,
        *adam_update(vectors, vector_grad, first_vectors, second_vectors, RATE_VECTOR, 0.0),
        *adam_update(expand_bias, grad_bias, first_bias, second_bias, RATE_VECTOR, 0.0),
    )


def solution(mesh):
    rows = P(AXES, None)
    states = (
        *(P(None, "dp", "tensor"),) * 3,
        *(P("tensor", "dp"),) * 3,
        *(P("dp", "tensor"),) * 3,
        *(P("tensor", "dp"),) * 3,
        *(P(None, "dp"),) * 3,
        *(P("dp"),) * 3,
    )
    return jax.shard_map(
        functools.partial(on_device, mesh.shape["dp"]),
        mesh=mesh,
        in_specs=(rows, rows, rows, *states),
        out_specs=(rows, rows, *states),
        check_vma=False,
    )
```

time: 296 us -> 216 us (0.73)
  the two profiles are of different devices: /device:TPU:1 before, /device:TPU:0 now
where the time goes in v2:
time: 216 us; the launch traced here: 215 us
  waiting for transfers between devices  81.7 us (38%)
  Pallas kernels  58.8 us (27%)
  starting transfers between devices  38.1 us (18%)
  other arithmetic  26.8 us (12%)
  local copies, waits for them, and re-layouts  8.53 us (4%)
    pallas_call x15, Pallas kernels, call(): pl.pallas_call(kernel, out_shape=outs, in_specs=[SMEM] * table + [VMEM] *...  58.8 us
    ppermute x12, waiting for transfers between devices, start(): lax.ppermute(self.held, AXES, pairs_of(self.orders, self.level))  56.1 us
    convert_element_type x12, other arithmetic, step(): sent = self.total(size, 2 * size).astype(BF16)  17.3 us
    ppermute x12, waiting for transfers between devices, step(): lax.ppermute(sent, AXES, pairs_of(self.orders, self.level))  16.1 us
    ppermute x12, starting transfers between devices, start(): lax.ppermute(self.held, AXES, pairs_of(self.orders, self.level))  15.3 us
    ppermute x12, starting transfers between devices, step(): lax.ppermute(sent, AXES, pairs_of(self.orders, self.level))  11.8 us
    ppermute x5, starting transfers between devices, add_across(): values = values + lax.ppermute(values, AXES, pairs)  6.36 us
    unnamed x90, local copies, waits for them, and re-layouts  6.17 us
  transfers between devices with their start and end apart: 38, of which 21 were waited for; matrix products, arithmetic and copies ran while one was open for 11% of the time, Pallas kernels for 27%

profile of v2, /device:TPU:0, one launch (start us, length us, event | category | flops | bytes accessed | tf_op | source)
XLA Modules:
  0.0 215.3 jit_solution(3520810605606846359)
XLA Ops:
  4.1 3.1 %collective-permute-start = (bf16[1,104,768]{2,1,0:T(8,128)(2,1)S(1)}, bf16[1,104,768]{2,1,0:T(8,128)(2,1)S(1)}, u32[]{:S(2)}, u32[]{:S(2)}) collective-permute-start(bf16[1,104,768]{2,1,0:T(8,128)(2,1)S(1)} %bitcast.29), channel_id=1, source_target_pairs={{0,8},{1,17},{2,10},{3,19},{4,12},{5,21},{6,14},{7,23},{8,0},{9,25... | collective-permute-start | bytes 479240 | tf_op jit(solution)/shard_map/ppermute | solution.py:458
  16.7 2.6 %collective-permute-start.1 = (bf16[2,104,768]{2,1,0:T(8,128)(2,1)S(1)}, bf16[2,104,768]{2,1,0:T(8,128)(2,1)S(1)}, u32[]{:S(2)}, u32[]{:S(2)}) collective-permute-start(bf16[2,104,768]{2,1,0:T(8,128)(2,1)S(1)} %pad_maximum_fusion.6), channel_id=1, source_target_pairs={{0,16},{1,9},{2,18},{3,11},{4,20},{5,13},{6,22},{7,15},{8,24},{9,1... | collective-permute-start | bytes 958472 | tf_op jit(solution)/shard_map/ppermute | solution.py:458
  20.1 2.1 collective-permute-done.3
  22.3 3.6 %collective-permute-start.8 = (bf16[4,96,768]{2,1,0:T(8,128)(2,1)S(1)}, bf16[4,96,768]{2,1,0:T(8,128)(2,1)S(1)}, u32[]{:S(2)}, u32[]{:S(2)}) collective-permute-start(bf16[4,96,768]{2,1,0:T(8,128)(2,1)S(1)} %pad_maximum_fusion.4), channel_id=1, source_target_pairs={{0,16},{1,9},{2,18},{3,11},{4,20},{5,13},{6,22},{7,15},{8,24},{9,1... | collective-permute-start | bytes 1769480 | tf_op jit(solution)/shard_map/ppermute | solution.py:458
  25.9 11.4 %collective-permute-done.1 = bf16[2,104,768]{2,1,0:T(8,128)(2,1)S(1)} collective-permute-done((bf16[2,104,768]{2,1,0:T(8,128)(2,1)S(1)}, bf16[2,104,768]{2,1,0:T(8,128)(2,1)S(1)}, u32[]{:S(2)}, u32[]{:S(2)}) %collective-permute-start.1) | collective-permute-done | bytes 319520 | tf_op jit(solution)/shard_map/ppermute | solution.py:458
  37.7 12.1 %collective-permute-done.8 = bf16[4,96,768]{2,1,0:T(8,128)(2,1)S(1)} collective-permute-done((bf16[4,96,768]{2,1,0:T(8,128)(2,1)S(1)}, bf16[4,96,768]{2,1,0:T(8,128)(2,1)S(1)}, u32[]{:S(2)}, u32[]{:S(2)}) %collective-permute-start.8) | collective-permute-done | bytes 589856 | tf_op jit(solution)/shard_map/ppermute | solution.py:458
  51.0 7.8 %collective-permute-done.9 = bf16[4,96,768]{2,1,0:T(8,128)(2,1)S(1)} collective-permute-done((bf16[4,96,768]{2,1,0:T(8,128)(2,1)S(1)}, bf16[4,96,768]{2,1,0:T(8,128)(2,1)S(1)}, u32[]{:S(2)}, u32[]{:S(2)}) %collective-permute-start.9) | collective-permute-done | bytes 589856 | tf_op jit(solution)/shard_map/ppermute | solution.py:458
  61.6 14.9 %collective-permute-done.7.b1 = bf16[8,104,768]{2,1,0:T(8,128)(2,1)} collective-permute-done((bf16[8,104,768]{2,1,0:T(8,128)(2,1)S(1)}, bf16[8,104,768]{2,1,0:T(8,128)(2,1)}, u32[]{:S(2)}, u32[]{:S(2)}) %collective-permute-start.7) | collective-permute-done | bytes 1277984 | tf_op jit(solution)/shard_map/ppermute | solution.py:458
  79.8 12.5 %shard_map.368 = (f32[16,768]{1,0:T(8,128)S(1)}, f32[4,1,768]{2,1,0:T(1,128)S(1)}, bf16[4,768,768]{2,1,0:T(8,128)(2,1)S(1)}, bf16[416,768]{1,0:T(8,128)(2,1)S(1)...) custom-call(s32[80]{0:T(128)S(1)} %get-tuple-element.196.tab, ...), custom_call_target="tpu_custom_call" | custom-call | flops 1 | bytes 1 | tf_op jit(solution)/shard_map/pallas_call | solution.py:426
  96.1 5.1 %shard_map.369 = (bf16[4,768,768]{2,1,0:T(8,128)(2,1)S(1)}, bf16[2,416,768]{2,1,0:T(8,128)(2,1)S(1)}, f32[2,416,768]{2,1,0:T(8,128)S(1)}, bf16[416,768]{1,0:T(8,128)(2,1)S(1)}, bf16[16,96,768]{2,1,0:T(8,128)(2,1)S(1)}) custom-call(s32[80]{0:T(128)S(1)} %get-tuple-element.195.tab, bf16[416,768]{1,0:T(8,128)(2,1)S(1)} %get-tuple-element.112.normed_two, ...), custom_call_target="tpu_custom_call" | custom-call | flops 1 | bytes 1 | tf_op jit(solution)/shard_map/pallas_call | solution.py:426
  101.4 3.6 %shard_map.370 = (bf16[2,416,768]{2,1,0:T(8,128)(2,1)S(1)}, f32[2,416,768]{2,1,0:T(8,128)S(1)}, bf16[16,96,768]{2,1,0:T(8,128)(2,1)S(1)}) custom-call(s32[80]{0:T(128)S(1)} %get-tuple-element.195.tab, bf16[416,768]{1,0:T(8,128)(2,1)S(1)} %get-tuple-element.112.normed_two, bf16[416,768]{1,0:T(8,128)(2,1)S(1)} %get-tuple-element.117.grad_branch, ...), custom_call_target="tpu_custom_call" | custom-call | flops 99999997952 | bytes 1 | tf_op jit(solution)/shard_map/pallas_call | solution.py:426
  105.0 4.2 %collective-permute-done.15.b1 = bf16[8,96,768]{2,1,0:T(8,128)(2,1)S(1)} collective-permute-done((bf16[8,96,768]{2,1,0:T(8,128)(2,1)S(1)}, bf16[8,96,768]{2,1,0:T(8,128)(2,1)S(1)}, u32[]{:S(2)}, u32[]{:S(2)}) %collective-permute-start.15) | collective-permute-done | bytes 1179680 | tf_op jit(solution)/shard_map/ppermute | solution.py:458
  112.1 3.7 %shard_map.371 = (bf16[4,768,768]{2,1,0:T(8,128)(2,1)S(1)}, bf16[2,416,768]{2,1,0:T(8,128)(2,1)S(1)}, f32[2,1,768]{2,1,0:T(1,128)S(1)}, bf16[16,96,768]{2,1,0:T(8,128)(2,1)S(1)}) custom-call(s32[80]{0:T(128)S(1)} %get-tuple-element.194.tab, bf16[416,768]{1,0:T(8,128)(2,1)S(1)} %get-tuple-element.112.normed_two, ...), custom_call_target="tpu_custom_call" | custom-call | flops 1 | bytes 1 | tf_op jit(solution)/shard_map/pallas_call | solution.py:426
  116.0 3.4 %shard_map.372 = (bf16[2,416,768]{2,1,0:T(8,128)(2,1)S(1)}, f32[2,1,768]{2,1,0:T(1,128)S(1)}, bf16[16,96,768]{2,1,0:T(8,128)(2,1)S(1)}) custom-call(s32[80]{0:T(128)S(1)} %get-tuple-element.194.tab, bf16[416,768]{1,0:T(8,128)(2,1)S(1)} %get-tuple-element.112.normed_two, bf16[416,768]{1,0:T(8,128)(2,1)S(1)} %get-tuple-element.117.grad_branch, ...), custom_call_target="tpu_custom_call" | custom-call | flops 99999997952 | bytes 1 | tf_op jit(solution)/shard_map/pallas_call | solution.py:426
  121.9 7.3 %shard_map.373 = (bf16[416,768]{1,0:T(8,128)(2,1)S(1)}, f32[416,768]{1,0:T(8,128)S(1)}, bf16[416,768]{1,0:T(8,128)(2,1)S(1)}, f32[16,768]{1,0:T(8,128)S(1)}) custom-call(s32[80]{0:T(128)S(1)} %get-tuple-element.196.tab, bf16[2,416,768]{2,1,0:T(8,128)(2,1)S(1)} %get-tuple-element.116.act_sib, bf16[2,416,768]{2,1,0:T(8,128)(2,1)S(1)} %get-tuple-element.119.act_own, ...), custom_call_target="tpu_custom_call" | custom-call | flops 1 | bytes 1 | tf_op jit(solution)/shard_map/pallas_call | solution.py:426
  131.0 8.9 %shard_map.375 = (bf16[16,96,768]{2,1,0:T(8,128)(2,1)S(1)}, f32[416,768]{1,0:T(8,128)S(1)}, f32[2,2,192]{2,1,0:T(2,128)S(1)}) custom-call(s32[80]{0:T(128)S(1)} %get-tuple-element.196.tab, bf16[4,768,768]{2,1,0:T(8,128)(2,1)S(1)} %get-tuple-element.138.w1, bf16[416,768]{1,0:T(8,128)(2,1)S(1)} %get-tuple-element.139.normed, ...), custom_call_target="tpu_custom_call" | custom-call | flops 1 | bytes 1 | tf_op jit(solution)/shard_map/pallas_call | solution.py:426
  147.2 9.1 %shard_map.376 = (bf16[16,96,768]{2,1,0:T(8,128)(2,1)S(1)}, f32[416,768]{1,0:T(8,128)S(1)}, f32[2,2,192]{2,1,0:T(2,128)S(1)}) custom-call(s32[80]{0:T(128)S(1)} %get-tuple-element.196.tab, bf16[4,768,768]{2,1,0:T(8,128)(2,1)S(1)} %get-tuple-element.138.w1, bf16[416,768]{1,0:T(8,128)(2,1)S(1)} %get-tuple-element.139.normed, ...), custom_call_target="tpu_custom_call" | custom-call | flops 99999997952 | bytes 1 | tf_op jit(solution)/shard_map/pallas_call | solution.py:426
  156.3 3.5 %add_convert_fusion = bf16[8,96,768]{2,1,0:T(8,128)(2,1)} fusion(bf16[16,96,768]{2,1,0:T(8,128)(2,1)} %collective-permute-done.25, bf16[16,96,768]{2,1,0:T(8,128)(2,1)S(1)} %get-tuple-element.154), kind=kLoop, calls=%fused_computation | loop fusion | flops 2359296 | bytes 3538944 | tf_op jit(solution)/shard_map/convert_element_type | solution.py:501
  168.6 3.3 %collective-permute-done.28 = f32[24,768]{1,0:T(8,128)S(1)} collective-permute-done((f32[24,768]{1,0:T(8,128)S(1)}, f32[24,768]{1,0:T(8,128)S(1)}, u32[]{:S(2)}, u32[]{:S(2)}) %collective-permute-start.28) | collective-permute-done | bytes 73760 | tf_op jit(solution)/shard_map/ppermute | solution.py:444
  187.5 1.8 collective-permute-start.37
  190.5 3.8 %collective-permute-done.30 = bf16[4,96,768]{2,1,0:T(8,128)(2,1)S(1)} collective-permute-done((bf16[4,96,768]{2,1,0:T(8,128)(2,1)S(1)}, bf16[4,96,768]{2,1,0:T(8,128)(2,1)S(1)}, u32[]{:S(2)}, u32[]{:S(2)}) %collective-permute-start.30) | collective-permute-done | bytes 589856 | tf_op jit(solution)/shard_map/ppermute | solution.py:502
  195.9 1.9 collective-permute-start.35
  201.9 3.8 %collective-permute-done.34 = bf16[2,96,768]{2,1,0:T(8,128)(2,1)S(1)} collective-permute-done((bf16[2,96,768]{2,1,0:T(8,128)(2,1)S(1)}, bf16[2,96,768]{2,1,0:T(8,128)(2,1)S(1)}, u32[]{:S(2)}, u32[]{:S(2)}) %collective-permute-start.34) | collective-permute-done | bytes 294944 | tf_op jit(solution)/shard_map/ppermute | solution.py:502
  208.7 5.3 %collective-permute-done.36 = bf16[1,96,768]{2,1,0:T(8,128)(2,1)S(1)} collective-permute-done((bf16[1,96,768]{2,1,0:T(8,128)(2,1)S(1)}, bf16[1,96,768]{2,1,0:T(8,128)(2,1)S(1)}, u32[]{:S(2)}, u32[]{:S(2)}) %collective-permute-start.36) | collective-permute-done | bytes 147488 | tf_op jit(solution)/shard_map/ppermute | solution.py:502
  (201 shorter events, 74.9 us)
Async XLA Ops:
  4.1 9.3 %collective-permute-start = (bf16[1,104,768]{2,1,0:T(8,128)(2,1)S(1)}, bf16[1,104,768]{2,1,0:T(8,128)(2,1)S(1)}, u32[]{:S(2)}, u32[]{:S(2)}) collective-permute-start(bf16[1,104,768]{2,1,0:T(8,128)(2,1)S(1)} %bitcast.29), channel_id=1, source_target_pairs={{0,8},{1,17},{2,10},{3,19},{4,12},{5,21},{6,14},{7,23},{8,0},{9,25... | collective-permute-start | bytes 479240 | tf_op jit(solution)/shard_map/ppermute | solution.py:458
  13.4 8.8 %collective-permute-start.3 = (bf16[2,96,768]{2,1,0:T(8,128)(2,1)S(1)}, bf16[2,96,768]{2,1,0:T(8,128)(2,1)S(1)}, u32[]{:S(2)}, u32[]{:S(2)}) collective-permute-start(bf16[2,96,768]{2,1,0:T(8,128)(2,1)S(1)} %pad_maximum_fusion.7), channel_id=1, source_target_pairs={{0,4},{1,5},{2,6},{3,7},{4,0},{5,1},{6,2},{7,3},{8,12},{9,13},{10,... | collective-permute-start | bytes 884744 | tf_op jit(solution)/shard_map/ppermute | solution.py:458
  16.3 9.5 %collective-permute-start.6 = (bf16[2,96,768]{2,1,0:T(8,128)(2,1)S(1)}, bf16[2,96,768]{2,1,0:T(8,128)(2,1)S(1)}, u32[]{:S(2)}, u32[]{:S(2)}) collective-permute-start(bf16[2,96,768]{2,1,0:T(8,128)(2,1)S(1)} %pad_maximum_fusion.8), channel_id=1, source_target_pairs={{0,2},{1,17},{2,0},{3,19},{4,6},{5,21},{6,4},{7,23},{8,10},{9,25},... | collective-permute-start | bytes 884744 | tf_op jit(solution)/shard_map/ppermute | solution.py:458
  16.7 20.7 %collective-permute-start.1 = (bf16[2,104,768]{2,1,0:T(8,128)(2,1)S(1)}, bf16[2,104,768]{2,1,0:T(8,128)(2,1)S(1)}, u32[]{:S(2)}, u32[]{:S(2)}) collective-permute-start(bf16[2,104,768]{2,1,0:T(8,128)(2,1)S(1)} %pad_maximum_fusion.6), channel_id=1, source_target_pairs={{0,16},{1,9},{2,18},{3,11},{4,20},{5,13},{6,22},{7,15},{8,24},{9,1... | collective-permute-start | bytes 958472 | tf_op jit(solution)/shard_map/ppermute | solution.py:458
  22.3 27.6 %collective-permute-start.8 = (bf16[4,96,768]{2,1,0:T(8,128)(2,1)S(1)}, bf16[4,96,768]{2,1,0:T(8,128)(2,1)S(1)}, u32[]{:S(2)}, u32[]{:S(2)}) collective-permute-start(bf16[4,96,768]{2,1,0:T(8,128)(2,1)S(1)} %pad_maximum_fusion.4), channel_id=1, source_target_pairs={{0,16},{1,9},{2,18},{3,11},{4,20},{5,13},{6,22},{7,15},{8,24},{9,1... | collective-permute-start | bytes 1769480 | tf_op jit(solution)/shard_map/ppermute | solution.py:458
  37.6 21.3 %collective-permute-start.9 = (bf16[4,96,768]{2,1,0:T(8,128)(2,1)S(1)}, bf16[4,96,768]{2,1,0:T(8,128)(2,1)S(1)}, u32[]{:S(2)}, u32[]{:S(2)}) collective-permute-start(bf16[4,96,768]{2,1,0:T(8,128)(2,1)S(1)} %pad_maximum_fusion.5), channel_id=1, source_target_pairs={{0,16},{1,9},{2,18},{3,11},{4,20},{5,13},{6,22},{7,15},{8,24},{9,1... | collective-permute-start | bytes 1769480 | tf_op jit(solution)/shard_map/ppermute | solution.py:458
  37.6 21.3 %collective-permute-start.5 = (bf16[4,104,768]{2,1,0:T(8,128)(2,1)S(1)}, bf16[4,104,768]{2,1,0:T(8,128)(2,1)S(1)}, u32[]{:S(2)}, u32[]{:S(2)}) collective-permute-start(bf16[4,104,768]{2,1,0:T(8,128)(2,1)S(1)} %pad_maximum_fusion.3), channel_id=1, source_target_pairs={{0,4},{1,3},{2,6},{3,1},{4,0},{5,7},{6,2},{7,5},{8,12},{9,11},{10,... | collective-permute-start | bytes 1916936 | tf_op jit(solution)/shard_map/ppermute | solution.py:458
  59.1 17.4 %collective-permute-start.7 = (bf16[8,104,768]{2,1,0:T(8,128)(2,1)S(1)}, bf16[8,104,768]{2,1,0:T(8,128)(2,1)}, u32[]{:S(2)}, u32[]{:S(2)}) collective-permute-start(bf16[8,104,768]{2,1,0:T(8,128)(2,1)S(1)} %pad_maximum_fusion.b0), channel_id=1, source_target_pairs={{0,2},{1,5},{2,0},{3,7},{4,6},{5,1},{6,4},{7,3},{8,10},{9,13},{10,... | collective-permute-start | bytes 3833864 | tf_op jit(solution)/shard_map/ppermute | solution.py:458
  60.6 17.8 %collective-permute-start.10 = (bf16[8,104,768]{2,1,0:T(8,128)(2,1)S(1)}, bf16[8,104,768]{2,1,0:T(8,128)(2,1)}, u32[]{:S(2)}, u32[]{:S(2)}) collective-permute-start(bf16[8,104,768]{2,1,0:T(8,128)(2,1)S(1)} %pad_maximum_fusion.b0), channel_id=1, source_target_pairs={{0,1},{1,0},{2,3},{3,2},{4,5},{5,4},{6,7},{7,6},{8,9},{9,8},{10,11... | collective-permute-start | bytes 3833864 | tf_op jit(solution)/shard_map/ppermute | solution.py:461
  76.5 16.5 %collective-permute-start.12 = (bf16[8,96,768]{2,1,0:T(8,128)(2,1)}, bf16[8,96,768]{2,1,0:T(8,128)(2,1)}, u32[]{:S(2)}, u32[]{:S(2)}) collective-permute-start(bf16[8,96,768]{2,1,0:T(8,128)(2,1)} %pad_maximum_fusion.1.b0), channel_id=1, source_target_pairs={{0,8},{1,3},{2,10},{3,1},{4,12},{5,7},{6,14},{7,5},{8,0},{9,11},{1... | collective-permute-start | bytes 3538952 | tf_op jit(solution)/shard_map/ppermute | solution.py:458
  76.7 18.0 %collective-permute-start.13 = (bf16[8,96,768]{2,1,0:T(8,128)(2,1)}, bf16[8,96,768]{2,1,0:T(8,128)(2,1)S(1)}, u32[]{:S(2)}, u32[]{:S(2)}) collective-permute-start(bf16[8,96,768]{2,1,0:T(8,128)(2,1)} %pad_maximum_fusion.1.b0), channel_id=1, source_target_pairs={{0,1},{1,0},{2,3},{3,2},{4,5},{5,4},{6,7},{7,6},{8,9},{9,8},{10,11... | collective-permute-start | bytes 3538952 | tf_op jit(solution)/shard_map/ppermute | solution.py:461
  93.0 16.2 %collective-permute-start.15 = (bf16[8,96,768]{2,1,0:T(8,128)(2,1)S(1)}, bf16[8,96,768]{2,1,0:T(8,128)(2,1)S(1)}, u32[]{:S(2)}, u32[]{:S(2)}) collective-permute-start(bf16[8,96,768]{2,1,0:T(8,128)(2,1)S(1)} %pad_maximum_fusion.2.b0), channel_id=1, source_target_pairs={{0,4},{1,3},{2,6},{3,1},{4,0},{5,7},{6,2},{7,5},{8,12},{9,11},{10,... | collective-permute-start | bytes 3538952 | tf_op jit(solution)/shard_map/ppermute | solution.py:458
  93.5 17.5 %collective-permute-start.16 = (bf16[8,96,768]{2,1,0:T(8,128)(2,1)S(1)}, bf16[8,96,768]{2,1,0:T(8,128)(2,1)S(1)}, u32[]{:S(2)}, u32[]{:S(2)}) collective-permute-start(bf16[8,96,768]{2,1,0:T(8,128)(2,1)S(1)} %pad_maximum_fusion.2.b0), channel_id=1, source_target_pairs={{0,1},{1,0},{2,3},{3,2},{4,5},{5,4},{6,7},{7,6},{8,9},{9,8},{10,11... | collective-permute-start | bytes 3538952 | tf_op jit(solution)/shard_map/ppermute | solution.py:461
  101.2 8.0 %collective-permute-start.18 = (bf16[16,96,768]{2,1,0:T(8,128)(2,1)S(1)}, bf16[16,96,768]{2,1,0:T(8,128)(2,1)S(1)}, u32[]{:S(2)}, u32[]{:S(2)}) collective-permute-start(bf16[16,96,768]{2,1,0:T(8,128)(2,1)S(1)} %get-tuple-element.123), channel_id=1, source_target_pairs={{0,1},{1,0},{2,3},{3,2},{4,5},{5,4},{6,7},{7,6},{8,9},{9,8},{10,11... | collective-permute-start | bytes 7077896 | tf_op jit(solution)/shard_map/ppermute | solution.py:488
  109.6 19.6 %collective-permute-start.20 = (bf16[8,96,768]{2,1,0:T(8,128)(2,1)S(1)}, bf16[8,96,768]{2,1,0:T(8,128)(2,1)}, u32[]{:S(2)}, u32[]{:S(2)}) collective-permute-start(bf16[8,96,768]{2,1,0:T(8,128)(2,1)S(1)} %add_convert_fusion.2), channel_id=1, source_target_pairs={{0,2},{1,5},{2,0},{3,7},{4,6},{5,1},{6,4},{7,3},{8,10},{9,13},{10,... | collective-permute-start | bytes 3538952 | tf_op jit(solution)/shard_map/ppermute | solution.py:502
  120.7 23.8 %collective-permute-start.22 = (bf16[8,96,768]{2,1,0:T(8,128)(2,1)S(1)}, bf16[8,96,768]{2,1,0:T(8,128)(2,1)}, u32[]{:S(2)}, u32[]{:S(2)}) collective-permute-start(bf16[8,96,768]{2,1,0:T(8,128)(2,1)S(1)} %add_convert_fusion.1), channel_id=1, source_target_pairs={{0,4},{1,9},{2,6},{3,11},{4,0},{5,13},{6,2},{7,15},{8,12},{9,1},{1... | collective-permute-start | bytes 3538952 | tf_op jit(solution)/shard_map/ppermute | solution.py:502
  130.9 11.6 %collective-permute-start.21 = (bf16[4,96,768]{2,1,0:T(8,128)(2,1)S(1)}, bf16[4,96,768]{2,1,0:T(8,128)(2,1)S(1)}, u32[]{:S(2)}, u32[]{:S(2)}) collective-permute-start(bf16[4,96,768]{2,1,0:T(8,128)(2,1)S(1)} %add_convert_fusion.5), channel_id=1, source_target_pairs={{0,8},{1,3},{2,10},{3,1},{4,12},{5,7},{6,14},{7,5},{8,0},{9,11},{1... | collective-permute-start | bytes 1769480 | tf_op jit(solution)/shard_map/ppermute | solution.py:502
  139.9 16.5 %collective-permute-start.25 = (bf16[16,96,768]{2,1,0:T(8,128)(2,1)S(1)}, bf16[16,96,768]{2,1,0:T(8,128)(2,1)}, u32[]{:S(2)}, u32[]{:S(2)}) collective-permute-start(bf16[16,96,768]{2,1,0:T(8,128)(2,1)S(1)} %get-tuple-element.155), channel_id=1, source_target_pairs={{0,1},{1,0},{2,3},{3,2},{4,5},{5,4},{6,7},{7,6},{8,9},{9,8},{10,11... | collective-permute-start | bytes 7077896 | tf_op jit(solution)/shard_map/ppermute | solution.py:488
  143.9 12.4 %collective-permute-start.23 = (bf16[2,96,768]{2,1,0:T(8,128)(2,1)S(1)}, bf16[2,96,768]{2,1,0:T(8,128)(2,1)S(1)}, u32[]{:S(2)}, u32[]{:S(2)}) collective-permute-start(bf16[2,96,768]{2,1,0:T(8,128)(2,1)S(1)} %add_convert_fusion.8), channel_id=1, source_target_pairs={{0,4},{1,17},{2,6},{3,19},{4,0},{5,21},{6,2},{7,23},{8,12},{9,25},... | collective-permute-start | bytes 884744 | tf_op jit(solution)/shard_map/ppermute | solution.py:502
  145.7 10.6 %collective-permute-start.24 = (bf16[4,96,768]{2,1,0:T(8,128)(2,1)S(1)}, bf16[4,96,768]{2,1,0:T(8,128)(2,1)S(1)}, u32[]{:S(2)}, u32[]{:S(2)}) collective-permute-start(bf16[4,96,768]{2,1,0:T(8,128)(2,1)S(1)} %add_convert_fusion.4), channel_id=1, source_target_pairs={{0,2},{1,5},{2,0},{3,7},{4,6},{5,1},{6,4},{7,3},{8,10},{9,13},{10,... | collective-permute-start | bytes 1769480 | tf_op jit(solution)/shard_map/ppermute | solution.py:502
  159.8 19.2 %collective-permute-start.26 = (bf16[8,96,768]{2,1,0:T(8,128)(2,1)}, bf16[8,96,768]{2,1,0:T(8,128)(2,1)}, u32[]{:S(2)}, u32[]{:S(2)}) collective-permute-start(bf16[8,96,768]{2,1,0:T(8,128)(2,1)} %add_convert_fusion), channel_id=1, source_target_pairs={{0,2},{1,5},{2,0},{3,7},{4,6},{5,1},{6,4},{7,3},{8,10},{9,13},{10,... | collective-permute-start | bytes 3538952 | tf_op jit(solution)/shard_map/ppermute | solution.py:502
  176.9 7.9 %collective-permute-start.32 = (bf16[2,96,768]{2,1,0:T(8,128)(2,1)S(1)}, bf16[2,96,768]{2,1,0:T(8,128)(2,1)S(1)}, u32[]{:S(2)}, u32[]{:S(2)}) collective-permute-start(bf16[2,96,768]{2,1,0:T(8,128)(2,1)S(1)} %copy-done.37), channel_id=1, source_target_pairs={{0,8},{1,3},{2,10},{3,1},{4,12},{5,7},{6,14},{7,5},{8,0},{9,11},{1... | collective-permute-start | bytes 884744 | tf_op jit(solution)/shard_map/ppermute | solution.py:502
  180.8 13.5 %collective-permute-start.30 = (bf16[4,96,768]{2,1,0:T(8,128)(2,1)S(1)}, bf16[4,96,768]{2,1,0:T(8,128)(2,1)S(1)}, u32[]{:S(2)}, u32[]{:S(2)}) collective-permute-start(bf16[4,96,768]{2,1,0:T(8,128)(2,1)S(1)} %add_convert_fusion.3), channel_id=1, source_target_pairs={{0,8},{1,3},{2,10},{3,1},{4,12},{5,7},{6,14},{7,5},{8,0},{9,11},{1... | collective-permute-start | bytes 1769480 | tf_op jit(solution)/shard_map/ppermute | solution.py:502
  187.5 10.3 %collective-permute-start.37 = (bf16[1,96,768]{2,1,0:T(8,128)(2,1)S(1)}, bf16[1,96,768]{2,1,0:T(8,128)(2,1)S(1)}, u32[]{:S(2)}, u32[]{:S(2)}) collective-permute-start(bf16[1,96,768]{2,1,0:T(8,128)(2,1)S(1)} %add_convert_fusion.10), channel_id=1, source_target_pairs={{0,16},{1,17},{2,18},{3,19},{4,20},{5,21},{6,22},{7,23},{8,24},{9,... | collective-permute-start | bytes 442376 | tf_op jit(solution)/shard_map/ppermute | solution.py:502
  (59 other events, 456.5 us)

commit v3 on v2

--- a/solution.py
+++ b/solution.py
@@ -37,8 +37,8 @@
 
 BIT = {"c": 1, "x": 2, "y": 4, "1": 8, "2": 16}
 GATHER = (("12yx", "21xy"), ("xy21", "2y1x"), ("1x2y", "y21x"))
-SCATTER = (("2y1x", "12xy"), ("21xy", "2xy1"), ("2y1x", "12xy"))
-STEPS = "S0S1S2D0S0D1S1D2S2D1S1D0S0F0D2S2D0S0D1S1D2S2F1D0"
+SCATTER = (("21yx", "12xy"), ("2x1y", "x21y"), ("y2x1", "y21x"))
+STEPS = "S0S1S2D0S0D1S1D2S2D0S0F0D1S1D0S0D2S2D1S1F1D0"
 
 
 def offset_of(order, place):
@@ -75,7 +75,8 @@
 def plain_table():
     table = np.zeros((80,), np.int32)
     for place in range(32):
-        table[place] = (place % 8) * 4 + place // 8
+        part, along_x, block = place // 16, place // 8 % 2, place % 8
+        table[place] = block * 4 + along_x * 2 + part
     for block in range(8):
         table[32 + block] = block
         for group in range(4):
@@ -114,12 +115,12 @@
     return jnp.sum(values, axis=0, keepdims=True)
 
 
-def assemble(tab, parts, whole):
+def assemble(tab, first, parts, whole):
     for index, part in enumerate(parts):
-        for place in range(8):
-            owner = tab[index * 8 + place]
+        for place in range(4):
+            owner = tab[first + index * 4 + place]
             row = pl.multiple_of((owner >> 2) * BLOCK_ROWS, BLOCK_ROWS)
-            whole[owner & 3, pl.ds(row, BLOCK_ROWS), :] = part[place, 0:BLOCK_ROWS, :]
+            whole[(owner >> 1) & 1, pl.ds(row, BLOCK_ROWS), :] = part[place, 0:BLOCK_ROWS, :]
 
 
 def put_blocks(tab, group, grad, out):
@@ -143,10 +144,9 @@
     out[...] = jnp.concatenate(rows, axis=0).astype(BF16)
 
 
-def cut_kernel(values, out):
-    wide = values[...].astype(F32)
+def cut_rows(wide):
     rows = [wide[start : start + SEQ] for start in range(0, wide.shape[0], PAD)]
-    out[...] = jnp.concatenate(rows, axis=0).astype(BF16)
+    return jnp.concatenate(rows, axis=0).astype(BF16)
 
 
 def fence_kernel(values, out):
@@ -165,18 +165,47 @@
     out[...] = jnp.concatenate([block, extra], axis=0).astype(BF16)
 
 
-def attend_kernel(
+def attend_groups(imgs, tab, part, normed, qb, vb, w1, qkv, soft, att, attn):
+    keep = lax.broadcasted_iota(jnp.int32, (PAD, PAD), 1) < SEQ
+
+    def step(along_x, carry):
+        group = along_x * 2 + (tab[72] ^ part)
+        result = dot(normed[...], w1[along_x, :, 0:576])
+        qkv[along_x, :, 0:192] = (result[:, 0:192] + qb[group, 0:1, :]).astype(BF16)
+        qkv[along_x, :, 192:384] = result[:, 192:384].astype(BF16)
+        qkv[along_x, :, 384:576] = (result[:, 384:576] + vb[group, 0:1, :]).astype(BF16)
+        for head in range(HEADS_IN_GROUP):
+            c0 = head * HEAD_DIM
+            for img in range(imgs):
+                rows = slice(img * PAD, (img + 1) * PAD)
+                q = qkv[along_x, rows, c0 : c0 + 64]
+                k = qkv[along_x, rows, 192 + c0 : 256 + c0]
+                v = qkv[along_x, rows, 384 + c0 : 448 + c0]
+                scores = jnp.where(keep, dot_rt(q, k) * SCALE, -1e30)
+                top = jnp.max(scores, axis=-1, keepdims=True)
+                raised = jnp.exp(scores - top)
+                weights = raised / jnp.sum(raised, axis=-1, keepdims=True)
+                soft[along_x * (HEADS_IN_GROUP * imgs) + head * imgs + img] = weights
+                att[along_x, rows, c0 : c0 + 64] = dot(weights.astype(BF16), v).astype(BF16)
+        attn[...] += dot_rt(att[along_x], w1[along_x, :, 576:768])
+        return carry
+
+    lax.fori_loop(0, 2, step, 0)
+
+
+def attend_own_kernel(
     imgs, tab, tok, rep, b0, b1, b2, b3,
-    vec, bias, w1, normed, qkv, soft, att, attn, mid, normed_two, qb, vb,
+    vec, bias, start_rows, normed, qb, vb, w1, qkv, soft, att, attn,
 ):
     low = jnp.zeros((8, D), F32)
     high = jnp.zeros((8, D), F32)
     fill = jnp.zeros((8, D - 128), F32)
     for block in range(BLOCKS):
         place = tab[32 + block]
-        near = b0[place & 7].astype(F32)[BLOCK_ROWS:]
-        far = b1[place & 7].astype(F32)[BLOCK_ROWS:]
-        piece = jnp.where(place < 8, near, far)
+        piece = jnp.zeros((EXTRA, D), F32)
+        for index, part in enumerate((b0, b1, b2, b3)):
+            rows = part[place & 3].astype(F32)[BLOCK_ROWS:]
+            piece = jnp.where(place >> 2 == index, rows, piece)
         low += pltpu.roll(jnp.concatenate([piece[:, 0:128], fill], 1), block * BLOCK_ROWS, 1)
         high += pltpu.roll(jnp.concatenate([piece[:, 128:256], fill], 1), block * BLOCK_ROWS, 1)
         half = (block % 2) * 384
@@ -187,36 +216,23 @@
         cols = slice(group * GROUP_COLS, (group + 1) * GROUP_COLS)
         qb[group, 0:1, :] = vec[9:10, cols]
         vb[group, 0:1, :] = vec[10:11, cols]
-    assemble(tab, (b0, b1, b2, b3), w1)
+    assemble(tab, 0, (b0, b1, b2, b3), w1)
     start = mask_rows(tok, rep, vec)
+    start_rows[...] = start
     unit, _ = norm_stats(start)
     normed[...] = (unit * vec[0:1, :] + vec[1:2, :]).astype(BF16)
     attn[...] = jnp.zeros_like(attn)
-    keep = lax.broadcasted_iota(jnp.int32, (PAD, PAD), 1) < SEQ
-
-    def step(group, carry):
-        result = dot(normed[...], w1[group, :, 0:576])
-        qkv[group, :, 0:192] = (result[:, 0:192] + qb[group, 0:1, :]).astype(BF16)
-        qkv[group, :, 192:384] = result[:, 192:384].astype(BF16)
-        qkv[group, :, 384:576] = (result[:, 384:576] + vb[group, 0:1, :]).astype(BF16)
-        for head in range(HEADS_IN_GROUP):
-            c0 = head * HEAD_DIM
-            for img in range(imgs):
-                rows = slice(img * PAD, (img + 1) * PAD)
-                q = qkv[group, rows, c0 : c0 + 64]
-                k = qkv[group, rows, 192 + c0 : 256 + c0]
-                v = qkv[group, rows, 384 + c0 : 448 + c0]
-                scores = jnp.where(keep, dot_rt(q, k) * SCALE, -1e30)
-                top = jnp.max(scores, axis=-1, keepdims=True)
-                raised = jnp.exp(scores - top)
-                weights = raised / jnp.sum(raised, axis=-1, keepdims=True)
-                soft[group * (HEADS_IN_GROUP * imgs) + head * imgs + img] = weights
-                att[group, rows, c0 : c0 + 64] = dot(weights.astype(BF16), v).astype(BF16)
-        attn[...] += dot_rt(att[group], w1[group, :, 576:768])
-        return carry
-
-    lax.fori_loop(0, GROUPS, step, 0)
-    middle = start + vec[4:5, :] * (attn[...] + vec[7:8, :])
+    attend_groups(imgs, tab, 0, normed, qb, vb, w1, qkv, soft, att, attn)
+
+
+def attend_sib_kernel(
+    imgs, tab, vec, start_rows, normed, qb, vb, attn_in, b0, b1, b2, b3,
+    w1, qkv, soft, att, attn, mid, normed_two,
+):
+    assemble(tab, 16, (b0, b1, b2, b3), w1)
+    attn[...] = attn_in[...]
+    attend_groups(imgs, tab, 1, normed, qb, vb, w1, qkv, soft, att, attn)
+    middle = start_rows[...] + vec[4:5, :] * (attn[...] + vec[7:8, :])
     mid[...] = middle
     unit_two, _ = norm_stats(middle)
     normed_two[...] = (unit_two * vec[2:3, :] + vec[3:4, :]).astype(BF16)
@@ -225,7 +241,7 @@
 def expand_groups(tab, part, normed_two, grad_branch, bias, w2, active, slope, out):
     def step(along_x, carry):
         group = along_x * 2 + (tab[72] ^ part)
-        hidden = dot(normed_two[...], w2[group]) + bias[group, 0:1, :]
+        hidden = dot(normed_two[...], w2[along_x]) + bias[group, 0:1, :]
         cdf = 0.5 * (1.0 + lax.erf(hidden * 0.7071067811865476))
         pdf = 0.3989422804014327 * jnp.exp(-0.5 * hidden * hidden)
         act = (hidden * cdf).astype(BF16)
@@ -237,22 +253,25 @@
     lax.fori_loop(0, 2, step, 0)
 
 
+def expand_own_kernel(
+    tab, normed_two, cot, vec, bias, b0, b1, b2, b3, w2, active, slope, grad_branch, out
+):
+    assemble(tab, 0, (b0, b1, b2, b3), w2)
+    grad_branch[...] = (cot[...].astype(F32) * vec[5:6, :]).astype(BF16)
+    expand_groups(tab, 0, normed_two, grad_branch, bias, w2, active, slope, out)
+
+
 def expand_sib_kernel(
-    tab, normed_two, cot, vec, bias, b0, b1, b2, b3, w2, active, slope, grad_branch, out
-):
-    assemble(tab, (b0, b1, b2, b3), w2)
-    grad_branch[...] = (cot[...].astype(F32) * vec[5:6, :]).astype(BF16)
+    tab, normed_two, grad_branch, bias, b0, b1, b2, b3, w2, active, slope, out
+):
+    assemble(tab, 16, (b0, b1, b2, b3), w2)
     expand_groups(tab, 1, normed_two, grad_branch, bias, w2, active, slope, out)
-
-
-def expand_own_kernel(tab, normed_two, grad_branch, bias, w2, active, slope, out):
-    expand_groups(tab, 0, normed_two, grad_branch, bias, w2, active, slope, out)
 
 
 def hidden_groups(tab, part, normed_two, grad_branch, slope, w3, grad_hidden, bias_grad, out):
     def step(along_x, carry):
         group = along_x * 2 + (tab[72] ^ part)
-        grad = (dot(grad_branch[...], w3[group]) * slope[along_x]).astype(BF16)
+        grad = (dot(grad_branch[...], w3[along_x]) * slope[along_x]).astype(BF16)
         grad_hidden[along_x] = grad
         bias_grad[along_x, 0:1, :] = col_sum(grad.astype(F32))
         put_blocks(tab, group, dot_lt(normed_two[...], grad), out)
@@ -261,36 +280,31 @@
     lax.fori_loop(0, 2, step, 0)
 
 
-def hidden_sib_kernel(
-    tab, normed_two, grad_branch, slope, b0, b1, b2, b3, w3, grad_hidden, bias_grad, out
-):
-    assemble(tab, (b0, b1, b2, b3), w3)
-    hidden_groups(tab, 1, normed_two, grad_branch, slope, w3, grad_hidden, bias_grad, out)
-
-
-def hidden_own_kernel(tab, normed_two, grad_branch, slope, w3, grad_hidden, bias_grad, out):
-    hidden_groups(tab, 0, normed_two, grad_branch, slope, w3, grad_hidden, bias_grad, out)
+def hidden_kernel(
+    part, tab, normed_two, grad_branch, slope, b0, b1, b2, b3, w3, grad_hidden, bias_grad, out
+):
+    assemble(tab, 16 * part, (b0, b1, b2, b3), w3)
+    hidden_groups(tab, part, normed_two, grad_branch, slope, w3, grad_hidden, bias_grad, out)
 
 
 def middle_kernel(
-    tab, act_sib, act_own, hid_sib, hid_own, w2, w3, mid, attn, cot, vec,
+    act_sib, act_own, hid_sib, hid_own, w2_sib, w2_own, w3_sib, w3_own, mid, attn, cot, vec,
     block_out, grad_mid, grad_attn, sums, branch, grad_two,
 ):
-    branch[...] = jnp.zeros_like(branch)
-    grad_two[...] = jnp.zeros_like(grad_two)
     sums[...] = jnp.zeros_like(sums)
-    for part, active, grad_hidden in ((1, act_sib, hid_sib), (0, act_own, hid_own)):
-
-        def step(along_x, carry, part=part, active=active, grad_hidden=grad_hidden):
-            group = along_x * 2 + (tab[72] ^ part)
-            branch[...] += dot_rt(active[along_x], w3[group])
-            grad_two[...] += dot_rt(grad_hidden[along_x], w2[group])
-            return carry
-
-        lax.fori_loop(0, 2, step, 0)
+    found = jnp.zeros(branch.shape, F32)
+    for active, w3 in ((act_sib, w3_sib), (act_own, w3_own)):
+        for along_x in range(2):
+            found += dot_rt(active[along_x], w3[along_x])
+    branch[...] = found
+    found = jnp.zeros(branch.shape, F32)
+    for grad_hidden, w2 in ((hid_sib, w2_sib), (hid_own, w2_own)):
+        for along_x in range(2):
+            found += dot_rt(grad_hidden[along_x], w2[along_x])
+    grad_two[...] = found
     middle = mid[...]
     total = branch[...] + vec[8:9, :]
-    block_out[...] = (middle + vec[5:6, :] * total).astype(BF16)
+    block_out[...] = cut_rows(middle + vec[5:6, :] * total)
     grad_out = cot[...].astype(F32)
     sums[5:6, :] = col_sum(grad_out * total)
     sums[8:9, :] = col_sum(grad_out * vec[5:6, :])
@@ -311,15 +325,15 @@
 ):
     def step(along_x, carry):
         group = along_x * 2 + (tab[72] ^ part)
-        grad_att = dot(grad_attn[...], w1[group, :, 576:768]).astype(BF16)
+        grad_att = dot(grad_attn[...], w1[along_x, :, 576:768]).astype(BF16)
         for head in range(HEADS_IN_GROUP):
             c0 = head * HEAD_DIM
             for img in range(imgs):
                 rows = slice(img * PAD, (img + 1) * PAD)
-                q = qkv[group, rows, c0 : c0 + 64]
-                k = qkv[group, rows, 192 + c0 : 256 + c0]
-                v = qkv[group, rows, 384 + c0 : 448 + c0]
-                weights = soft[group * (HEADS_IN_GROUP * imgs) + head * imgs + img]
+                q = qkv[along_x, rows, c0 : c0 + 64]
+                k = qkv[along_x, rows, 192 + c0 : 256 + c0]
+                v = qkv[along_x, rows, 384 + c0 : 448 + c0]
+                weights = soft[along_x * (HEADS_IN_GROUP * imgs) + head * imgs + img]
                 grad = grad_att[rows, c0 : c0 + 64]
                 grad_soft = dot_rt(grad, v)
                 grad_v = dot_lt(weights.astype(BF16), grad)
@@ -333,9 +347,9 @@
         all_grads = gqkv[...]
         bias_sums[along_x, 0:1, :] = col_sum(all_grads[:, 0:192].astype(F32))
         bias_sums[along_x, 1:2, :] = col_sum(all_grads[:, 384:576].astype(F32))
-        grad_one[...] += dot_rt(all_grads, w1[group, :, 0:576])
+        grad_one[...] += dot_rt(all_grads, w1[along_x, :, 0:576])
         both = jnp.concatenate(
-            [dot_lt(normed[...], all_grads), dot_lt(grad_attn[...], att[group])], axis=1
+            [dot_lt(normed[...], all_grads), dot_lt(grad_attn[...], att[along_x])], axis=1
         )
         put_blocks(tab, group, both, out)
         return carry
@@ -373,7 +387,7 @@
     sums[0:1, :] = col_sum(grad * unit)
     sums[1:2, :] = col_sum(grad)
     grad_start = grad_mid[...] + norm_back(grad, vec[0:1, :], unit, rstd)
-    tok_grad[...] = (grad_start * (1.0 - replaced)).astype(BF16)
+    tok_grad[...] = cut_rows(grad_start * (1.0 - replaced))
     sums[6:7, :] = col_sum(grad_start * replaced)
     for group in range(GROUPS):
         cols = slice(group * GROUP_COLS, (group + 1) * GROUP_COLS)
@@ -438,6 +452,11 @@
     return lax.optimization_barrier((value, earlier))[0]
 
 
+def fence(*earlier):
+    mark = after(jnp.zeros((8, 128), F32), *earlier)
+    return call(fence_kernel, (mark,), (shape((8, 128), F32),), flops=LONG, table=False)[0]
+
+
 def add_across(values, *masks):
     for mask in masks:
         pairs = [(dev, dev ^ mask) for dev in range(32)]
@@ -445,25 +464,46 @@
     return values
 
 
+def send_all(values, one, two):
+    return [
+        lax.ppermute(values, AXES, [(dev, dev ^ mask) for dev in range(32)])
+        for mask in (one, two, one ^ two)
+    ]
+
+
+def take_all(values, parts):
+    return (values + parts[0]) + (parts[1] + parts[2])
+
+
 class Gather:
     def __init__(self, block, orders):
         self.held = block[None]
         self.orders = orders
         self.level = 0
-        self.taken = None
+
+    def send(self, values, level):
+        return lax.ppermute(values, AXES, pairs_of(self.orders, level))
 
     def start(self, *earlier):
         if earlier:
             self.held = after(self.held, *earlier)
-        self.taken = lax.ppermute(self.held, AXES, pairs_of(self.orders, self.level))
+        if self.level < 3:
+            self.taken = self.send(self.held, self.level)
+            if self.level == 2:
+                self.far = self.send(self.held, 3)
+        else:
+            self.last = self.send(self.held, 3)
         self.level += 1
-        if self.level == 4:
-            self.held_sib = lax.ppermute(self.held, AXES, CORE_PAIRS)
 
     def take(self):
-        if self.level < 4:
+        if self.level < 3:
             self.held = jnp.concatenate([self.held, self.taken], axis=0)
-        return self.taken
+            return self.taken
+        if self.level == 3:
+            self.near = self.held
+            self.held = self.taken
+            return self.taken, self.far
+        return self.last
 
     def finish(self, *earlier):
         while self.level < 4:
@@ -471,11 +511,12 @@
             self.take()
             self.start()
 
-    def parts(self, *earlier):
-        if earlier:
-            self.taken = after(self.taken, *earlier)
-        self.taken_sib = lax.ppermute(self.taken, AXES, CORE_PAIRS)
-        return self.held, self.taken, self.held_sib, self.taken_sib
+    def own(self):
+        return self.near, self.taken, self.far, self.last
+
+    def sib(self, *earlier):
+        own = self.near, self.taken, self.far, after(self.last, *earlier)
+        return tuple(lax.ppermute(values, AXES, CORE_PAIRS) for values in own)
 
 
 class Scatter:
@@ -502,6 +543,9 @@
         self.terms.append(lax.ppermute(sent, AXES, pairs_of(self.orders, self.level)))
         return sent
 
+    def hold(self, *earlier):
+        self.terms[-1] = after(self.terms[-1], *earlier)
+
     def result(self):
         return self.total(0, 1)[0]
 
@@ -509,8 +553,9 @@
 def gather_plain(block):
     whole = lax.all_gather(block, AXES, axis=0, tiled=False)
     whole = whole.reshape(-1, GROUPS, *block.shape).transpose(1, 0, 2, 3)
-    whole = whole.reshape(GROUPS, BLOCKS, BLOCK_ROWS, D)
-    return tuple(whole[group] for group in range(GROUPS))
+    whole = whole.reshape(2, 2, BLOCKS, BLOCK_ROWS, D).transpose(1, 0, 2, 3, 4)
+    whole = whole.reshape(2, 4, 4, BLOCK_ROWS, D)
+    return tuple(tuple(part[index] for index in range(4)) for part in whole)
 
 
 def scatter_plain(own, sib, n_dp):
@@ -559,10 +604,6 @@
     replaced = jnp.where((patch_mask == 1) & (positions > 0), 1.0, 0.0).astype(F32)
     rep = padded(replaced)
 
-    def cut(values):
-        out = shape((imgs * SEQ, D))
-        return call(cut_kernel, (values,), (out,), table=False)[0]
-
     def pad_rows(values):
         return call(pad_kernel, (values,), (shape((rows, D)),), flops=LONG, table=False)[0]
 
@@ -585,14 +626,11 @@
             for piece, orders in zip((piece_one, piece_two, piece_three), GATHER, strict=True)
         ]
         seen = {}
-        mark = jnp.zeros((8, 128), F32)
         for kind, index in zip(STEPS[0::2], STEPS[1::2], strict=True):
             stream = streams[int(index)]
             held = [stream.held for stream in streams]
             if kind == "X":
-                mark = after(mark, *held, *seen.values())
-                (mark,) = call(fence_kernel, (mark,), (shape((8, 128), F32),), flops=LONG, table=False)
-                seen["mark"] = mark
+                seen["mark"] = fence(*held, *seen.values())
             elif kind == "F":
                 if index == "0":
                     tok = pad_rows(after(tokens, *held))
@@ -604,14 +642,15 @@
                 stream.start(*seen.values())
             else:
                 seen[index] = stream.take()
-        w1_parts = streams[0].parts(*[seen[name] for name in seen if name not in "12"])
+        marks = [seen[name] for name in seen if name not in "12"]
+        w1_own, w1_sib = streams[0].own(), streams[0].sib(*marks)
     else:
         tables = [jnp.asarray(plain_table())] * 3
         tok, cot = pad_rows(tokens), pad_rows(cotangent)
         piece_one = jnp.concatenate(
             [project_qkv[0], project_qkv[1], project_qkv[2], project_out.T], axis=1
         ).astype(BF16)
-        w1_parts, w2_parts, w3_parts = (
+        w1_parts, (w2_own, w2_sib), (w3_own, w3_sib) = (
             gather_plain(piece) for piece in (piece_one, piece_two, piece_three)
         )
         vector_all = lax.all_gather(vectors.astype(BF16), "dp", axis=1, tiled=True)
@@ -621,7 +660,13 @@
         extras = extras.at[:, :, 0:BLOCK_ROWS].set(by_block[:, 0:8])
         extras = extras.at[:, 0:3, 128 : 128 + BLOCK_ROWS].set(by_block[:, 8:11])
         extras = extras.at[:, 0, 256:640].set(bias_all.reshape(BLOCKS, FF // BLOCKS))
-        w1_parts = tuple(jnp.concatenate([part, extras], axis=1) for part in w1_parts)
+        w1_own, w1_sib = (
+            tuple(
+                jnp.concatenate([part, extras[4 * (at % 2) : 4 * (at % 2) + 4]], axis=1)
+                for at, part in enumerate(parts)
+            )
+            for parts in w1_parts
+        )
 
     full = (GROUPS, D, D)
     row_f32 = shape((rows, D), F32)
@@ -630,61 +675,64 @@
     two_low = shape((2, rows, D))
     two_f32 = shape((2, rows, D), F32)
     two_bias = shape((2, 1, D), F32)
-    group_bias = pltpu.VMEM((GROUPS, 1, GROUP_COLS), F32)
-    n_soft = GROUPS * HEADS_IN_GROUP * imgs
-    vec, bias, w1, normed, qkv, soft, att, attn, mid, normed_two = call(
-        functools.partial(attend_kernel, imgs),
-        (tables[0], tok, rep, *w1_parts),
+    group_bias = shape((GROUPS, 1, GROUP_COLS), F32)
+    weights = shape((2, D, D))
+    heads = (
+        shape((2, rows, 3 * GROUP_COLS)),
+        shape((2 * HEADS_IN_GROUP * imgs, PAD, PAD), F32),
+        shape((2, rows, GROUP_COLS)),
+        row_f32,
+    )
+    vec, bias, start_rows, normed, qb, vb, w1_own, *heads_own, attn = call(
+        functools.partial(attend_own_kernel, imgs),
+        (tables[0], tok, rep, *w1_own),
         (
-            shape((16, D), F32),
-            shape((GROUPS, 1, D), F32),
-            shape(full),
-            row_low,
-            shape((GROUPS, rows, 3 * GROUP_COLS)),
-            shape((n_soft, PAD, PAD), F32),
-            shape((GROUPS, rows, GROUP_COLS)),
-            row_f32,
-            row_f32,
-            row_low,
+            shape((16, D), F32), shape((GROUPS, 1, D), F32), row_f32, row_low,
+            group_bias, group_bias, weights, *heads,
         ),
-        (group_bias, group_bias),
         flops=SHORT,
     )
+    w1_sib, *heads_sib, attn, mid, normed_two = call(
+        functools.partial(attend_sib_kernel, imgs),
+        (tables[0], vec, start_rows, normed, qb, vb, attn, *w1_sib),
+        (weights, *heads, row_f32, row_low),
+        flops=SHORT,
+    )
     if direct:
-        streams[1].finish(normed_two)
-        streams[2].finish(normed_two)
-        w2_parts = streams[1].parts(normed_two)
+        streams[1].finish(normed)
+        w2_own, w2_sib = streams[1].own(), streams[1].sib(normed_two)
     three, two, one = (Scatter(SCATTER[index]) for index in (2, 1, 0))
-    w2, act_sib, slope_sib, grad_branch, reduce_sib = call(
+    w2_own, act_own, slope_own, grad_branch, reduce_own = call(
+        expand_own_kernel,
+        (tables[1], normed_two, cot, vec, bias, *w2_own),
+        (weights, two_low, two_f32, row_low, half),
+        flops=LONG,
+    )
+    if direct:
+        streams[2].finish(grad_branch)
+    w2_sib, act_sib, slope_sib, reduce_sib = call(
         expand_sib_kernel,
-        (tables[1], normed_two, cot, vec, bias, *w2_parts),
-        (shape(full), two_low, two_f32, row_low, half),
+        (tables[1], normed_two, grad_branch, bias, *w2_sib),
+        (weights, two_low, two_f32, half),
         flops=SHORT,
     )
     if direct:
         three.swap(reduce_sib)
-    act_own, slope_own, reduce_own = call(
-        expand_own_kernel,
-        (tables[1], normed_two, grad_branch, bias, w2),
-        (two_low, two_f32, half),
+        w3_own, w3_sib = streams[2].own(), streams[2].sib(reduce_sib)
+    w3_sib, hid_sib, units_sib, expand_sib = call(
+        functools.partial(hidden_kernel, 1),
+        (tables[2], normed_two, grad_branch, slope_sib, *w3_sib),
+        (weights, two_low, two_bias, half),
         flops=LONG,
-    )
-    if direct:
-        w3_parts = streams[2].parts(reduce_own)
-        three.add(reduce_own)
-        w3_parts = after(w3_parts, three.step())
-    w3, hid_sib, units_sib, expand_sib = call(
-        hidden_sib_kernel,
-        (tables[2], normed_two, grad_branch, slope_sib, *w3_parts),
-        (shape(full), two_low, two_bias, half),
-        flops=SHORT,
     )
     if direct:
         two.swap(expand_sib)
-    hid_own, units_own, expand_own = call(
-        hidden_own_kernel,
-        (tables[2], normed_two, grad_branch, slope_own, w3),
-        (two_low, two_bias, half),
+        three.add(reduce_own)
+        slope_own = after(slope_own, three.step(expand_sib))
+    w3_own, hid_own, units_own, expand_own = call(
+        functools.partial(hidden_kernel, 0),
+        (tables[2], normed_two, grad_branch, slope_own, *w3_own),
+        (weights, two_low, two_bias, half),
         flops=LONG,
     )
     if direct:
@@ -692,61 +740,71 @@
         mid = after(mid, two.step())
     block_out, grad_mid, grad_attn, sums = call(
         middle_kernel,
-        (tables[0], act_sib, act_own, hid_sib, hid_own, w2, w3, mid, attn, cot, vec),
-        (row_low, row_f32, row_low, shape((16, D), F32)),
+        (
+            act_sib, act_own, hid_sib, hid_own, w2_sib, w2_own, w3_sib, w3_own,
+            mid, attn, cot, vec,
+        ),
+        (shape(tokens.shape), row_f32, row_low, shape((16, D), F32)),
         (pltpu.VMEM((rows, D), F32), pltpu.VMEM((rows, D), F32)),
         flops=SHORT,
-    )
-    if direct:
-        grad_attn = after(grad_attn, three.step(sums))
-    shared = (w1, normed, qkv, soft, att, grad_attn)
+        table=False,
+    )
     held = pltpu.VMEM((rows, 3 * GROUP_COLS), BF16)
     bias_sums = (2, 2, GROUP_COLS)
     first_sib, grad_one, bias_sib = call(
         functools.partial(back_sib_kernel, imgs),
-        (tables[0], *shared),
+        (tables[0], w1_sib, normed, *heads_sib, grad_attn),
         (half, row_f32, shape(bias_sums, F32)),
         (held,),
         flops=SHORT,
     )
     if direct:
         one.swap(first_sib)
-        grad_one = after(grad_one, three.step(grad_one), two.step(grad_one))
+        grad_one = after(grad_one, three.step(grad_one))
     first_own, grad_one, bias_own = call(
         functools.partial(back_own_kernel, imgs),
-        (tables[0], *shared, grad_one),
+        (tables[0], w1_own, normed, *heads_own, grad_attn, grad_one),
         (half, row_f32, shape(bias_sums, F32)),
         (held,),
         flops=LONG,
     )
     if direct:
-        first_own, grad_one = after((first_own, grad_one), three.terms[-1], two.terms[-1])
+        first_own, grad_one = after((first_own, grad_one), three.terms[-1])
         one.add(first_own)
         sent = one.step()
-        grad_one = after(grad_one, three.step(sent), two.step(sent))
+        sent_three, sent_two = three.step(sent), two.step(sent)
+        grad_one = after(grad_one, sent)
     tok_grad, sums = call(
         start_kernel,
         (
             tables[0], tok, rep, vec, grad_one, bias_sib, bias_own, grad_mid, sums,
             units_sib, units_own,
         ),
-        (row_low, shape((24, D), F32)),
+        (shape(tokens.shape), shape((24, D), F32)),
     )
 
     if direct:
-        sums = add_across(sums, 1, 8, 16)
-        block_rows, token_rows = cut(block_out), cut(tok_grad)
-        sent = one.step(sums, block_rows, token_rows)
-        grad_three = after(three.result(), sent)
+        sums = add_across(sums, 1)
+        one.hold(fence(sums, sent_three, sent_two))
+        parts = send_all(sums, 8, 16)
+        sent = one.step()
+        mark = sent
+        sums = take_all(sums, after(parts, mark))
+        three.step(mark)
+        two.step(mark)
+        sent = one.step()
+        mark = sent
+        parts = send_all(after(sums, mark), 2, 4)
+        three.hold(mark)
+        two.step(mark)
+        sent = one.step()
+        sums = take_all(sums, after(parts, sent))
+        grad_three = three.result()
         states_three = adam_update(
             reduce_weight, grad_three.T, first_reduce, second_reduce, RATE_MATRIX, DECAY
         )
-        sums = add_across(after(sums, sent), 4)
-        sent_two = two.step(sent)
-        sent = one.step(states_three[0], sent_two, sums)
-        sums = add_across(after(sums, sent), 2)
-        sent = one.step(sums)
-        grad_two = after(two.result(), sent)
+        two.hold(sent)
+        grad_two = two.result()
         partial = sum(term[0].astype(F32) for term in one.terms[:-1])
         finished = call(
             finish_kernel,
@@ -758,7 +816,6 @@
             table=False,
         )
     else:
-        block_rows, token_rows = cut(block_out), cut(tok_grad)
         grad_three = scatter_plain(reduce_own, reduce_sib, n_dp)
         grad_two = scatter_plain(expand_own, expand_sib, n_dp)
         grad_one = scatter_plain(first_own, first_sib, n_dp)
@@ -776,8 +833,8 @@
     vector_grad = lax.dynamic_slice_in_dim(sums[0:11], spot * wide, wide, 1)
     grad_bias = lax.dynamic_slice_in_dim(sums[16:20].reshape(-1), spot * units, units, 0)
     return (
-        block_rows,
-        token_rows,
+        block_out,
+        tok_grad,
         *finished,
         *adam_update(expand_weight, grad_two, first_expand, second_expand, RATE_MATRIX, DECAY),
         *states_three,

time: 216 us -> 206 us (0.954)
  the two profiles are of different devices: /device:TPU:0 before, /device:TPU:1 now
where the time goes in v3:
time: 206 us; the launch traced here: 205 us
  waiting for transfers between devices  73.5 us (36%)
  Pallas kernels  57.4 us (28%)
  starting transfers between devices  39.1 us (19%)
  other arithmetic  26 us (13%)
  local copies, waits for them, and re-layouts  7.19 us (3%)
    pallas_call x14, Pallas kernels, call(): pl.pallas_call(kernel, out_shape=outs, in_specs=[SMEM] * table + [VMEM] *...  57.4 us
    ppermute x15, waiting for transfers between devices, send(): return lax.ppermute(values, AXES, pairs_of(self.orders, level))  44 us
    ppermute x12, waiting for transfers between devices, step(): lax.ppermute(sent, AXES, pairs_of(self.orders, self.level))  23.3 us
    convert_element_type x12, other arithmetic, step(): sent = self.total(size, 2 * size).astype(BF16)  15.6 us
    ppermute x15, starting transfers between devices, send(): return lax.ppermute(values, AXES, pairs_of(self.orders, level))  12.5 us
    ppermute x12, starting transfers between devices, sib(): return tuple((lax.ppermute(values, AXES, CORE_PAIRS) for values in own))  11 us
    ppermute x12, starting transfers between devices, step(): lax.ppermute(sent, AXES, pairs_of(self.orders, self.level))  7.21 us
    ppermute x6, starting transfers between devices, send_all(): lax.ppermute(values, AXES, [(dev, dev ^ mask) for dev in range(32)])  6.71 us
  transfers between devices with their start and end apart: 49, of which 18 were waited for; matrix products, arithmetic and copies ran while one was open for 14% of the time, Pallas kernels for 27%

profile of v3, /device:TPU:1, one launch (start us, length us, event | category | flops | bytes accessed | tf_op | source)
XLA Modules:
  0.0 204.6 jit_solution(5834374608274684101)
XLA Ops:
  4.1 3.2 %collective-permute-start = (bf16[1,104,768]{2,1,0:T(8,128)(2,1)S(1)}, bf16[1,104,768]{2,1,0:T(8,128)(2,1)S(1)}, u32[]{:S(2)}, u32[]{:S(2)}) collective-permute-start(bf16[1,104,768]{2,1,0:T(8,128)(2,1)S(1)} %bitcast.32), channel_id=1, source_target_pairs={{0,8},{1,17},{2,10},{3,19},{4,12},{5,21},{6,14},{7,23},{8,0},{9,25... | collective-permute-start | bytes 479240 | tf_op jit(solution)/shard_map/ppermute | solution.py:485
  12.0 5.1 %collective-permute-done.2 = bf16[1,96,768]{2,1,0:T(8,128)(2,1)S(1)} collective-permute-done((bf16[1,96,768]{2,1,0:T(8,128)(2,1)S(1)}, bf16[1,96,768]{2,1,0:T(8,128)(2,1)S(1)}, u32[]{:S(2)}, u32[]{:S(2)}) %collective-permute-start.2) | collective-permute-done | bytes 147488 | tf_op jit(solution)/shard_map/ppermute | solution.py:485
  18.9 5.2 %collective-permute-done.6 = bf16[2,96,768]{2,1,0:T(8,128)(2,1)S(1)} collective-permute-done((bf16[2,96,768]{2,1,0:T(8,128)(2,1)S(1)}, bf16[2,96,768]{2,1,0:T(8,128)(2,1)S(1)}, u32[]{:S(2)}, u32[]{:S(2)}) %collective-permute-start.6) | collective-permute-done | bytes 294944 | tf_op jit(solution)/shard_map/ppermute | solution.py:485
  24.2 2.5 %collective-permute-done.1 = bf16[2,104,768]{2,1,0:T(8,128)(2,1)S(1)} collective-permute-done((bf16[2,104,768]{2,1,0:T(8,128)(2,1)S(1)}, bf16[2,104,768]{2,1,0:T(8,128)(2,1)S(1)}, u32[]{:S(2)}, u32[]{:S(2)}) %collective-permute-start.1) | collective-permute-done | bytes 319520 | tf_op jit(solution)/shard_map/ppermute | solution.py:485
  30.2 18.2 %collective-permute-done.13 = bf16[2,96,768]{2,1,0:T(8,128)(2,1)S(1)} collective-permute-done((bf16[2,96,768]{2,1,0:T(8,128)(2,1)S(1)}, bf16[2,96,768]{2,1,0:T(8,128)(2,1)S(1)}, u32[]{:S(2)}, u32[]{:S(2)}) %collective-permute-start.13) | collective-permute-done | bytes 294944 | tf_op jit(solution)/shard_map/ppermute | solution.py:485
  49.3 2.4 %collective-permute-start.8 = (bf16[4,104,768]{2,1,0:T(8,128)(2,1)S(1)}, bf16[4,104,768]{2,1,0:T(8,128)(2,1)}, u32[]{:S(2)}, u32[]{:S(2)}) collective-permute-start(bf16[4,104,768]{2,1,0:T(8,128)(2,1)S(1)} %pad_maximum_fusion.b0), channel_id=1, source_target_pairs={{0,1},{1,0},{2,3},{3,2},{4,5},{5,4},{6,7},{7,6},{8,9},{9,8},{10,11... | collective-permute-start | bytes 1916936 | tf_op jit(solution)/shard_map/ppermute | solution.py:519
  55.6 7.0 %collective-permute-done.7.b3 = bf16[4,104,768]{2,1,0:T(8,128)(2,1)} collective-permute-done((bf16[4,104,768]{2,1,0:T(8,128)(2,1)}, bf16[4,104,768]{2,1,0:T(8,128)(2,1)}, u32[]{:S(2)}, u32[]{:S(2)}) %collective-permute-start.7) | collective-permute-done | bytes 639008 | tf_op jit(solution)/shard_map/ppermute | solution.py:485
  65.3 6.9 %shard_map.367 = (f32[16,768]{1,0:T(8,128)S(1)}, f32[4,1,768]{2,1,0:T(1,128)S(1)}, f32[416,768]{1,0:T(8,128)S(1)}, bf16[416,768]{1,0:T(8,128)(2,1)S(1)}, f32[4,1...) custom-call(s32[80]{0:T(128)S(1)} %get-tuple-element.213.tab, ...), custom_call_target="tpu_custom_call" | custom-call | flops 1 | bytes 1 | tf_op jit(solution)/shard_map/pallas_call | solution.py:440
  74.5 6.9 %shard_map.369 = (bf16[2,768,768]{2,1,0:T(8,128)(2,1)S(1)}, bf16[2,416,576]{2,1,0:T(8,128)(2,1)S(1)}, f32[12,208,208]{2,1,0:T(8,128)S(1)}, bf16[2,416,192]{2,1,0...) custom-call(s32[80]{0:T(128)S(1)} %get-tuple-element.213.tab, ...), custom_call_target="tpu_custom_call" | custom-call | flops 1 | bytes 1 | tf_op jit(solution)/shard_map/pallas_call | solution.py:440
  81.6 4.7 %shard_map.370 = (bf16[2,768,768]{2,1,0:T(8,128)(2,1)S(1)}, bf16[2,416,768]{2,1,0:T(8,128)(2,1)S(1)}, f32[2,416,768]{2,1,0:T(8,128)S(1)}, bf16[416,768]{1,0:T(8,128)(2,1)S(1)}, bf16[16,96,768]{2,1,0:T(8,128)(2,1)S(1)}) custom-call(s32[80]{0:T(128)S(1)} %get-tuple-element.214.tab, bf16[416,768]{1,0:T(8,128)(2,1)S(1)} %get-tuple-element.126.normed_two, ...), custom_call_target="tpu_custom_call" | custom-call | flops 99999997952 | bytes 1 | tf_op jit(solution)/shard_map/pallas_call | solution.py:440
  88.0 2.7 %collective-permute-start.19 = (bf16[4,96,768]{2,1,0:T(8,128)(2,1)}, bf16[4,96,768]{2,1,0:T(8,128)(2,1)S(1)}, u32[]{:S(2)}, u32[]{:S(2)}) collective-permute-start(bf16[4,96,768]{2,1,0:T(8,128)(2,1)} %collective-permute-done.15.b3), channel_id=1, source_target_pairs={{0,1},{1,0},{2,3},{3,2},{4,5},{5,4},{6,7},{7,6},{8,9},{9,8},{10,11... | collective-permute-start | bytes 1769480 | tf_op jit(solution)/shard_map/ppermute | solution.py:519
  92.5 3.8 %shard_map.371 = (bf16[2,768,768]{2,1,0:T(8,128)(2,1)S(1)}, bf16[2,416,768]{2,1,0:T(8,128)(2,1)S(1)}, f32[2,416,768]{2,1,0:T(8,128)S(1)}, bf16[16,96,768]{2,1,0:T(8,128)(2,1)S(1)}) custom-call(s32[80]{0:T(128)S(1)} %get-tuple-element.214.tab, bf16[416,768]{1,0:T(8,128)(2,1)S(1)} %get-tuple-element.126.normed_two, ...), custom_call_target="tpu_custom_call" | custom-call | flops 1 | bytes 1 | tf_op jit(solution)/shard_map/pallas_call | solution.py:440
  96.3 3.4 %collective-permute-done.25.b3 = bf16[4,96,768]{2,1,0:T(8,128)(2,1)S(1)} collective-permute-done((bf16[4,96,768]{2,1,0:T(8,128)(2,1)S(1)}, bf16[4,96,768]{2,1,0:T(8,128)(2,1)S(1)}, u32[]{:S(2)}, u32[]{:S(2)}) %collective-permute-start.25) | collective-permute-done | bytes 589856 | tf_op jit(solution)/shard_map/ppermute | solution.py:485
  102.2 3.6 %shard_map.372 = (bf16[2,768,768]{2,1,0:T(8,128)(2,1)S(1)}, bf16[2,416,768]{2,1,0:T(8,128)(2,1)S(1)}, f32[2,1,768]{2,1,0:T(1,128)S(1)}, bf16[16,96,768]{2,1,0:T(8,128)(2,1)S(1)}) custom-call(s32[80]{0:T(128)S(1)} %get-tuple-element.212.tab, bf16[416,768]{1,0:T(8,128)(2,1)S(1)} %get-tuple-element.126.normed_two, ...), custom_call_target="tpu_custom_call" | custom-call | flops 99999997952 | bytes 1 | tf_op jit(solution)/shard_map/pallas_call | solution.py:440
  109.1 3.7 %shard_map.373 = (bf16[2,768,768]{2,1,0:T(8,128)(2,1)S(1)}, bf16[2,416,768]{2,1,0:T(8,128)(2,1)S(1)}, f32[2,1,768]{2,1,0:T(1,128)S(1)}, bf16[16,96,768]{2,1,0:T(8,128)(2,1)S(1)}) custom-call(s32[80]{0:T(128)S(1)} %get-tuple-element.212.tab, bf16[416,768]{1,0:T(8,128)(2,1)S(1)} %get-tuple-element.126.normed_two, ...), custom_call_target="tpu_custom_call" | custom-call | flops 99999997952 | bytes 1 | tf_op jit(solution)/shard_map/pallas_call | solution.py:440
  114.4 5.6 %shard_map.374 = (bf16[394,768]{1,0:T(8,128)(2,1)}, f32[416,768]{1,0:T(8,128)S(1)}, bf16[416,768]{1,0:T(8,128)(2,1)S(1)}, f32[16,768]{1,0:T(8,128)S(1)}) custom-call(bf16[2,416,768]{2,1,0:T(8,128)(2,1)S(1)} %get-tuple-element.130.act_sib, bf16[2,416,768]{2,1,0:T(8,128)(2,1)S(1)} %get-tuple-element.131.act_own, ...), custom_call_target="tpu_custom_call" | custom-call | flops 1 | bytes 1 | tf_op jit(solution)/shard_map/pallas_call | solution.py:440
  120.0 8.8 %shard_map.375 = (bf16[16,96,768]{2,1,0:T(8,128)(2,1)S(1)}, f32[416,768]{1,0:T(8,128)S(1)}, f32[2,2,192]{2,1,0:T(2,128)S(1)}) custom-call(s32[80]{0:T(128)S(1)} %get-tuple-element.213.tab, bf16[2,768,768]{2,1,0:T(8,128)(2,1)S(1)} %get-tuple-element.157.w1, bf16[416,768]{1,0:T(8,128)(2,1)S(1)} %copy-done.1, bf16[2,416,576]{2,1,0:T(8,128)(2,1)S(1)} %get-tuple-element.158.qkv, ...), custom_call_target="tpu_custom_call" | custom-call | flops 1 | bytes 1 | tf_op jit(solution)/shard_map/pallas_call | solution.py:440
  131.1 9.1 %shard_map.376 = (bf16[16,96,768]{2,1,0:T(8,128)(2,1)S(1)}, f32[416,768]{1,0:T(8,128)S(1)}, f32[2,2,192]{2,1,0:T(2,128)S(1)}) custom-call(s32[80]{0:T(128)S(1)} %get-tuple-element.213.tab, bf16[2,768,768]{2,1,0:T(8,128)(2,1)S(1)} %get-tuple-element.152.w1, bf16[416,768]{1,0:T(8,128)(2,1)S(1)} %copy-done.1, bf16[2,416,576]{2,1,0:T(8,128)(2,1)S(1)} %get-tuple-element.153.qkv, ...), custom_call_target="tpu_custom_call" | custom-call | flops 99999997952 | bytes 1 | tf_op jit(solution)/shard_map/pallas_call | solution.py:440
  142.4 2.7 %shard_map.377 = (bf16[394,768]{1,0:T(8,128)(2,1)}, f32[24,768]{1,0:T(8,128)S(1)}) custom-call(s32[80]{0:T(128)S(1)} %copy-done.23, bf16[416,768]{1,0:T(8,128)(2,1)S(1)} %shard_map.366.tok, f32[416,1]{1,0:T(8,128)S(1)} %copy.42.rep, f32[16,768]{1,0:T(8,128)S(1)} %copy-done.13, f32[416,768]{1,0:T(8,128)S(1)} %get-tuple-element.169.grad_one, ...), custom_call_target="tpu_custom_call" | custom-call | flops 1 | bytes 1 | tf_op jit(solution)/shard_map/pallas_call | solution.py:440
  153.1 4.2 %collective-permute-done.32 = bf16[8,96,768]{2,1,0:T(8,128)(2,1)} collective-permute-done((bf16[8,96,768]{2,1,0:T(8,128)(2,1)}, bf16[8,96,768]{2,1,0:T(8,128)(2,1)}, u32[]{:S(2)}, u32[]{:S(2)}) %collective-permute-start.32) | collective-permute-done | bytes 1179680 | tf_op jit(solution)/shard_map/ppermute | solution.py:543
  160.6 6.6 %collective-permute-done.40 = bf16[2,96,768]{2,1,0:T(8,128)(2,1)} collective-permute-done((bf16[2,96,768]{2,1,0:T(8,128)(2,1)}, bf16[2,96,768]{2,1,0:T(8,128)(2,1)}, u32[]{:S(2)}, u32[]{:S(2)}) %collective-permute-start.40) | collective-permute-done | bytes 294944 | tf_op jit(solution)/shard_map/ppermute | solution.py:543
  169.0 2.7 %collective-permute-done.43 = f32[24,768]{1,0:T(8,128)S(1)} collective-permute-done((f32[24,768]{1,0:T(8,128)S(1)}, f32[24,768]{1,0:T(8,128)S(1)}, u32[]{:S(2)}, u32[]{:S(2)}) %collective-permute-start.43) | collective-permute-done | bytes 73760 | tf_op jit(solution)/shard_map/ppermute | solution.py:469
  180.2 4.9 %collective-permute-done.38 = bf16[2,96,768]{2,1,0:T(8,128)(2,1)S(1)} collective-permute-done((bf16[2,96,768]{2,1,0:T(8,128)(2,1)S(1)}, bf16[2,96,768]{2,1,0:T(8,128)(2,1)S(1)}, u32[]{:S(2)}, u32[]{:S(2)}) %collective-permute-start.38) | collective-permute-done | bytes 294944 | tf_op jit(solution)/shard_map/ppermute | solution.py:543
  190.1 6.0 %collective-permute-done.34 = bf16[2,96,768]{2,1,0:T(8,128)(2,1)S(1)} collective-permute-done((bf16[2,96,768]{2,1,0:T(8,128)(2,1)S(1)}, bf16[2,96,768]{2,1,0:T(8,128)(2,1)S(1)}, u32[]{:S(2)}, u32[]{:S(2)}) %collective-permute-start.34) | collective-permute-done | bytes 294944 | tf_op jit(solution)/shard_map/ppermute | solution.py:543
  (211 shorter events, 73.3 us)
Async XLA Ops:
  26.7 26.1 %collective-permute-start.4 = (bf16[4,104,768]{2,1,0:T(8,128)(2,1)S(1)}, bf16[4,104,768]{2,1,0:T(8,128)(2,1)}, u32[]{:S(2)}, u32[]{:S(2)}) collective-permute-start(bf16[4,104,768]{2,1,0:T(8,128)(2,1)S(1)} %pad_maximum_fusion.b0), channel_id=1, source_target_pairs={{0,4},{1,3},{2,6},{3,1},{4,0},{5,7},{6,2},{7,5},{8,12},{9,11},{10,... | collective-permute-start | bytes 1916936 | tf_op jit(solution)/shard_map/ppermute | solution.py:485
  28.0 24.8 %collective-permute-start.5 = (bf16[4,104,768]{2,1,0:T(8,128)(2,1)S(1)}, bf16[4,104,768]{2,1,0:T(8,128)(2,1)}, u32[]{:S(2)}, u32[]{:S(2)}) collective-permute-start(bf16[4,104,768]{2,1,0:T(8,128)(2,1)S(1)} %pad_maximum_fusion.b0), channel_id=1, source_target_pairs={{0,2},{1,5},{2,0},{3,7},{4,6},{5,1},{6,4},{7,3},{8,10},{9,13},{10,... | collective-permute-start | bytes 1916936 | tf_op jit(solution)/shard_map/ppermute | solution.py:485
  28.9 23.5 %collective-permute-start.11 = (bf16[4,96,768]{2,1,0:T(8,128)(2,1)S(1)}, bf16[4,96,768]{2,1,0:T(8,128)(2,1)}, u32[]{:S(2)}, u32[]{:S(2)}) collective-permute-start(bf16[4,96,768]{2,1,0:T(8,128)(2,1)S(1)} %pad_maximum_fusion.1.b0), channel_id=1, source_target_pairs={{0,16},{1,9},{2,18},{3,11},{4,20},{5,13},{6,22},{7,15},{8,24},{9,1... | collective-permute-start | bytes 1769480 | tf_op jit(solution)/shard_map/ppermute | solution.py:485
  29.0 23.8 %collective-permute-start.12 = (bf16[4,96,768]{2,1,0:T(8,128)(2,1)S(1)}, bf16[4,96,768]{2,1,0:T(8,128)(2,1)}, u32[]{:S(2)}, u32[]{:S(2)}) collective-permute-start(bf16[4,96,768]{2,1,0:T(8,128)(2,1)S(1)} %pad_maximum_fusion.1.b0), channel_id=1, source_target_pairs={{0,8},{1,3},{2,10},{3,1},{4,12},{5,7},{6,14},{7,5},{8,0},{9,11},{1... | collective-permute-start | bytes 1769480 | tf_op jit(solution)/shard_map/ppermute | solution.py:485
  29.2 19.1 %collective-permute-start.13 = (bf16[2,96,768]{2,1,0:T(8,128)(2,1)S(1)}, bf16[2,96,768]{2,1,0:T(8,128)(2,1)S(1)}, u32[]{:S(2)}, u32[]{:S(2)}) collective-permute-start(bf16[2,96,768]{2,1,0:T(8,128)(2,1)S(1)} %pad_maximum_fusion.5), channel_id=1, source_target_pairs={{0,2},{1,17},{2,0},{3,19},{4,6},{5,21},{6,4},{7,23},{8,10},{9,25},... | collective-permute-start | bytes 884744 | tf_op jit(solution)/shard_map/ppermute | solution.py:485
  49.3 23.0 %collective-permute-start.8 = (bf16[4,104,768]{2,1,0:T(8,128)(2,1)S(1)}, bf16[4,104,768]{2,1,0:T(8,128)(2,1)}, u32[]{:S(2)}, u32[]{:S(2)}) collective-permute-start(bf16[4,104,768]{2,1,0:T(8,128)(2,1)S(1)} %pad_maximum_fusion.b0), channel_id=1, source_target_pairs={{0,1},{1,0},{2,3},{3,2},{4,5},{5,4},{6,7},{7,6},{8,9},{9,8},{10,11... | collective-permute-start | bytes 1916936 | tf_op jit(solution)/shard_map/ppermute | solution.py:519
  54.5 18.1 %collective-permute-start.10 = (bf16[4,104,768]{2,1,0:T(8,128)(2,1)}, bf16[4,104,768]{2,1,0:T(8,128)(2,1)}, u32[]{:S(2)}, u32[]{:S(2)}) collective-permute-start(bf16[4,104,768]{2,1,0:T(8,128)(2,1)} %collective-permute-done.5.b2), channel_id=1, source_target_pairs={{0,1},{1,0},{2,3},{3,2},{4,5},{5,4},{6,7},{7,6},{8,9},{9,8},{10,11... | collective-permute-start | bytes 1916936 | tf_op jit(solution)/shard_map/ppermute | solution.py:519
  55.6 17.2 %collective-permute-start.9 = (bf16[4,104,768]{2,1,0:T(8,128)(2,1)}, bf16[4,104,768]{2,1,0:T(8,128)(2,1)}, u32[]{:S(2)}, u32[]{:S(2)}) collective-permute-start(bf16[4,104,768]{2,1,0:T(8,128)(2,1)} %collective-permute-done.4.b1), channel_id=1, source_target_pairs={{0,1},{1,0},{2,3},{3,2},{4,5},{5,4},{6,7},{7,6},{8,9},{9,8},{10,11... | collective-permute-start | bytes 1916936 | tf_op jit(solution)/shard_map/ppermute | solution.py:519
  65.1 16.4 %collective-permute-start.15 = (bf16[4,96,768]{2,1,0:T(8,128)(2,1)}, bf16[4,96,768]{2,1,0:T(8,128)(2,1)}, u32[]{:S(2)}, u32[]{:S(2)}) collective-permute-start(bf16[4,96,768]{2,1,0:T(8,128)(2,1)} %collective-permute-done.11.b1), channel_id=1, source_target_pairs={{0,8},{1,3},{2,10},{3,1},{4,12},{5,7},{6,14},{7,5},{8,0},{9,11},{1... | collective-permute-start | bytes 1769480 | tf_op jit(solution)/shard_map/ppermute | solution.py:485
  72.2 18.5 %collective-permute-start.16 = (bf16[4,96,768]{2,1,0:T(8,128)(2,1)}, bf16[4,96,768]{2,1,0:T(8,128)(2,1)S(1)}, u32[]{:S(2)}, u32[]{:S(2)}) collective-permute-start(bf16[4,96,768]{2,1,0:T(8,128)(2,1)} %copy-done.10), channel_id=1, source_target_pairs={{0,1},{1,0},{2,3},{3,2},{4,5},{5,4},{6,7},{7,6},{8,9},{9,8},{10,11... | collective-permute-start | bytes 1769480 | tf_op jit(solution)/shard_map/ppermute | solution.py:519
  72.6 19.4 %collective-permute-start.17 = (bf16[4,96,768]{2,1,0:T(8,128)(2,1)}, bf16[4,96,768]{2,1,0:T(8,128)(2,1)S(1)}, u32[]{:S(2)}, u32[]{:S(2)}) collective-permute-start(bf16[4,96,768]{2,1,0:T(8,128)(2,1)} %collective-permute-done.11.b1), channel_id=1, source_target_pairs={{0,1},{1,0},{2,3},{3,2},{4,5},{5,4},{6,7},{7,6},{8,9},{9,8},{10,11... | collective-permute-start | bytes 1769480 | tf_op jit(solution)/shard_map/ppermute | solution.py:519
  72.8 19.6 %collective-permute-start.18 = (bf16[4,96,768]{2,1,0:T(8,128)(2,1)}, bf16[4,96,768]{2,1,0:T(8,128)(2,1)S(1)}, u32[]{:S(2)}, u32[]{:S(2)}) collective-permute-start(bf16[4,96,768]{2,1,0:T(8,128)(2,1)} %collective-permute-done.12.b2), channel_id=1, source_target_pairs={{0,1},{1,0},{2,3},{3,2},{4,5},{5,4},{6,7},{7,6},{8,9},{9,8},{10,11... | collective-permute-start | bytes 1769480 | tf_op jit(solution)/shard_map/ppermute | solution.py:519
  73.1 14.9 %collective-permute-start.21 = (bf16[4,96,768]{2,1,0:T(8,128)(2,1)}, bf16[4,96,768]{2,1,0:T(8,128)(2,1)S(1)}, u32[]{:S(2)}, u32[]{:S(2)}) collective-permute-start(bf16[4,96,768]{2,1,0:T(8,128)(2,1)} %pad_maximum_fusion.2.b0), channel_id=1, source_target_pairs={{0,16},{1,9},{2,18},{3,11},{4,20},{5,13},{6,22},{7,15},{8,24},{9,1... | collective-permute-start | bytes 1769480 | tf_op jit(solution)/shard_map/ppermute | solution.py:485
  107.9 21.1 %collective-permute-start.29 = (bf16[8,96,768]{2,1,0:T(8,128)(2,1)}, bf16[8,96,768]{2,1,0:T(8,128)(2,1)}, u32[]{:S(2)}, u32[]{:S(2)}) collective-permute-start(bf16[8,96,768]{2,1,0:T(8,128)(2,1)} %add_convert_fusion.2), channel_id=1, source_target_pairs={{0,8},{1,3},{2,10},{3,1},{4,12},{5,7},{6,14},{7,5},{8,0},{9,11},{1... | collective-permute-start | bytes 3538952 | tf_op jit(solution)/shard_map/ppermute | solution.py:543
  113.2 33.0 %collective-permute-start.36 = (bf16[8,96,768]{2,1,0:T(8,128)(2,1)S(1)}, bf16[8,96,768]{2,1,0:T(8,128)(2,1)S(1)}, u32[]{:S(2)}, u32[]{:S(2)}) collective-permute-start(bf16[8,96,768]{2,1,0:T(8,128)(2,1)S(1)} %add_convert_fusion.1), channel_id=1, source_target_pairs={{0,4},{1,5},{2,6},{3,7},{4,0},{5,1},{6,2},{7,3},{8,12},{9,13},{10,... | collective-permute-start | bytes 3538952 | tf_op jit(solution)/shard_map/ppermute | solution.py:543
  141.6 15.7 %collective-permute-start.32 = (bf16[8,96,768]{2,1,0:T(8,128)(2,1)}, bf16[8,96,768]{2,1,0:T(8,128)(2,1)}, u32[]{:S(2)}, u32[]{:S(2)}) collective-permute-start(bf16[8,96,768]{2,1,0:T(8,128)(2,1)} %add_convert_fusion), channel_id=1, source_target_pairs={{0,2},{1,5},{2,0},{3,7},{4,6},{5,1},{6,4},{7,3},{8,10},{9,13},{10,... | collective-permute-start | bytes 3538952 | tf_op jit(solution)/shard_map/ppermute | solution.py:543
  147.3 27.0 %collective-permute-start.37 = (bf16[4,96,768]{2,1,0:T(8,128)(2,1)S(1)}, bf16[4,96,768]{2,1,0:T(8,128)(2,1)}, u32[]{:S(2)}, u32[]{:S(2)}) collective-permute-start(bf16[4,96,768]{2,1,0:T(8,128)(2,1)S(1)} %add_convert_fusion.3), channel_id=1, source_target_pairs={{0,8},{1,9},{2,10},{3,11},{4,12},{5,13},{6,14},{7,15},{8,0},{9,1},... | collective-permute-start | bytes 1769480 | tf_op jit(solution)/shard_map/ppermute | solution.py:543
  149.9 17.2 %collective-permute-start.40 = (bf16[2,96,768]{2,1,0:T(8,128)(2,1)}, bf16[2,96,768]{2,1,0:T(8,128)(2,1)}, u32[]{:S(2)}, u32[]{:S(2)}) collective-permute-start(bf16[2,96,768]{2,1,0:T(8,128)(2,1)} %add_convert_fusion.6), channel_id=1, source_target_pairs={{0,16},{1,17},{2,18},{3,19},{4,20},{5,21},{6,22},{7,23},{8,24},{9,... | collective-permute-start | bytes 884744 | tf_op jit(solution)/shard_map/ppermute | solution.py:543
  150.7 21.0 %collective-permute-start.43 = (f32[24,768]{1,0:T(8,128)S(1)}, f32[24,768]{1,0:T(8,128)S(1)}, u32[]{:S(2)}, u32[]{:S(2)}) collective-permute-start(f32[24,768]{1,0:T(8,128)S(1)} %add.290), channel_id=1, source_target_pairs={{0,8},{1,9},{2,10},{3,11},{4,12},{5,13},{6,14},{7,15},{8,0},{9,1},... | collective-permute-start | bytes 221192 | tf_op jit(solution)/shard_map/ppermute | solution.py:469
  151.3 20.4 %collective-permute-start.44 = (f32[24,768]{1,0:T(8,128)S(1)}, f32[24,768]{1,0:T(8,128)S(1)}, u32[]{:S(2)}, u32[]{:S(2)}) collective-permute-start(f32[24,768]{1,0:T(8,128)S(1)} %add.290), channel_id=1, source_target_pairs={{0,16},{1,17},{2,18},{3,19},{4,20},{5,21},{6,22},{7,23},{8,24},{9,... | collective-permute-start | bytes 221192 | tf_op jit(solution)/shard_map/ppermute | solution.py:469
  157.3 16.3 %collective-permute-start.45 = (f32[24,768]{1,0:T(8,128)S(1)}, f32[24,768]{1,0:T(8,128)S(1)}, u32[]{:S(2)}, u32[]{:S(2)}) collective-permute-start(f32[24,768]{1,0:T(8,128)S(1)} %add.290), channel_id=1, source_target_pairs={{0,24},{1,25},{2,26},{3,27},{4,28},{5,29},{6,30},{7,31},{8,16},{9,... | collective-permute-start | bytes 221192 | tf_op jit(solution)/shard_map/ppermute | solution.py:469
  177.5 20.0 %collective-permute-start.46 = (f32[24,768]{1,0:T(8,128)S(1)}, f32[24,768]{1,0:T(8,128)S(1)}, u32[]{:S(2)}, u32[]{:S(2)}) collective-permute-start(f32[24,768]{1,0:T(8,128)S(1)} %add_add_fusion.1), channel_id=1, source_target_pairs={{0,2},{1,3},{2,0},{3,1},{4,6},{5,7},{6,4},{7,5},{8,10},{9,11},{10,... | collective-permute-start | bytes 221192 | tf_op jit(solution)/shard_map/ppermute | solution.py:469
  178.2 19.3 %collective-permute-start.47 = (f32[24,768]{1,0:T(8,128)S(1)}, f32[24,768]{1,0:T(8,128)S(1)}, u32[]{:S(2)}, u32[]{:S(2)}) collective-permute-start(f32[24,768]{1,0:T(8,128)S(1)} %add_add_fusion.1), channel_id=1, source_target_pairs={{0,4},{1,5},{2,6},{3,7},{4,0},{5,1},{6,2},{7,3},{8,12},{9,13},{10,... | collective-permute-start | bytes 221192 | tf_op jit(solution)/shard_map/ppermute | solution.py:469
  178.9 18.7 %collective-permute-start.48 = (f32[24,768]{1,0:T(8,128)S(1)}, f32[24,768]{1,0:T(8,128)S(1)}, u32[]{:S(2)}, u32[]{:S(2)}) collective-permute-start(f32[24,768]{1,0:T(8,128)S(1)} %add_add_fusion.1), channel_id=1, source_target_pairs={{0,6},{1,7},{2,4},{3,5},{4,2},{5,3},{6,0},{7,1},{8,14},{9,15},{10,... | collective-permute-start | bytes 221192 | tf_op jit(solution)/shard_map/ppermute | solution.py:469
  (68 other events, 811.3 us)

commit v4 on v3

--- a/solution.py
+++ b/solution.py
@@ -36,9 +36,9 @@
 BF16 = jnp.bfloat16
 
 BIT = {"c": 1, "x": 2, "y": 4, "1": 8, "2": 16}
-GATHER = (("12yx", "21xy"), ("xy21", "2y1x"), ("1x2y", "y21x"))
+GATHER = (("21xy", "12yx"), ("2y1x", "yx21"), ("y21x", "1x2y"))
 SCATTER = (("21yx", "12xy"), ("2x1y", "x21y"), ("y2x1", "y21x"))
-STEPS = "S0S1S2D0S0D1S1D2S2D0S0F0D1S1D0S0D2S2D1S1F1D0"
+STEPS = "S0S1S2D0S0D1S1D0S0D2S2F0D1S1D0S0D2S2D1S1F1D0"
 
 
 def offset_of(order, place):
@@ -457,22 +457,12 @@
     return call(fence_kernel, (mark,), (shape((8, 128), F32),), flops=LONG, table=False)[0]
 
 
-def add_across(values, *masks):
-    for mask in masks:
-        pairs = [(dev, dev ^ mask) for dev in range(32)]
-        values = values + lax.ppermute(values, AXES, pairs)
-    return values
-
-
-def send_all(values, one, two):
-    return [
-        lax.ppermute(values, AXES, [(dev, dev ^ mask) for dev in range(32)])
-        for mask in (one, two, one ^ two)
-    ]
-
-
-def take_all(values, parts):
-    return (values + parts[0]) + (parts[1] + parts[2])
+def send_across(values, mask):
+    return lax.ppermute(values, AXES, [(dev, dev ^ mask) for dev in range(32)])
+
+
+def add_across(values, mask):
+    return values + send_across(values, mask)
 
 
 class Gather:
@@ -633,10 +623,10 @@
                 seen["mark"] = fence(*held, *seen.values())
             elif kind == "F":
                 if index == "0":
-                    tok = pad_rows(after(tokens, *held))
+                    tok = pad_rows(after(tokens, *held[:2]))
                     seen["tok"] = (tok, rep, *tables)
                 else:
-                    cot = pad_rows(after(cotangent, *held))
+                    cot = pad_rows(after(cotangent, held[1]))
                     seen["cot"] = cot
             elif kind == "S":
                 stream.start(*seen.values())
@@ -786,19 +776,18 @@
     if direct:
         sums = add_across(sums, 1)
         one.hold(fence(sums, sent_three, sent_two))
-        parts = send_all(sums, 8, 16)
+        part = send_across(sums, 2)
         sent = one.step()
-        mark = sent
-        sums = take_all(sums, after(parts, mark))
-        three.step(mark)
-        two.step(mark)
+        sums = sums + after(part, sent)
+        part = send_across(sums, 16)
+        three.step(sent)
+        two.step(sent)
         sent = one.step()
-        mark = sent
-        parts = send_all(after(sums, mark), 2, 4)
-        three.hold(mark)
-        two.step(mark)
+        sums = sums + after(part, sent)
+        part = send_across(sums, 8)
+        two.step(sent)
         sent = one.step()
-        sums = take_all(sums, after(parts, sent))
+        sums = add_across(sums + after(part, sent), 4)
         grad_three = three.result()
         states_three = adam_update(
             reduce_weight, grad_three.T, first_reduce, second_reduce, RATE_MATRIX, DECAY

time: 206 us -> 201 us (0.976)
  waiting for transfers between devices: 73.5 us -> 52.3 us
  starting transfers between devices: 39.1 us -> 55.3 us
    ppermute x15, waiting for transfers between devices: 44 us -> 26.8 us  [send(): return lax.ppermute(values, AXES, pairs_of(self.orders, level))]
    ppermute x12, starting transfers between devices: 11 us -> 20.2 us  [sib(): return tuple((lax.ppermute(values, AXES, CORE_PAIRS) for values in own))]
    ppermute x12, waiting for transfers between devices: 23.3 us -> 14.3 us  [step(): lax.ppermute(sent, AXES, pairs_of(self.orders, self.level))]
    ppermute x15, starting transfers between devices: 12.5 us -> 18.3 us  [send(): return lax.ppermute(values, AXES, pairs_of(self.orders, level))]
    ppermute x7 -> x5, waiting for transfers between devices: 4.63 us -> 9.36 us  [send_across(): return lax.ppermute(values, AXES, [(dev, dev ^ mask) for dev in range(32)])]
    ppermute x12, starting transfers between devices: 7.21 us -> 11 us  [step(): lax.ppermute(sent, AXES, pairs_of(self.orders, self.level))]
    ppermute x7 -> x5, starting transfers between devices: 7.83 us -> 4.78 us  [send_across(): return lax.ppermute(values, AXES, [(dev, dev ^ mask) for dev in range(32)])]
    unnamed x86 -> x94, local copies, waits for them, and re-layouts: 4.83 us -> 4.84 us
  transfers between devices with their start and end apart: 49 -> 47, of which waited for: 18 -> 14; matrix products, arithmetic and copies ran while one was open for 14% -> 15% of each run, Pallas kernels for 27% -> 28%
where the time goes in v4:
time: 201 us
  Pallas kernels  56.6 us (28%)
  starting transfers between devices  55.3 us (28%)
  waiting for transfers between devices  52.3 us (26%)
  other arithmetic  27.8 us (14%)
  local copies, waits for them, and re-layouts  7.19 us (4%)
    pallas_call x14, Pallas kernels, call(): pl.pallas_call(kernel, out_shape=outs, in_specs=[SMEM] * table + [VMEM] *...  56.6 us
    ppermute x15, waiting for transfers between devices, send(): return lax.ppermute(values, AXES, pairs_of(self.orders, level))  26.8 us
    ppermute x12, starting transfers between devices, sib(): return tuple((lax.ppermute(values, AXES, CORE_PAIRS) for values in own))  20.2 us
    ppermute x15, starting transfers between devices, send(): return lax.ppermute(values, AXES, pairs_of(self.orders, level))  18.3 us
    convert_element_type x12, other arithmetic, step(): sent = self.total(size, 2 * size).astype(BF16)  16.7 us
    ppermute x12, waiting for transfers between devices, step(): lax.ppermute(sent, AXES, pairs_of(self.orders, self.level))  14.3 us
    ppermute x12, starting transfers between devices, step(): lax.ppermute(sent, AXES, pairs_of(self.orders, self.level))  11 us
    ppermute x5, waiting for transfers between devices, send_across(): return lax.ppermute(values, AXES, [(dev, dev ^ mask) for dev in range(32)])  9.36 us
  transfers between devices with their start and end apart: 47, of which 14 were waited for; matrix products, arithmetic and copies ran while one was open for 15% of the time, Pallas kernels for 28%

profile of v4, /device:TPU:1, one launch (start us, length us, event | category | flops | bytes accessed | tf_op | source)
XLA Modules:
  0.0 200.7 jit_solution(16903541100062156334)
XLA Ops:
  16.8 2.8 %collective-permute-done.5 = bf16[2,96,768]{2,1,0:T(8,128)(2,1)S(1)} collective-permute-done((bf16[2,96,768]{2,1,0:T(8,128)(2,1)S(1)}, bf16[2,96,768]{2,1,0:T(8,128)(2,1)S(1)}, u32[]{:S(2)}, u32[]{:S(2)}) %collective-permute-start.5) | collective-permute-done | bytes 294944 | tf_op jit(solution)/shard_map/ppermute | solution.py:475
  19.7 3.4 %collective-permute-done.1 = bf16[2,104,768]{2,1,0:T(8,128)(2,1)S(1)} collective-permute-done((bf16[2,104,768]{2,1,0:T(8,128)(2,1)S(1)}, bf16[2,104,768]{2,1,0:T(8,128)(2,1)S(1)}, u32[]{:S(2)}, u32[]{:S(2)}) %collective-permute-start.1) | collective-permute-done | bytes 319520 | tf_op jit(solution)/shard_map/ppermute | solution.py:475
  26.5 3.3 %collective-permute-start.12 = (bf16[4,96,768]{2,1,0:T(8,128)(2,1)S(1)}, bf16[4,96,768]{2,1,0:T(8,128)(2,1)S(1)}, u32[]{:S(2)}, u32[]{:S(2)}) collective-permute-start(bf16[4,96,768]{2,1,0:T(8,128)(2,1)S(1)} %pad_maximum_fusion.1.b0), channel_id=1, source_target_pairs={{0,2},{1,9},{2,0},{3,11},{4,6},{5,13},{6,4},{7,15},{8,10},{9,1},{1... | collective-permute-start | bytes 1769480 | tf_op jit(solution)/shard_map/ppermute | solution.py:475
  31.7 7.8 %collective-permute-done.13 = bf16[2,96,768]{2,1,0:T(8,128)(2,1)} collective-permute-done((bf16[2,96,768]{2,1,0:T(8,128)(2,1)}, bf16[2,96,768]{2,1,0:T(8,128)(2,1)}, u32[]{:S(2)}, u32[]{:S(2)}) %collective-permute-start.13) | collective-permute-done | bytes 294944 | tf_op jit(solution)/shard_map/ppermute | solution.py:475
  39.5 10.2 %collective-permute-start.8 = (bf16[4,104,768]{2,1,0:T(8,128)(2,1)S(1)}, bf16[4,104,768]{2,1,0:T(8,128)(2,1)S(1)}, u32[]{:S(2)}, u32[]{:S(2)}) collective-permute-start(bf16[4,104,768]{2,1,0:T(8,128)(2,1)S(1)} %pad_maximum_fusion.b0), channel_id=1, source_target_pairs={{0,1},{1,0},{2,3},{3,2},{4,5},{5,4},{6,7},{7,6},{8,9},{9,8},{10,11... | collective-permute-start | bytes 1916936 | tf_op jit(solution)/shard_map/ppermute | solution.py:509
  51.7 3.0 %collective-permute-start.10 = (bf16[4,104,768]{2,1,0:T(8,128)(2,1)}, bf16[4,104,768]{2,1,0:T(8,128)(2,1)S(1)}, u32[]{:S(2)}, u32[]{:S(2)}) collective-permute-start(bf16[4,104,768]{2,1,0:T(8,128)(2,1)} %collective-permute-done.4.b2), channel_id=1, source_target_pairs={{0,1},{1,0},{2,3},{3,2},{4,5},{5,4},{6,7},{7,6},{8,9},{9,8},{10,11... | collective-permute-start | bytes 1916936 | tf_op jit(solution)/shard_map/ppermute | solution.py:509
  54.7 5.0 %collective-permute-done.7.b3 = bf16[4,104,768]{2,1,0:T(8,128)(2,1)} collective-permute-done((bf16[4,104,768]{2,1,0:T(8,128)(2,1)}, bf16[4,104,768]{2,1,0:T(8,128)(2,1)}, u32[]{:S(2)}, u32[]{:S(2)}) %collective-permute-start.7) | collective-permute-done | bytes 639008 | tf_op jit(solution)/shard_map/ppermute | solution.py:475
  59.6 4.0 %collective-permute-start.14 = (bf16[4,104,768]{2,1,0:T(8,128)(2,1)}, bf16[4,104,768]{2,1,0:T(8,128)(2,1)}, u32[]{:S(2)}, u32[]{:S(2)}) collective-permute-start(bf16[4,104,768]{2,1,0:T(8,128)(2,1)} %collective-permute-done.7.b3), channel_id=1, source_target_pairs={{0,1},{1,0},{2,3},{3,2},{4,5},{5,4},{6,7},{7,6},{8,9},{9,8},{10,11... | collective-permute-start | bytes 1916936 | tf_op jit(solution)/shard_map/ppermute | solution.py:509
  65.9 6.9 %shard_map.367 = (f32[16,768]{1,0:T(8,128)S(1)}, f32[4,1,768]{2,1,0:T(1,128)S(1)}, f32[416,768]{1,0:T(8,128)S(1)}, bf16[416,768]{1,0:T(8,128)(2,1)S(1)}, f32[4,1...) custom-call(s32[80]{0:T(128)S(1)} %get-tuple-element.203.tab, ...), custom_call_target="tpu_custom_call" | custom-call | flops 1 | bytes 1 | tf_op jit(solution)/shard_map/pallas_call | solution.py:440
  74.9 6.3 %shard_map.369 = (bf16[2,768,768]{2,1,0:T(8,128)(2,1)S(1)}, bf16[2,416,576]{2,1,0:T(8,128)(2,1)S(1)}, f32[12,208,208]{2,1,0:T(8,128)S(1)}, bf16[2,416,192]{2,1,0...) custom-call(s32[80]{0:T(128)S(1)} %get-tuple-element.203.tab, ...), custom_call_target="tpu_custom_call" | custom-call | flops 1 | bytes 1 | tf_op jit(solution)/shard_map/pallas_call | solution.py:440
  82.1 4.6 %shard_map.370 = (bf16[2,768,768]{2,1,0:T(8,128)(2,1)S(1)}, bf16[2,416,768]{2,1,0:T(8,128)(2,1)S(1)}, f32[2,416,768]{2,1,0:T(8,128)S(1)}, bf16[416,768]{1,0:T(8,128)(2,1)S(1)}, bf16[16,96,768]{2,1,0:T(8,128)(2,1)S(1)}) custom-call(s32[80]{0:T(128)S(1)} %get-tuple-element.204.tab, bf16[416,768]{1,0:T(8,128)(2,1)S(1)} %get-tuple-element.120.normed_two, ...), custom_call_target="tpu_custom_call" | custom-call | flops 99999997952 | bytes 1 | tf_op jit(solution)/shard_map/pallas_call | solution.py:440
  86.7 2.8 %collective-permute-done.21.b1 = bf16[4,96,768]{2,1,0:T(8,128)(2,1)S(1)} collective-permute-done((bf16[4,96,768]{2,1,0:T(8,128)(2,1)S(1)}, bf16[4,96,768]{2,1,0:T(8,128)(2,1)S(1)}, u32[]{:S(2)}, u32[]{:S(2)}) %collective-permute-start.21) | collective-permute-done | bytes 589856 | tf_op jit(solution)/shard_map/ppermute | solution.py:475
  91.8 3.8 %shard_map.371 = (bf16[2,768,768]{2,1,0:T(8,128)(2,1)S(1)}, bf16[2,416,768]{2,1,0:T(8,128)(2,1)S(1)}, f32[2,416,768]{2,1,0:T(8,128)S(1)}, bf16[16,96,768]{2,1,0:T(8,128)(2,1)S(1)}) custom-call(s32[80]{0:T(128)S(1)} %get-tuple-element.204.tab, bf16[416,768]{1,0:T(8,128)(2,1)S(1)} %get-tuple-element.120.normed_two, ...), custom_call_target="tpu_custom_call" | custom-call | flops 1 | bytes 1 | tf_op jit(solution)/shard_map/pallas_call | solution.py:440
  95.5 3.4 %collective-permute-done.25.b3 = bf16[4,96,768]{2,1,0:T(8,128)(2,1)S(1)} collective-permute-done((bf16[4,96,768]{2,1,0:T(8,128)(2,1)S(1)}, bf16[4,96,768]{2,1,0:T(8,128)(2,1)S(1)}, u32[]{:S(2)}, u32[]{:S(2)}) %collective-permute-start.25) | collective-permute-done | bytes 589856 | tf_op jit(solution)/shard_map/ppermute | solution.py:475
  101.5 3.6 %shard_map.372 = (bf16[2,768,768]{2,1,0:T(8,128)(2,1)S(1)}, bf16[2,416,768]{2,1,0:T(8,128)(2,1)S(1)}, f32[2,1,768]{2,1,0:T(1,128)S(1)}, bf16[16,96,768]{2,1,0:T(8,128)(2,1)S(1)}) custom-call(s32[80]{0:T(128)S(1)} %get-tuple-element.202.tab, bf16[416,768]{1,0:T(8,128)(2,1)S(1)} %get-tuple-element.120.normed_two, ...), custom_call_target="tpu_custom_call" | custom-call | flops 99999997952 | bytes 1 | tf_op jit(solution)/shard_map/pallas_call | solution.py:440
  107.0 3.7 %shard_map.373 = (bf16[2,768,768]{2,1,0:T(8,128)(2,1)S(1)}, bf16[2,416,768]{2,1,0:T(8,128)(2,1)S(1)}, f32[2,1,768]{2,1,0:T(1,128)S(1)}, bf16[16,96,768]{2,1,0:T(8,128)(2,1)S(1)}) custom-call(s32[80]{0:T(128)S(1)} %get-tuple-element.202.tab, bf16[416,768]{1,0:T(8,128)(2,1)S(1)} %get-tuple-element.120.normed_two, ...), custom_call_target="tpu_custom_call" | custom-call | flops 99999997952 | bytes 1 | tf_op jit(solution)/shard_map/pallas_call | solution.py:440
  114.0 5.6 %shard_map.374 = (bf16[394,768]{1,0:T(8,128)(2,1)}, f32[416,768]{1,0:T(8,128)S(1)}, bf16[416,768]{1,0:T(8,128)(2,1)S(1)}, f32[16,768]{1,0:T(8,128)S(1)}) custom-call(bf16[2,416,768]{2,1,0:T(8,128)(2,1)S(1)} %get-tuple-element.124.act_sib, bf16[2,416,768]{2,1,0:T(8,128)(2,1)S(1)} %get-tuple-element.125.act_own, ...), custom_call_target="tpu_custom_call" | custom-call | flops 1 | bytes 1 | tf_op jit(solution)/shard_map/pallas_call | solution.py:440
  119.6 8.8 %shard_map.375 = (bf16[16,96,768]{2,1,0:T(8,128)(2,1)S(1)}, f32[416,768]{1,0:T(8,128)S(1)}, f32[2,2,192]{2,1,0:T(2,128)S(1)}) custom-call(s32[80]{0:T(128)S(1)} %get-tuple-element.203.tab, bf16[2,768,768]{2,1,0:T(8,128)(2,1)S(1)} %get-tuple-element.152.w1, bf16[416,768]{1,0:T(8,128)(2,1)S(1)} %copy-done.1, bf16[2,416,576]{2,1,0:T(8,128)(2,1)S(1)} %get-tuple-element.153.qkv, ...), custom_call_target="tpu_custom_call" | custom-call | flops 1 | bytes 1 | tf_op jit(solution)/shard_map/pallas_call | solution.py:440
  131.5 9.1 %shard_map.376 = (bf16[16,96,768]{2,1,0:T(8,128)(2,1)S(1)}, f32[416,768]{1,0:T(8,128)S(1)}, f32[2,2,192]{2,1,0:T(2,128)S(1)}) custom-call(s32[80]{0:T(128)S(1)} %get-tuple-element.203.tab, bf16[2,768,768]{2,1,0:T(8,128)(2,1)S(1)} %get-tuple-element.147.w1, bf16[416,768]{1,0:T(8,128)(2,1)S(1)} %copy-done.1, bf16[2,416,576]{2,1,0:T(8,128)(2,1)S(1)} %get-tuple-element.148.qkv, ...), custom_call_target="tpu_custom_call" | custom-call | flops 99999997952 | bytes 1 | tf_op jit(solution)/shard_map/pallas_call | solution.py:440
  141.7 2.7 %shard_map.377 = (bf16[394,768]{1,0:T(8,128)(2,1)}, f32[24,768]{1,0:T(8,128)S(1)}) custom-call(s32[80]{0:T(128)S(1)} %get-tuple-element.203.tab, bf16[416,768]{1,0:T(8,128)(2,1)S(1)} %shard_map.366.tok, f32[416,1]{1,0:T(8,128)S(1)} %copy-done.5, f32[16,768]{1,0:T(8,128)S(1)} %copy-done.14, f32[416,768]{1,0:T(8,128)S(1)} %get-tuple-element.164.grad_one, ...), custom_call_target="tpu_custom_call" | custom-call | flops 1 | bytes 1 | tf_op jit(solution)/shard_map/pallas_call | solution.py:440
  151.9 4.5 %collective-permute-done.32 = bf16[8,96,768]{2,1,0:T(8,128)(2,1)S(1)} collective-permute-done((bf16[8,96,768]{2,1,0:T(8,128)(2,1)S(1)}, bf16[8,96,768]{2,1,0:T(8,128)(2,1)S(1)}, u32[]{:S(2)}, u32[]{:S(2)}) %collective-permute-start.32) | collective-permute-done | bytes 1179680 | tf_op jit(solution)/shard_map/ppermute | solution.py:533
  159.2 9.4 %collective-permute-done.43 = f32[24,768]{1,0:T(8,128)S(1)} collective-permute-done((f32[24,768]{1,0:T(8,128)S(1)}, f32[24,768]{1,0:T(8,128)S(1)}, u32[]{:S(2)}, u32[]{:S(2)}) %collective-permute-start.43) | collective-permute-done | bytes 73760 | tf_op jit(solution)/shard_map/ppermute | solution.py:461
  180.7 5.6 %collective-permute-done.38 = bf16[2,96,768]{2,1,0:T(8,128)(2,1)S(1)} collective-permute-done((bf16[2,96,768]{2,1,0:T(8,128)(2,1)S(1)}, bf16[2,96,768]{2,1,0:T(8,128)(2,1)S(1)}, u32[]{:S(2)}, u32[]{:S(2)}) %collective-permute-start.38) | collective-permute-done | bytes 294944 | tf_op jit(solution)/shard_map/ppermute | solution.py:533
  188.9 4.1 %collective-permute-done.34 = bf16[2,96,768]{2,1,0:T(8,128)(2,1)S(1)} collective-permute-done((bf16[2,96,768]{2,1,0:T(8,128)(2,1)S(1)}, bf16[2,96,768]{2,1,0:T(8,128)(2,1)S(1)}, u32[]{:S(2)}, u32[]{:S(2)}) %collective-permute-start.34) | collective-permute-done | bytes 294944 | tf_op jit(solution)/shard_map/ppermute | solution.py:533
  (217 shorter events, 75.0 us)
Async XLA Ops:
  9.6 16.2 %collective-permute-start.6 = (bf16[1,96,768]{2,1,0:T(8,128)(2,1)S(1)}, bf16[1,96,768]{2,1,0:T(8,128)(2,1)S(1)}, u32[]{:S(2)}, u32[]{:S(2)}) collective-permute-start(bf16[1,96,768]{2,1,0:T(8,128)(2,1)S(1)} %convert_bitcast_fusion), channel_id=1, source_target_pairs={{0,4},{1,9},{2,6},{3,11},{4,0},{5,13},{6,2},{7,15},{8,12},{9,1},{1... | collective-permute-start | bytes 442376 | tf_op jit(solution)/shard_map/ppermute | solution.py:475
  23.2 26.5 %collective-permute-start.3 = (bf16[4,104,768]{2,1,0:T(8,128)(2,1)S(1)}, bf16[4,104,768]{2,1,0:T(8,128)(2,1)}, u32[]{:S(2)}, u32[]{:S(2)}) collective-permute-start(bf16[4,104,768]{2,1,0:T(8,128)(2,1)S(1)} %pad_maximum_fusion.b0), channel_id=1, source_target_pairs={{0,2},{1,5},{2,0},{3,7},{4,6},{5,1},{6,4},{7,3},{8,10},{9,13},{10,... | collective-permute-start | bytes 1916936 | tf_op jit(solution)/shard_map/ppermute | solution.py:475
  24.5 25.2 %collective-permute-start.4 = (bf16[4,104,768]{2,1,0:T(8,128)(2,1)S(1)}, bf16[4,104,768]{2,1,0:T(8,128)(2,1)}, u32[]{:S(2)}, u32[]{:S(2)}) collective-permute-start(bf16[4,104,768]{2,1,0:T(8,128)(2,1)S(1)} %pad_maximum_fusion.b0), channel_id=1, source_target_pairs={{0,4},{1,3},{2,6},{3,1},{4,0},{5,7},{6,2},{7,5},{8,12},{9,11},{10,... | collective-permute-start | bytes 1916936 | tf_op jit(solution)/shard_map/ppermute | solution.py:475
  26.4 23.2 %collective-permute-start.11 = (bf16[4,96,768]{2,1,0:T(8,128)(2,1)S(1)}, bf16[4,96,768]{2,1,0:T(8,128)(2,1)}, u32[]{:S(2)}, u32[]{:S(2)}) collective-permute-start(bf16[4,96,768]{2,1,0:T(8,128)(2,1)S(1)} %pad_maximum_fusion.1.b0), channel_id=1, source_target_pairs={{0,8},{1,17},{2,10},{3,19},{4,12},{5,21},{6,14},{7,23},{8,0},{9,25... | collective-permute-start | bytes 1769480 | tf_op jit(solution)/shard_map/ppermute | solution.py:475
  26.5 23.2 %collective-permute-start.12 = (bf16[4,96,768]{2,1,0:T(8,128)(2,1)S(1)}, bf16[4,96,768]{2,1,0:T(8,128)(2,1)S(1)}, u32[]{:S(2)}, u32[]{:S(2)}) collective-permute-start(bf16[4,96,768]{2,1,0:T(8,128)(2,1)S(1)} %pad_maximum_fusion.1.b0), channel_id=1, source_target_pairs={{0,2},{1,9},{2,0},{3,11},{4,6},{5,13},{6,4},{7,15},{8,10},{9,1},{1... | collective-permute-start | bytes 1769480 | tf_op jit(solution)/shard_map/ppermute | solution.py:475
  39.5 33.3 %collective-permute-start.8 = (bf16[4,104,768]{2,1,0:T(8,128)(2,1)S(1)}, bf16[4,104,768]{2,1,0:T(8,128)(2,1)S(1)}, u32[]{:S(2)}, u32[]{:S(2)}) collective-permute-start(bf16[4,104,768]{2,1,0:T(8,128)(2,1)S(1)} %pad_maximum_fusion.b0), channel_id=1, source_target_pairs={{0,1},{1,0},{2,3},{3,2},{4,5},{5,4},{6,7},{7,6},{8,9},{9,8},{10,11... | collective-permute-start | bytes 1916936 | tf_op jit(solution)/shard_map/ppermute | solution.py:509
  51.7 21.2 %collective-permute-start.10 = (bf16[4,104,768]{2,1,0:T(8,128)(2,1)}, bf16[4,104,768]{2,1,0:T(8,128)(2,1)S(1)}, u32[]{:S(2)}, u32[]{:S(2)}) collective-permute-start(bf16[4,104,768]{2,1,0:T(8,128)(2,1)} %collective-permute-done.4.b2), channel_id=1, source_target_pairs={{0,1},{1,0},{2,3},{3,2},{4,5},{5,4},{6,7},{7,6},{8,9},{9,8},{10,11... | collective-permute-start | bytes 1916936 | tf_op jit(solution)/shard_map/ppermute | solution.py:509
  54.7 18.7 %collective-permute-start.9 = (bf16[4,104,768]{2,1,0:T(8,128)(2,1)}, bf16[4,104,768]{2,1,0:T(8,128)(2,1)S(1)}, u32[]{:S(2)}, u32[]{:S(2)}) collective-permute-start(bf16[4,104,768]{2,1,0:T(8,128)(2,1)} %collective-permute-done.3.b1), channel_id=1, source_target_pairs={{0,1},{1,0},{2,3},{3,2},{4,5},{5,4},{6,7},{7,6},{8,9},{9,8},{10,11... | collective-permute-start | bytes 1916936 | tf_op jit(solution)/shard_map/ppermute | solution.py:509
  59.6 13.9 %collective-permute-start.14 = (bf16[4,104,768]{2,1,0:T(8,128)(2,1)}, bf16[4,104,768]{2,1,0:T(8,128)(2,1)}, u32[]{:S(2)}, u32[]{:S(2)}) collective-permute-start(bf16[4,104,768]{2,1,0:T(8,128)(2,1)} %collective-permute-done.7.b3), channel_id=1, source_target_pairs={{0,1},{1,0},{2,3},{3,2},{4,5},{5,4},{6,7},{7,6},{8,9},{9,8},{10,11... | collective-permute-start | bytes 1916936 | tf_op jit(solution)/shard_map/ppermute | solution.py:509
  63.7 17.6 %collective-permute-start.15 = (bf16[4,96,768]{2,1,0:T(8,128)(2,1)}, bf16[4,96,768]{2,1,0:T(8,128)(2,1)}, u32[]{:S(2)}, u32[]{:S(2)}) collective-permute-start(bf16[4,96,768]{2,1,0:T(8,128)(2,1)} %collective-permute-done.11.b1), channel_id=1, source_target_pairs={{0,2},{1,9},{2,0},{3,11},{4,6},{5,13},{6,4},{7,15},{8,10},{9,1},{1... | collective-permute-start | bytes 1769480 | tf_op jit(solution)/shard_map/ppermute | solution.py:475
  72.8 17.1 %collective-permute-start.16 = (bf16[4,96,768]{2,1,0:T(8,128)(2,1)S(1)}, bf16[4,96,768]{2,1,0:T(8,128)(2,1)S(1)}, u32[]{:S(2)}, u32[]{:S(2)}) collective-permute-start(bf16[4,96,768]{2,1,0:T(8,128)(2,1)S(1)} %copy-done.12), channel_id=1, source_target_pairs={{0,1},{1,0},{2,3},{3,2},{4,5},{5,4},{6,7},{7,6},{8,9},{9,8},{10,11... | collective-permute-start | bytes 1769480 | tf_op jit(solution)/shard_map/ppermute | solution.py:509
  72.9 17.7 %collective-permute-start.17 = (bf16[4,96,768]{2,1,0:T(8,128)(2,1)}, bf16[4,96,768]{2,1,0:T(8,128)(2,1)S(1)}, u32[]{:S(2)}, u32[]{:S(2)}) collective-permute-start(bf16[4,96,768]{2,1,0:T(8,128)(2,1)} %collective-permute-done.11.b1), channel_id=1, source_target_pairs={{0,1},{1,0},{2,3},{3,2},{4,5},{5,4},{6,7},{7,6},{8,9},{9,8},{10,11... | collective-permute-start | bytes 1769480 | tf_op jit(solution)/shard_map/ppermute | solution.py:509
  73.4 17.8 %collective-permute-start.18 = (bf16[4,96,768]{2,1,0:T(8,128)(2,1)S(1)}, bf16[4,96,768]{2,1,0:T(8,128)(2,1)S(1)}, u32[]{:S(2)}, u32[]{:S(2)}) collective-permute-start(bf16[4,96,768]{2,1,0:T(8,128)(2,1)S(1)} %copy-done.26), channel_id=1, source_target_pairs={{0,1},{1,0},{2,3},{3,2},{4,5},{5,4},{6,7},{7,6},{8,9},{9,8},{10,11... | collective-permute-start | bytes 1769480 | tf_op jit(solution)/shard_map/ppermute | solution.py:509
  73.5 16.0 %collective-permute-start.21 = (bf16[4,96,768]{2,1,0:T(8,128)(2,1)S(1)}, bf16[4,96,768]{2,1,0:T(8,128)(2,1)S(1)}, u32[]{:S(2)}, u32[]{:S(2)}) collective-permute-start(bf16[4,96,768]{2,1,0:T(8,128)(2,1)S(1)} %pad_maximum_fusion.2.b0), channel_id=1, source_target_pairs={{0,8},{1,17},{2,10},{3,19},{4,12},{5,21},{6,14},{7,23},{8,0},{9,25... | collective-permute-start | bytes 1769480 | tf_op jit(solution)/shard_map/ppermute | solution.py:475
  105.8 23.3 %collective-permute-start.29 = (bf16[8,96,768]{2,1,0:T(8,128)(2,1)S(1)}, bf16[8,96,768]{2,1,0:T(8,128)(2,1)}, u32[]{:S(2)}, u32[]{:S(2)}) collective-permute-start(bf16[8,96,768]{2,1,0:T(8,128)(2,1)S(1)} %add_convert_fusion.2), channel_id=1, source_target_pairs={{0,8},{1,3},{2,10},{3,1},{4,12},{5,7},{6,14},{7,5},{8,0},{9,11},{1... | collective-permute-start | bytes 3538952 | tf_op jit(solution)/shard_map/ppermute | solution.py:533
  113.2 35.3 %collective-permute-start.36 = (bf16[8,96,768]{2,1,0:T(8,128)(2,1)S(1)}, bf16[8,96,768]{2,1,0:T(8,128)(2,1)S(1)}, u32[]{:S(2)}, u32[]{:S(2)}) collective-permute-start(bf16[8,96,768]{2,1,0:T(8,128)(2,1)S(1)} %add_convert_fusion.1), channel_id=1, source_target_pairs={{0,4},{1,5},{2,6},{3,7},{4,0},{5,1},{6,2},{7,3},{8,12},{9,13},{10,... | collective-permute-start | bytes 3538952 | tf_op jit(solution)/shard_map/ppermute | solution.py:533
  140.9 15.5 %collective-permute-start.32 = (bf16[8,96,768]{2,1,0:T(8,128)(2,1)S(1)}, bf16[8,96,768]{2,1,0:T(8,128)(2,1)S(1)}, u32[]{:S(2)}, u32[]{:S(2)}) collective-permute-start(bf16[8,96,768]{2,1,0:T(8,128)(2,1)S(1)} %add_convert_fusion), channel_id=1, source_target_pairs={{0,2},{1,5},{2,0},{3,7},{4,6},{5,1},{6,4},{7,3},{8,10},{9,13},{10,... | collective-permute-start | bytes 3538952 | tf_op jit(solution)/shard_map/ppermute | solution.py:533
  144.4 14.0 %collective-permute-start.42 = (f32[24,768]{1,0:T(8,128)S(1)}, f32[24,768]{1,0:T(8,128)S(1)}, u32[]{:S(2)}, u32[]{:S(2)}) collective-permute-start(f32[24,768]{1,0:T(8,128)S(1)} %get-tuple-element.184), channel_id=1, source_target_pairs={{0,1},{1,0},{2,3},{3,2},{4,5},{5,4},{6,7},{7,6},{8,9},{9,8},{10,11... | collective-permute-start | bytes 221192 | tf_op jit(solution)/shard_map/ppermute | solution.py:461
  146.8 23.6 %collective-permute-start.40 = (bf16[2,96,768]{2,1,0:T(8,128)(2,1)}, bf16[2,96,768]{2,1,0:T(8,128)(2,1)}, u32[]{:S(2)}, u32[]{:S(2)}) collective-permute-start(bf16[2,96,768]{2,1,0:T(8,128)(2,1)} %add_convert_fusion.6), channel_id=1, source_target_pairs={{0,16},{1,17},{2,18},{3,19},{4,20},{5,21},{6,22},{7,23},{8,24},{9,... | collective-permute-start | bytes 884744 | tf_op jit(solution)/shard_map/ppermute | solution.py:533
  151.0 21.3 %collective-permute-start.37 = (bf16[4,96,768]{2,1,0:T(8,128)(2,1)}, bf16[4,96,768]{2,1,0:T(8,128)(2,1)}, u32[]{:S(2)}, u32[]{:S(2)}) collective-permute-start(bf16[4,96,768]{2,1,0:T(8,128)(2,1)} %add_convert_fusion.3), channel_id=1, source_target_pairs={{0,8},{1,9},{2,10},{3,11},{4,12},{5,13},{6,14},{7,15},{8,0},{9,1},... | collective-permute-start | bytes 1769480 | tf_op jit(solution)/shard_map/ppermute | solution.py:533
  157.7 16.6 %collective-permute-start.33 = (bf16[4,96,768]{2,1,0:T(8,128)(2,1)}, bf16[4,96,768]{2,1,0:T(8,128)(2,1)}, u32[]{:S(2)}, u32[]{:S(2)}) collective-permute-start(bf16[4,96,768]{2,1,0:T(8,128)(2,1)} %add_convert_fusion.4), channel_id=1, source_target_pairs={{0,4},{1,3},{2,6},{3,1},{4,0},{5,7},{6,2},{7,5},{8,12},{9,11},{10,... | collective-permute-start | bytes 1769480 | tf_op jit(solution)/shard_map/ppermute | solution.py:533
  173.8 12.5 %collective-permute-start.38 = (bf16[2,96,768]{2,1,0:T(8,128)(2,1)S(1)}, bf16[2,96,768]{2,1,0:T(8,128)(2,1)S(1)}, u32[]{:S(2)}, u32[]{:S(2)}) collective-permute-start(bf16[2,96,768]{2,1,0:T(8,128)(2,1)S(1)} %add_convert_fusion.7), channel_id=1, source_target_pairs={{0,2},{1,17},{2,0},{3,19},{4,6},{5,21},{6,4},{7,23},{8,10},{9,25},... | collective-permute-start | bytes 884744 | tf_op jit(solution)/shard_map/ppermute | solution.py:533
  175.6 17.5 %collective-permute-start.34 = (bf16[2,96,768]{2,1,0:T(8,128)(2,1)S(1)}, bf16[2,96,768]{2,1,0:T(8,128)(2,1)S(1)}, u32[]{:S(2)}, u32[]{:S(2)}) collective-permute-start(bf16[2,96,768]{2,1,0:T(8,128)(2,1)S(1)} %add_convert_fusion.8), channel_id=1, source_target_pairs={{0,8},{1,17},{2,10},{3,19},{4,12},{5,21},{6,14},{7,23},{8,0},{9,25... | collective-permute-start | bytes 884744 | tf_op jit(solution)/shard_map/ppermute | solution.py:533
  180.0 14.6 %collective-permute-start.45 = (f32[24,768]{1,0:T(8,128)S(1)}, f32[24,768]{1,0:T(8,128)S(1)}, u32[]{:S(2)}, u32[]{:S(2)}) collective-permute-start(f32[24,768]{1,0:T(8,128)S(1)} %add.286), channel_id=1, source_target_pairs={{0,8},{1,9},{2,10},{3,11},{4,12},{5,13},{6,14},{7,15},{8,0},{9,1},... | collective-permute-start | bytes 221192 | tf_op jit(solution)/shard_map/ppermute | solution.py:461
  (70 other events, 709.7 us)

commit v5 on v4

--- a/solution.py
+++ b/solution.py
@@ -160,7 +160,7 @@
     low = jnp.concatenate([vectors[0:8, :], fill], axis=1)
     high = jnp.concatenate([vectors[8:11, :], jnp.zeros((5, BLOCK_ROWS), F32)], axis=0)
     high = jnp.concatenate([high, fill], axis=1)
-    last = jnp.concatenate([expand_bias[...], jnp.zeros((EXTRA - 1, 384), F32)], axis=0)
+    last = jnp.concatenate([expand_bias[...].reshape(1, 384), jnp.zeros((EXTRA - 1, 384), F32)], axis=0)
     extra = jnp.concatenate([low, high, last, jnp.zeros((EXTRA, 128), F32)], axis=1)
     out[...] = jnp.concatenate([block, extra], axis=0).astype(BF16)
 
@@ -533,6 +533,15 @@
         self.terms.append(lax.ppermute(sent, AXES, pairs_of(self.orders, self.level)))
         return sent
 
+    def spread(self, *earlier):
+        if earlier:
+            self.hold(*earlier)
+        sent = [self.total(place, place + 1).astype(BF16) for place in (1, 2, 3)]
+        for place, values in zip((1, 2, 3), sent, strict=True):
+            pairs = [(dev, dev ^ offset_of(self.orders[dev & 1], place)) for dev in range(32)]
+            self.terms.append(lax.ppermute(values, AXES, pairs))
+        return sent
+
     def hold(self, *earlier):
         self.terms[-1] = after(self.terms[-1], *earlier)
 
@@ -607,7 +616,7 @@
         tables = [table[0:80], table[80:160], table[160:240]]
         (piece_one,) = call(
             pack_kernel,
-            (project_qkv, project_out, vectors, expand_bias[None]),
+            (project_qkv, project_out, vectors, expand_bias),
             (shape((BLOCK_ROWS + EXTRA, D)),),
             table=False,
         )
@@ -782,11 +791,10 @@
         part = send_across(sums, 16)
         three.step(sent)
         two.step(sent)
-        sent = one.step()
+        sent = one.spread()
         sums = sums + after(part, sent)
         part = send_across(sums, 8)
         two.step(sent)
-        sent = one.step()
         sums = add_across(sums + after(part, sent), 4)
         grad_three = three.result()
         states_three = adam_update(

time: 201 us -> 198 us (0.985)
  other arithmetic: 27.8 us -> 21.1 us
  starting transfers between devices: 55.3 us -> 59.7 us
    convert_element_type x12 -> x10, other arithmetic: 16.7 us -> 10.1 us  [step(): sent = self.total(size, 2 * size).astype(BF16)]
    ppermute x0 -> x3, starting transfers between devices: none -> 3.6 us  [spread(): self.terms.append(lax.ppermute(values, AXES, pairs))]
    ppermute x0 -> x3, waiting for transfers between devices: none -> 3 us  [spread(): self.terms.append(lax.ppermute(values, AXES, pairs))]
    concatenate x6, other arithmetic: 3.1 us -> 0.26 us  [take(): self.held = jnp.concatenate([self.held, self.taken], axis=0)]
    ppermute x12 -> x10, waiting for transfers between devices: 14.3 us -> 11.6 us  [step(): lax.ppermute(sent, AXES, pairs_of(self.orders, self.level))]
    ppermute x12 -> x10, starting transfers between devices: 11 us -> 9.8 us  [step(): lax.ppermute(sent, AXES, pairs_of(self.orders, self.level))]
    unnamed x94 -> x88, local copies, waits for them, and re-layouts: 4.84 us -> 4.27 us
  transfers between devices with their start and end apart: 47 -> 48, of which waited for: 14 -> 12; matrix products, arithmetic and copies ran while one was open for 15% -> 11% of each run, Pallas kernels for 28% -> 29%
where the time goes in v5:
time: 198 us
  starting transfers between devices  59.7 us (30%)
  Pallas kernels  57.4 us (29%)
  waiting for transfers between devices  52 us (26%)
  other arithmetic  21.1 us (11%)
  local copies, waits for them, and re-layouts  5.93 us (3%)
    pallas_call x14, Pallas kernels, call(): pl.pallas_call(kernel, out_shape=outs, in_specs=[SMEM] * table + [VMEM] *...  57.4 us
    ppermute x15, waiting for transfers between devices, send(): return lax.ppermute(values, AXES, pairs_of(self.orders, level))  26.6 us
    ppermute x12, starting transfers between devices, sib(): return tuple((lax.ppermute(values, AXES, CORE_PAIRS) for values in own))  20.3 us
    ppermute x15, starting transfers between devices, send(): return lax.ppermute(values, AXES, pairs_of(self.orders, level))  19.7 us
    ppermute x10, waiting for transfers between devices, step(): lax.ppermute(sent, AXES, pairs_of(self.orders, self.level))  11.6 us
    convert_element_type x10, other arithmetic, step(): sent = self.total(size, 2 * size).astype(BF16)  10.1 us
    ppermute x10, starting transfers between devices, step(): lax.ppermute(sent, AXES, pairs_of(self.orders, self.level))  9.8 us
    ppermute x5, waiting for transfers between devices, send_across(): return lax.ppermute(values, AXES, [(dev, dev ^ mask) for dev in range(32)])  9.23 us
  transfers between devices with their start and end apart: 48, of which 12 were waited for; matrix products, arithmetic and copies ran while one was open for 11% of the time, Pallas kernels for 29%

profile of v5, /device:TPU:1, one launch (start us, length us, event | category | flops | bytes accessed | tf_op | source)
XLA Modules:
  0.0 197.6 jit_solution(14203013967940392636)
XLA Ops:
  11.5 2.5 %collective-permute-start.1 = (bf16[2,104,768]{2,1,0:T(8,128)(2,1)S(1)}, bf16[2,104,768]{2,1,0:T(8,128)(2,1)S(1)}, u32[]{:S(2)}, u32[]{:S(2)}) collective-permute-start(bf16[2,104,768]{2,1,0:T(8,128)(2,1)S(1)} %pad_maximum_fusion.3), channel_id=1, source_target_pairs={{0,8},{1,17},{2,10},{3,19},{4,12},{5,21},{6,14},{7,23},{8,0},{9,25... | collective-permute-start | bytes 958472 | tf_op jit(solution)/shard_map/ppermute | solution.py:475
  16.8 2.8 %collective-permute-done.5 = bf16[2,96,768]{2,1,0:T(8,128)(2,1)S(1)} collective-permute-done((bf16[2,96,768]{2,1,0:T(8,128)(2,1)S(1)}, bf16[2,96,768]{2,1,0:T(8,128)(2,1)S(1)}, u32[]{:S(2)}, u32[]{:S(2)}) %collective-permute-start.5) | collective-permute-done | bytes 294944 | tf_op jit(solution)/shard_map/ppermute | solution.py:475
  19.7 3.4 %collective-permute-done.1 = bf16[2,104,768]{2,1,0:T(8,128)(2,1)S(1)} collective-permute-done((bf16[2,104,768]{2,1,0:T(8,128)(2,1)S(1)}, bf16[2,104,768]{2,1,0:T(8,128)(2,1)S(1)}, u32[]{:S(2)}, u32[]{:S(2)}) %collective-permute-start.1) | collective-permute-done | bytes 319520 | tf_op jit(solution)/shard_map/ppermute | solution.py:475
  25.9 3.3 %collective-permute-start.12 = (bf16[4,96,768]{2,1,0:T(8,128)(2,1)S(1)}, bf16[4,96,768]{2,1,0:T(8,128)(2,1)}, u32[]{:S(2)}, u32[]{:S(2)}) collective-permute-start(bf16[4,96,768]{2,1,0:T(8,128)(2,1)S(1)} %pad_maximum_fusion.1.b0), channel_id=1, source_target_pairs={{0,2},{1,9},{2,0},{3,11},{4,6},{5,13},{6,4},{7,15},{8,10},{9,1},{1... | collective-permute-start | bytes 1769480 | tf_op jit(solution)/shard_map/ppermute | solution.py:475
  29.5 9.2 %collective-permute-done.13 = bf16[2,96,768]{2,1,0:T(8,128)(2,1)S(1)} collective-permute-done((bf16[2,96,768]{2,1,0:T(8,128)(2,1)S(1)}, bf16[2,96,768]{2,1,0:T(8,128)(2,1)S(1)}, u32[]{:S(2)}, u32[]{:S(2)}) %collective-permute-start.13) | collective-permute-done | bytes 294944 | tf_op jit(solution)/shard_map/ppermute | solution.py:475
  38.7 10.6 %collective-permute-start.8 = (bf16[4,104,768]{2,1,0:T(8,128)(2,1)S(1)}, bf16[4,104,768]{2,1,0:T(8,128)(2,1)}, u32[]{:S(2)}, u32[]{:S(2)}) collective-permute-start(bf16[4,104,768]{2,1,0:T(8,128)(2,1)S(1)} %pad_maximum_fusion.b0), channel_id=1, source_target_pairs={{0,1},{1,0},{2,3},{3,2},{4,5},{5,4},{6,7},{7,6},{8,9},{9,8},{10,11... | collective-permute-start | bytes 1916936 | tf_op jit(solution)/shard_map/ppermute | solution.py:509
  53.7 5.5 %collective-permute-done.7.b3 = bf16[4,104,768]{2,1,0:T(8,128)(2,1)} collective-permute-done((bf16[4,104,768]{2,1,0:T(8,128)(2,1)}, bf16[4,104,768]{2,1,0:T(8,128)(2,1)}, u32[]{:S(2)}, u32[]{:S(2)}) %collective-permute-start.7) | collective-permute-done | bytes 639008 | tf_op jit(solution)/shard_map/ppermute | solution.py:475
  59.2 3.8 %collective-permute-start.14 = (bf16[4,104,768]{2,1,0:T(8,128)(2,1)}, bf16[4,104,768]{2,1,0:T(8,128)(2,1)}, u32[]{:S(2)}, u32[]{:S(2)}) collective-permute-start(bf16[4,104,768]{2,1,0:T(8,128)(2,1)} %collective-permute-done.7.b3), channel_id=1, source_target_pairs={{0,1},{1,0},{2,3},{3,2},{4,5},{5,4},{6,7},{7,6},{8,9},{9,8},{10,11... | collective-permute-start | bytes 1916936 | tf_op jit(solution)/shard_map/ppermute | solution.py:509
  64.0 6.9 %shard_map.367 = (f32[16,768]{1,0:T(8,128)S(1)}, f32[4,1,768]{2,1,0:T(1,128)S(1)}, f32[416,768]{1,0:T(8,128)S(1)}, bf16[416,768]{1,0:T(8,128)(2,1)S(1)}, f32[4,1...) custom-call(s32[80]{0:T(128)S(1)} %get-tuple-element.204.tab, ...), custom_call_target="tpu_custom_call" | custom-call | flops 1 | bytes 1 | tf_op jit(solution)/shard_map/pallas_call | solution.py:440
  73.3 6.9 %shard_map.369 = (bf16[2,768,768]{2,1,0:T(8,128)(2,1)S(1)}, bf16[2,416,576]{2,1,0:T(8,128)(2,1)S(1)}, f32[12,208,208]{2,1,0:T(8,128)S(1)}, bf16[2,416,192]{2,1,0...) custom-call(s32[80]{0:T(128)S(1)} %get-tuple-element.204.tab, ...), custom_call_target="tpu_custom_call" | custom-call | flops 1 | bytes 1 | tf_op jit(solution)/shard_map/pallas_call | solution.py:440
  81.5 4.7 %shard_map.370 = (bf16[2,768,768]{2,1,0:T(8,128)(2,1)S(1)}, bf16[2,416,768]{2,1,0:T(8,128)(2,1)S(1)}, f32[2,416,768]{2,1,0:T(8,128)S(1)}, bf16[416,768]{1,0:T(8,128)(2,1)S(1)}, bf16[16,96,768]{2,1,0:T(8,128)(2,1)S(1)}) custom-call(s32[80]{0:T(128)S(1)} %get-tuple-element.205.tab, bf16[416,768]{1,0:T(8,128)(2,1)S(1)} %get-tuple-element.120.normed_two, ...), custom_call_target="tpu_custom_call" | custom-call | flops 99999997952 | bytes 1 | tf_op jit(solution)/shard_map/pallas_call | solution.py:440
  90.2 3.7 %shard_map.371 = (bf16[2,768,768]{2,1,0:T(8,128)(2,1)S(1)}, bf16[2,416,768]{2,1,0:T(8,128)(2,1)S(1)}, f32[2,416,768]{2,1,0:T(8,128)S(1)}, bf16[16,96,768]{2,1,0:T(8,128)(2,1)S(1)}) custom-call(s32[80]{0:T(128)S(1)} %get-tuple-element.205.tab, bf16[416,768]{1,0:T(8,128)(2,1)S(1)} %get-tuple-element.120.normed_two, ...), custom_call_target="tpu_custom_call" | custom-call | flops 1 | bytes 1 | tf_op jit(solution)/shard_map/pallas_call | solution.py:440
  93.9 3.3 %collective-permute-done.25.b3 = bf16[4,96,768]{2,1,0:T(8,128)(2,1)S(1)} collective-permute-done((bf16[4,96,768]{2,1,0:T(8,128)(2,1)S(1)}, bf16[4,96,768]{2,1,0:T(8,128)(2,1)S(1)}, u32[]{:S(2)}, u32[]{:S(2)}) %collective-permute-start.25) | collective-permute-done | bytes 589856 | tf_op jit(solution)/shard_map/ppermute | solution.py:475
  99.7 3.6 %shard_map.372 = (bf16[2,768,768]{2,1,0:T(8,128)(2,1)S(1)}, bf16[2,416,768]{2,1,0:T(8,128)(2,1)S(1)}, f32[2,1,768]{2,1,0:T(1,128)S(1)}, bf16[16,96,768]{2,1,0:T(8,128)(2,1)S(1)}) custom-call(s32[80]{0:T(128)S(1)} %get-tuple-element.203.tab, bf16[416,768]{1,0:T(8,128)(2,1)S(1)} %get-tuple-element.120.normed_two, ...), custom_call_target="tpu_custom_call" | custom-call | flops 99999997952 | bytes 1 | tf_op jit(solution)/shard_map/pallas_call | solution.py:440
  106.3 3.7 %shard_map.373 = (bf16[2,768,768]{2,1,0:T(8,128)(2,1)S(1)}, bf16[2,416,768]{2,1,0:T(8,128)(2,1)S(1)}, f32[2,1,768]{2,1,0:T(1,128)S(1)}, bf16[16,96,768]{2,1,0:T(8,128)(2,1)S(1)}) custom-call(s32[80]{0:T(128)S(1)} %get-tuple-element.203.tab, bf16[416,768]{1,0:T(8,128)(2,1)S(1)} %get-tuple-element.120.normed_two, ...), custom_call_target="tpu_custom_call" | custom-call | flops 99999997952 | bytes 1 | tf_op jit(solution)/shard_map/pallas_call | solution.py:440
  111.7 5.7 %shard_map.374 = (bf16[394,768]{1,0:T(8,128)(2,1)}, f32[416,768]{1,0:T(8,128)S(1)}, bf16[416,768]{1,0:T(8,128)(2,1)S(1)}, f32[16,768]{1,0:T(8,128)S(1)}) custom-call(bf16[2,416,768]{2,1,0:T(8,128)(2,1)S(1)} %get-tuple-element.124.act_sib, bf16[2,416,768]{2,1,0:T(8,128)(2,1)S(1)} %get-tuple-element.125.act_own, ...), custom_call_target="tpu_custom_call" | custom-call | flops 1 | bytes 1 | tf_op jit(solution)/shard_map/pallas_call | solution.py:440
  117.4 8.8 %shard_map.375 = (bf16[16,96,768]{2,1,0:T(8,128)(2,1)S(1)}, f32[416,768]{1,0:T(8,128)S(1)}, f32[2,2,192]{2,1,0:T(2,128)S(1)}) custom-call(s32[80]{0:T(128)S(1)} %get-tuple-element.204.tab, bf16[2,768,768]{2,1,0:T(8,128)(2,1)S(1)} %get-tuple-element.152.w1, bf16[416,768]{1,0:T(8,128)(2,1)S(1)} %copy-done.1, bf16[2,416,576]{2,1,0:T(8,128)(2,1)S(1)} %get-tuple-element.153.qkv, ...), custom_call_target="tpu_custom_call" | custom-call | flops 1 | bytes 1 | tf_op jit(solution)/shard_map/pallas_call | solution.py:440
  128.9 9.1 %shard_map.376 = (bf16[16,96,768]{2,1,0:T(8,128)(2,1)S(1)}, f32[416,768]{1,0:T(8,128)S(1)}, f32[2,2,192]{2,1,0:T(2,128)S(1)}) custom-call(s32[80]{0:T(128)S(1)} %get-tuple-element.204.tab, bf16[2,768,768]{2,1,0:T(8,128)(2,1)S(1)} %get-tuple-element.147.w1, bf16[416,768]{1,0:T(8,128)(2,1)S(1)} %copy-done.1, bf16[2,416,576]{2,1,0:T(8,128)(2,1)S(1)} %get-tuple-element.148.qkv, ...), custom_call_target="tpu_custom_call" | custom-call | flops 99999997952 | bytes 1 | tf_op jit(solution)/shard_map/pallas_call | solution.py:440
  139.2 2.7 %shard_map.377 = (bf16[394,768]{1,0:T(8,128)(2,1)}, f32[24,768]{1,0:T(8,128)S(1)}) custom-call(s32[80]{0:T(128)S(1)} %get-tuple-element.204.tab, bf16[416,768]{1,0:T(8,128)(2,1)S(1)} %shard_map.366.tok, f32[416,1]{1,0:T(8,128)S(1)} %copy.42.rep, f32[16,768]{1,0:T(8,128)S(1)} %copy-done.12, f32[416,768]{1,0:T(8,128)S(1)} %get-tuple-element.164.grad_one, ...), custom_call_target="tpu_custom_call" | custom-call | flops 1 | bytes 1 | tf_op jit(solution)/shard_map/pallas_call | solution.py:440
  146.3 7.5 %collective-permute-done.32 = bf16[8,96,768]{2,1,0:T(8,128)(2,1)S(1)} collective-permute-done((bf16[8,96,768]{2,1,0:T(8,128)(2,1)S(1)}, bf16[8,96,768]{2,1,0:T(8,128)(2,1)S(1)}, u32[]{:S(2)}, u32[]{:S(2)}) %collective-permute-start.32) | collective-permute-done | bytes 1179680 | tf_op jit(solution)/shard_map/ppermute | solution.py:533
  156.6 9.2 %collective-permute-done.44 = f32[24,768]{1,0:T(8,128)S(1)} collective-permute-done((f32[24,768]{1,0:T(8,128)S(1)}, f32[24,768]{1,0:T(8,128)S(1)}, u32[]{:S(2)}, u32[]{:S(2)}) %collective-permute-start.44) | collective-permute-done | bytes 73760 | tf_op jit(solution)/shard_map/ppermute | solution.py:461
  174.7 4.0 %collective-permute-done.39 = bf16[2,96,768]{2,1,0:T(8,128)(2,1)S(1)} collective-permute-done((bf16[2,96,768]{2,1,0:T(8,128)(2,1)S(1)}, bf16[2,96,768]{2,1,0:T(8,128)(2,1)S(1)}, u32[]{:S(2)}, u32[]{:S(2)}) %collective-permute-start.39) | collective-permute-done | bytes 294944 | tf_op jit(solution)/shard_map/ppermute | solution.py:533
  188.3 2.3 %multiply_subtract_fusion.1 = (f32[96,768]{1,0:T(8,128)}, f32[96,768]{1,0:T(8,128)}, f32[96,768]{1,0:T(8,128)}) fusion(f32[96,768]{1,0:T(8,128)S(1)} %copy-done.29, bf16[1,96,768]{2,1,0:T(8,128)(2,1)S(1)} %collective-permute-done.40, bf16[2,96,768]{2,1,0:T(8,128)(2,1)S(1)} %collective-permute-done.39, bf16[4,96,768]{2,1,0:T(8,128)(2,1)} %collective-permute-done.38, ...), kind=kLoop, calls=%fused_computation.24 | loop fusion | flops 1843200 | bytes 2654208 | tf_op jit(solution)/shard_map/sub | solution.py:407
  190.6 3.0 %collective-permute-done.35 = bf16[1,96,768]{2,1,0:T(8,128)(2,1)S(1)} collective-permute-done((bf16[1,96,768]{2,1,0:T(8,128)(2,1)S(1)}, bf16[1,96,768]{2,1,0:T(8,128)(2,1)S(1)}, u32[]{:S(2)}, u32[]{:S(2)}) %collective-permute-start.35) | collective-permute-done | bytes 147488 | tf_op jit(solution)/shard_map/ppermute | solution.py:542
  (212 shorter events, 69.9 us)
Async XLA Ops:
  9.5 16.2 %collective-permute-start.6 = (bf16[1,96,768]{2,1,0:T(8,128)(2,1)S(1)}, bf16[1,96,768]{2,1,0:T(8,128)(2,1)S(1)}, u32[]{:S(2)}, u32[]{:S(2)}) collective-permute-start(bf16[1,96,768]{2,1,0:T(8,128)(2,1)S(1)} %convert_bitcast_fusion), channel_id=1, source_target_pairs={{0,4},{1,9},{2,6},{3,11},{4,0},{5,13},{6,2},{7,15},{8,12},{9,1},{1... | collective-permute-start | bytes 442376 | tf_op jit(solution)/shard_map/ppermute | solution.py:475
  11.5 11.6 %collective-permute-start.1 = (bf16[2,104,768]{2,1,0:T(8,128)(2,1)S(1)}, bf16[2,104,768]{2,1,0:T(8,128)(2,1)S(1)}, u32[]{:S(2)}, u32[]{:S(2)}) collective-permute-start(bf16[2,104,768]{2,1,0:T(8,128)(2,1)S(1)} %pad_maximum_fusion.3), channel_id=1, source_target_pairs={{0,8},{1,17},{2,10},{3,19},{4,12},{5,21},{6,14},{7,23},{8,0},{9,25... | collective-permute-start | bytes 958472 | tf_op jit(solution)/shard_map/ppermute | solution.py:475
  23.2 26.1 %collective-permute-start.3 = (bf16[4,104,768]{2,1,0:T(8,128)(2,1)S(1)}, bf16[4,104,768]{2,1,0:T(8,128)(2,1)}, u32[]{:S(2)}, u32[]{:S(2)}) collective-permute-start(bf16[4,104,768]{2,1,0:T(8,128)(2,1)S(1)} %pad_maximum_fusion.b0), channel_id=1, source_target_pairs={{0,2},{1,5},{2,0},{3,7},{4,6},{5,1},{6,4},{7,3},{8,10},{9,13},{10,... | collective-permute-start | bytes 1916936 | tf_op jit(solution)/shard_map/ppermute | solution.py:475
  24.4 24.8 %collective-permute-start.4 = (bf16[4,104,768]{2,1,0:T(8,128)(2,1)S(1)}, bf16[4,104,768]{2,1,0:T(8,128)(2,1)}, u32[]{:S(2)}, u32[]{:S(2)}) collective-permute-start(bf16[4,104,768]{2,1,0:T(8,128)(2,1)S(1)} %pad_maximum_fusion.b0), channel_id=1, source_target_pairs={{0,4},{1,3},{2,6},{3,1},{4,0},{5,7},{6,2},{7,5},{8,12},{9,11},{10,... | collective-permute-start | bytes 1916936 | tf_op jit(solution)/shard_map/ppermute | solution.py:475
  25.8 23.5 %collective-permute-start.11 = (bf16[4,96,768]{2,1,0:T(8,128)(2,1)S(1)}, bf16[4,96,768]{2,1,0:T(8,128)(2,1)}, u32[]{:S(2)}, u32[]{:S(2)}) collective-permute-start(bf16[4,96,768]{2,1,0:T(8,128)(2,1)S(1)} %pad_maximum_fusion.1.b0), channel_id=1, source_target_pairs={{0,8},{1,17},{2,10},{3,19},{4,12},{5,21},{6,14},{7,23},{8,0},{9,25... | collective-permute-start | bytes 1769480 | tf_op jit(solution)/shard_map/ppermute | solution.py:475
  25.9 23.4 %collective-permute-start.12 = (bf16[4,96,768]{2,1,0:T(8,128)(2,1)S(1)}, bf16[4,96,768]{2,1,0:T(8,128)(2,1)}, u32[]{:S(2)}, u32[]{:S(2)}) collective-permute-start(bf16[4,96,768]{2,1,0:T(8,128)(2,1)S(1)} %pad_maximum_fusion.1.b0), channel_id=1, source_target_pairs={{0,2},{1,9},{2,0},{3,11},{4,6},{5,13},{6,4},{7,15},{8,10},{9,1},{1... | collective-permute-start | bytes 1769480 | tf_op jit(solution)/shard_map/ppermute | solution.py:475
  38.7 32.2 %collective-permute-start.8 = (bf16[4,104,768]{2,1,0:T(8,128)(2,1)S(1)}, bf16[4,104,768]{2,1,0:T(8,128)(2,1)}, u32[]{:S(2)}, u32[]{:S(2)}) collective-permute-start(bf16[4,104,768]{2,1,0:T(8,128)(2,1)S(1)} %pad_maximum_fusion.b0), channel_id=1, source_target_pairs={{0,1},{1,0},{2,3},{3,2},{4,5},{5,4},{6,7},{7,6},{8,9},{9,8},{10,11... | collective-permute-start | bytes 1916936 | tf_op jit(solution)/shard_map/ppermute | solution.py:509
  51.5 19.5 %collective-permute-start.10 = (bf16[4,104,768]{2,1,0:T(8,128)(2,1)}, bf16[4,104,768]{2,1,0:T(8,128)(2,1)}, u32[]{:S(2)}, u32[]{:S(2)}) collective-permute-start(bf16[4,104,768]{2,1,0:T(8,128)(2,1)} %collective-permute-done.4.b2), channel_id=1, source_target_pairs={{0,1},{1,0},{2,3},{3,2},{4,5},{5,4},{6,7},{7,6},{8,9},{9,8},{10,11... | collective-permute-start | bytes 1916936 | tf_op jit(solution)/shard_map/ppermute | solution.py:509
  53.7 17.7 %collective-permute-start.9 = (bf16[4,104,768]{2,1,0:T(8,128)(2,1)}, bf16[4,104,768]{2,1,0:T(8,128)(2,1)}, u32[]{:S(2)}, u32[]{:S(2)}) collective-permute-start(bf16[4,104,768]{2,1,0:T(8,128)(2,1)} %collective-permute-done.3.b1), channel_id=1, source_target_pairs={{0,1},{1,0},{2,3},{3,2},{4,5},{5,4},{6,7},{7,6},{8,9},{9,8},{10,11... | collective-permute-start | bytes 1916936 | tf_op jit(solution)/shard_map/ppermute | solution.py:509
  59.2 12.4 %collective-permute-start.14 = (bf16[4,104,768]{2,1,0:T(8,128)(2,1)}, bf16[4,104,768]{2,1,0:T(8,128)(2,1)}, u32[]{:S(2)}, u32[]{:S(2)}) collective-permute-start(bf16[4,104,768]{2,1,0:T(8,128)(2,1)} %collective-permute-done.7.b3), channel_id=1, source_target_pairs={{0,1},{1,0},{2,3},{3,2},{4,5},{5,4},{6,7},{7,6},{8,9},{9,8},{10,11... | collective-permute-start | bytes 1916936 | tf_op jit(solution)/shard_map/ppermute | solution.py:509
  63.0 17.2 %collective-permute-start.15 = (bf16[4,96,768]{2,1,0:T(8,128)(2,1)}, bf16[4,96,768]{2,1,0:T(8,128)(2,1)}, u32[]{:S(2)}, u32[]{:S(2)}) collective-permute-start(bf16[4,96,768]{2,1,0:T(8,128)(2,1)} %collective-permute-done.11.b1), channel_id=1, source_target_pairs={{0,2},{1,9},{2,0},{3,11},{4,6},{5,13},{6,4},{7,15},{8,10},{9,1},{1... | collective-permute-start | bytes 1769480 | tf_op jit(solution)/shard_map/ppermute | solution.py:475
  70.9 17.3 %collective-permute-start.16 = (bf16[4,96,768]{2,1,0:T(8,128)(2,1)}, bf16[4,96,768]{2,1,0:T(8,128)(2,1)S(1)}, u32[]{:S(2)}, u32[]{:S(2)}) collective-permute-start(bf16[4,96,768]{2,1,0:T(8,128)(2,1)} %copy-done.9), channel_id=1, source_target_pairs={{0,1},{1,0},{2,3},{3,2},{4,5},{5,4},{6,7},{7,6},{8,9},{9,8},{10,11... | collective-permute-start | bytes 1769480 | tf_op jit(solution)/shard_map/ppermute | solution.py:509
  71.0 18.4 %collective-permute-start.17 = (bf16[4,96,768]{2,1,0:T(8,128)(2,1)}, bf16[4,96,768]{2,1,0:T(8,128)(2,1)S(1)}, u32[]{:S(2)}, u32[]{:S(2)}) collective-permute-start(bf16[4,96,768]{2,1,0:T(8,128)(2,1)} %collective-permute-done.11.b1), channel_id=1, source_target_pairs={{0,1},{1,0},{2,3},{3,2},{4,5},{5,4},{6,7},{7,6},{8,9},{9,8},{10,11... | collective-permute-start | bytes 1769480 | tf_op jit(solution)/shard_map/ppermute | solution.py:509
  71.5 18.7 %collective-permute-start.18 = (bf16[4,96,768]{2,1,0:T(8,128)(2,1)}, bf16[4,96,768]{2,1,0:T(8,128)(2,1)S(1)}, u32[]{:S(2)}, u32[]{:S(2)}) collective-permute-start(bf16[4,96,768]{2,1,0:T(8,128)(2,1)} %collective-permute-done.12.b2), channel_id=1, source_target_pairs={{0,1},{1,0},{2,3},{3,2},{4,5},{5,4},{6,7},{7,6},{8,9},{9,8},{10,11... | collective-permute-start | bytes 1769480 | tf_op jit(solution)/shard_map/ppermute | solution.py:509
  71.6 15.3 %collective-permute-start.21 = (bf16[4,96,768]{2,1,0:T(8,128)(2,1)S(1)}, bf16[4,96,768]{2,1,0:T(8,128)(2,1)S(1)}, u32[]{:S(2)}, u32[]{:S(2)}) collective-permute-start(bf16[4,96,768]{2,1,0:T(8,128)(2,1)S(1)} %pad_maximum_fusion.2.b0), channel_id=1, source_target_pairs={{0,8},{1,17},{2,10},{3,19},{4,12},{5,21},{6,14},{7,23},{8,0},{9,25... | collective-permute-start | bytes 1769480 | tf_op jit(solution)/shard_map/ppermute | solution.py:475
  105.3 21.5 %collective-permute-start.29 = (bf16[8,96,768]{2,1,0:T(8,128)(2,1)}, bf16[8,96,768]{2,1,0:T(8,128)(2,1)}, u32[]{:S(2)}, u32[]{:S(2)}) collective-permute-start(bf16[8,96,768]{2,1,0:T(8,128)(2,1)} %add_convert_fusion.2), channel_id=1, source_target_pairs={{0,8},{1,3},{2,10},{3,1},{4,12},{5,7},{6,14},{7,5},{8,0},{9,11},{1... | collective-permute-start | bytes 3538952 | tf_op jit(solution)/shard_map/ppermute | solution.py:533
  110.4 32.2 %collective-permute-start.37 = (bf16[8,96,768]{2,1,0:T(8,128)(2,1)S(1)}, bf16[8,96,768]{2,1,0:T(8,128)(2,1)S(1)}, u32[]{:S(2)}, u32[]{:S(2)}) collective-permute-start(bf16[8,96,768]{2,1,0:T(8,128)(2,1)S(1)} %add_convert_fusion.1), channel_id=1, source_target_pairs={{0,4},{1,5},{2,6},{3,7},{4,0},{5,1},{6,2},{7,3},{8,12},{9,13},{10,... | collective-permute-start | bytes 3538952 | tf_op jit(solution)/shard_map/ppermute | solution.py:533
  126.2 11.8 %collective-permute-start.31 = (bf16[16,96,768]{2,1,0:T(8,128)(2,1)S(1)}, bf16[16,96,768]{2,1,0:T(8,128)(2,1)S(1)}, u32[]{:S(2)}, u32[]{:S(2)}) collective-permute-start(bf16[16,96,768]{2,1,0:T(8,128)(2,1)S(1)} %get-tuple-element.163), channel_id=1, source_target_pairs={{0,1},{1,0},{2,3},{3,2},{4,5},{5,4},{6,7},{7,6},{8,9},{9,8},{10,11... | collective-permute-start | bytes 7077896 | tf_op jit(solution)/shard_map/ppermute | solution.py:519
  138.3 15.5 %collective-permute-start.32 = (bf16[8,96,768]{2,1,0:T(8,128)(2,1)S(1)}, bf16[8,96,768]{2,1,0:T(8,128)(2,1)S(1)}, u32[]{:S(2)}, u32[]{:S(2)}) collective-permute-start(bf16[8,96,768]{2,1,0:T(8,128)(2,1)S(1)} %add_convert_fusion), channel_id=1, source_target_pairs={{0,2},{1,5},{2,0},{3,7},{4,6},{5,1},{6,4},{7,3},{8,10},{9,13},{10,... | collective-permute-start | bytes 3538952 | tf_op jit(solution)/shard_map/ppermute | solution.py:533
  141.9 14.2 %collective-permute-start.43 = (f32[24,768]{1,0:T(8,128)S(1)}, f32[24,768]{1,0:T(8,128)S(1)}, u32[]{:S(2)}, u32[]{:S(2)}) collective-permute-start(f32[24,768]{1,0:T(8,128)S(1)} %get-tuple-element.184), channel_id=1, source_target_pairs={{0,1},{1,0},{2,3},{3,2},{4,5},{5,4},{6,7},{7,6},{8,9},{9,8},{10,11... | collective-permute-start | bytes 221192 | tf_op jit(solution)/shard_map/ppermute | solution.py:461
  142.8 24.7 %collective-permute-start.38 = (bf16[4,96,768]{2,1,0:T(8,128)(2,1)S(1)}, bf16[4,96,768]{2,1,0:T(8,128)(2,1)}, u32[]{:S(2)}, u32[]{:S(2)}) collective-permute-start(bf16[4,96,768]{2,1,0:T(8,128)(2,1)S(1)} %add_convert_fusion.3), channel_id=1, source_target_pairs={{0,8},{1,9},{2,10},{3,11},{4,12},{5,13},{6,14},{7,15},{8,0},{9,1},... | collective-permute-start | bytes 1769480 | tf_op jit(solution)/shard_map/ppermute | solution.py:533
  144.7 22.8 %collective-permute-start.41 = (bf16[2,96,768]{2,1,0:T(8,128)(2,1)S(1)}, bf16[2,96,768]{2,1,0:T(8,128)(2,1)}, u32[]{:S(2)}, u32[]{:S(2)}) collective-permute-start(bf16[2,96,768]{2,1,0:T(8,128)(2,1)S(1)} %add_convert_fusion.6), channel_id=1, source_target_pairs={{0,16},{1,17},{2,18},{3,19},{4,20},{5,21},{6,22},{7,23},{8,24},{9,... | collective-permute-start | bytes 884744 | tf_op jit(solution)/shard_map/ppermute | solution.py:533
  155.0 17.0 %collective-permute-start.33 = (bf16[4,96,768]{2,1,0:T(8,128)(2,1)}, bf16[4,96,768]{2,1,0:T(8,128)(2,1)}, u32[]{:S(2)}, u32[]{:S(2)}) collective-permute-start(bf16[4,96,768]{2,1,0:T(8,128)(2,1)} %add_convert_fusion.4), channel_id=1, source_target_pairs={{0,4},{1,3},{2,6},{3,1},{4,0},{5,7},{6,2},{7,5},{8,12},{9,11},{10,... | collective-permute-start | bytes 1769480 | tf_op jit(solution)/shard_map/ppermute | solution.py:533
  173.7 13.0 %collective-permute-start.46 = (f32[24,768]{1,0:T(8,128)S(1)}, f32[24,768]{1,0:T(8,128)S(1)}, u32[]{:S(2)}, u32[]{:S(2)}) collective-permute-start(f32[24,768]{1,0:T(8,128)S(1)} %add.298), channel_id=1, source_target_pairs={{0,8},{1,9},{2,10},{3,11},{4,12},{5,13},{6,14},{7,15},{8,0},{9,1},... | collective-permute-start | bytes 221192 | tf_op jit(solution)/shard_map/ppermute | solution.py:461
  (68 other events, 686.2 us)

commit v6 on v5

--- a/solution.py
+++ b/solution.py
@@ -38,7 +38,8 @@
 BIT = {"c": 1, "x": 2, "y": 4, "1": 8, "2": 16}
 GATHER = (("21xy", "12yx"), ("2y1x", "yx21"), ("y21x", "1x2y"))
 SCATTER = (("21yx", "12xy"), ("2x1y", "x21y"), ("y2x1", "y21x"))
-STEPS = "S0S1S2D0S0D1S1D0S0D2S2F0D1S1D0S0D2S2D1S1F1D0"
+STEPS = "S0S1S2D1S1D0S0D2S2F0D1S1D0S0D2S2D1S1F1D0"
+SPREAD = (True, False, False)
 
 
 def offset_of(order, place):
@@ -51,6 +52,10 @@
 
 def pairs_of(orders, level):
     return [(dev, dev ^ BIT[orders[dev & 1][level]]) for dev in range(32)]
+
+
+def partners_of(orders, place):
+    return [(dev, dev ^ offset_of(orders[dev & 1], place)) for dev in range(32)]
 
 
 CORE_PAIRS = [(dev, dev ^ 1) for dev in range(32)]
@@ -466,10 +471,11 @@
 
 
 class Gather:
-    def __init__(self, block, orders):
+    def __init__(self, block, orders, spread):
         self.held = block[None]
         self.orders = orders
         self.level = 0
+        self.spread = spread
 
     def send(self, values, level):
         return lax.ppermute(values, AXES, pairs_of(self.orders, level))
@@ -477,8 +483,14 @@
     def start(self, *earlier):
         if earlier:
             self.held = after(self.held, *earlier)
-        if self.level < 3:
-            self.taken = self.send(self.held, self.level)
+        if self.level == 0 and self.spread:
+            self.taken = [
+                lax.ppermute(self.held, AXES, partners_of(self.orders, place))
+                for place in (1, 2, 3)
+            ]
+            self.level = 1
+        elif self.level < 3:
+            self.taken = [self.send(self.held, self.level)]
             if self.level == 2:
                 self.far = self.send(self.held, 3)
         else:
@@ -487,10 +499,11 @@
 
     def take(self):
         if self.level < 3:
-            self.held = jnp.concatenate([self.held, self.taken], axis=0)
+            self.held = jnp.concatenate([self.held, *self.taken], axis=0)
             return self.taken
         if self.level == 3:
             self.near = self.held
+            (self.taken,) = self.taken
             self.held = self.taken
             return self.taken, self.far
         return self.last
@@ -538,8 +551,7 @@
             self.hold(*earlier)
         sent = [self.total(place, place + 1).astype(BF16) for place in (1, 2, 3)]
         for place, values in zip((1, 2, 3), sent, strict=True):
-            pairs = [(dev, dev ^ offset_of(self.orders[dev & 1], place)) for dev in range(32)]
-            self.terms.append(lax.ppermute(values, AXES, pairs))
+            self.terms.append(lax.ppermute(values, AXES, partners_of(self.orders, place)))
         return sent
 
     def hold(self, *earlier):
@@ -621,8 +633,10 @@
             table=False,
         )
         streams = [
-            Gather(piece, orders)
-            for piece, orders in zip((piece_one, piece_two, piece_three), GATHER, strict=True)
+            Gather(piece, orders, spread)
+            for piece, orders, spread in zip(
+                (piece_one, piece_two, piece_three), GATHER, SPREAD, strict=True
+            )
         ]
         seen = {}
         for kind, index in zip(STEPS[0::2], STEPS[1::2], strict=True):

time: 198 us -> 197 us (level)
  waiting for transfers between devices: 52 us -> 33.1 us
  starting transfers between devices: 59.7 us -> 71.5 us
  other arithmetic: 21.1 us -> 26 us
    ppermute x15 -> x13, waiting for transfers between devices: 26.6 us -> 4.76 us  [send(): return lax.ppermute(values, AXES, pairs_of(self.orders, level))]
    ppermute x12, starting transfers between devices: 20.3 us -> 28 us  [sib(): return tuple((lax.ppermute(values, AXES, CORE_PAIRS) for values in own))]
    ppermute x3 -> x6, waiting for transfers between devices: 3 us -> 8.86 us  [the longest x3 5.54 us: spread(): lax.ppermute(values, AXES, partners_of(self.orders, place))]
    ppermute x3 -> x6, starting transfers between devices: 3.6 us -> 8.11 us  [the longest x3 4.5 us: start(): lax.ppermute(self.held, AXES, partners_of(self.orders, place))]
    convert_element_type x10, other arithmetic: 10.1 us -> 13.3 us  [step(): sent = self.total(size, 2 * size).astype(BF16)]
    ppermute x10, waiting for transfers between devices: 11.6 us -> 8.49 us  [step(): lax.ppermute(sent, AXES, pairs_of(self.orders, self.level))]
    unnamed x88 -> x98, local copies, waits for them, and re-layouts: 4.27 us -> 5.82 us
    ppermute x15 -> x13, starting transfers between devices: 19.7 us -> 20.1 us  [send(): return lax.ppermute(values, AXES, pairs_of(self.orders, level))]
  transfers between devices with their start and end apart: 48 -> 49, of which waited for: 12 -> 9; matrix products, arithmetic and copies ran while one was open for 11% -> 13% of each run, Pallas kernels for 29% -> 29%
where the time goes in v6:
time: 197 us; the launch traced here: 196 us
  starting transfers between devices  71.5 us (36%)
  Pallas kernels  56.6 us (29%)
  waiting for transfers between devices  33.1 us (17%)
  other arithmetic  26 us (13%)
  local copies, waits for them, and re-layouts  7.49 us (4%)
    pallas_call x14, Pallas kernels, call(): pl.pallas_call(kernel, out_shape=outs, in_specs=[SMEM] * table + [VMEM] *...  56.6 us
    ppermute x12, starting transfers between devices, sib(): return tuple((lax.ppermute(values, AXES, CORE_PAIRS) for values in own))  28 us
    ppermute x13, starting transfers between devices, send(): return lax.ppermute(values, AXES, pairs_of(self.orders, level))  20.1 us
    convert_element_type x10, other arithmetic, step(): sent = self.total(size, 2 * size).astype(BF16)  13.3 us
    ppermute x5, waiting for transfers between devices, send_across(): return lax.ppermute(values, AXES, [(dev, dev ^ mask) for dev in range(32)])  9.36 us
    ppermute x10, starting transfers between devices, step(): lax.ppermute(sent, AXES, pairs_of(self.orders, self.level))  9.3 us
    ppermute x10, waiting for transfers between devices, step(): lax.ppermute(sent, AXES, pairs_of(self.orders, self.level))  8.49 us
    sub x4, other arithmetic, adam_update(): weight - step_rate * (first_hat / (jnp.sqrt(second_hat) + EPSILON) + deca...  5.95 us
  transfers between devices with their start and end apart: 49, of which 9 were waited for; matrix products, arithmetic and copies ran while one was open for 13% of the time, Pallas kernels for 29%

profile of v6, /device:TPU:1, one launch (start us, length us, event | category | flops | bytes accessed | tf_op | source)
XLA Modules:
  0.0 196.2 jit_solution(7760844699215534087)
XLA Ops:
  6.3 2.3 %collective-permute-start.1 = (bf16[1,104,768]{2,1,0:T(8,128)(2,1)S(1)}, bf16[1,104,768]{2,1,0:T(8,128)(2,1)S(1)}, u32[]{:S(2)}, u32[]{:S(2)}) collective-permute-start(bf16[1,104,768]{2,1,0:T(8,128)(2,1)S(1)} %bitcast.33), channel_id=1, source_target_pairs={{0,8},{1,17},{2,10},{3,19},{4,12},{5,21},{6,14},{7,23},{8,0},{9,25... | collective-permute-start | bytes 479240 | tf_op jit(solution)/shard_map/ppermute | solution.py:488
  15.8 3.3 %collective-permute-done.1 = bf16[1,104,768]{2,1,0:T(8,128)(2,1)S(1)} collective-permute-done((bf16[1,104,768]{2,1,0:T(8,128)(2,1)S(1)}, bf16[1,104,768]{2,1,0:T(8,128)(2,1)S(1)}, u32[]{:S(2)}, u32[]{:S(2)}) %collective-permute-start.1) | collective-permute-done | bytes 159776 | tf_op jit(solution)/shard_map/ppermute | solution.py:488
  22.1 6.3 %collective-permute-start.12 = (bf16[4,96,768]{2,1,0:T(8,128)(2,1)S(1)}, bf16[4,96,768]{2,1,0:T(8,128)(2,1)}, u32[]{:S(2)}, u32[]{:S(2)}) collective-permute-start(bf16[4,96,768]{2,1,0:T(8,128)(2,1)S(1)} %pad_maximum_fusion.1.b0), channel_id=1, source_target_pairs={{0,8},{1,17},{2,10},{3,19},{4,12},{5,21},{6,14},{7,23},{8,0},{9,25... | collective-permute-start | bytes 1769480 | tf_op jit(solution)/shard_map/ppermute | solution.py:481
  28.8 13.0 %collective-permute-start.9 = (bf16[4,104,768]{2,1,0:T(8,128)(2,1)S(1)}, bf16[4,104,768]{2,1,0:T(8,128)(2,1)S(1)}, u32[]{:S(2)}, u32[]{:S(2)}) collective-permute-start(bf16[4,104,768]{2,1,0:T(8,128)(2,1)S(1)} %pad_maximum_fusion.b0), channel_id=1, source_target_pairs={{0,1},{1,0},{2,3},{3,2},{4,5},{5,4},{6,7},{7,6},{8,9},{9,8},{10,11... | collective-permute-start | bytes 1916936 | tf_op jit(solution)/shard_map/ppermute | solution.py:522
  42.0 9.5 %collective-permute-start.10 = (bf16[4,104,768]{2,1,0:T(8,128)(2,1)}, bf16[4,104,768]{2,1,0:T(8,128)(2,1)S(1)}, u32[]{:S(2)}, u32[]{:S(2)}) collective-permute-start(bf16[4,104,768]{2,1,0:T(8,128)(2,1)} %collective-permute-done.4.b1), channel_id=1, source_target_pairs={{0,1},{1,0},{2,3},{3,2},{4,5},{5,4},{6,7},{7,6},{8,9},{9,8},{10,11... | collective-permute-start | bytes 1916936 | tf_op jit(solution)/shard_map/ppermute | solution.py:522
  54.2 4.9 %collective-permute-start.16 = (bf16[4,96,768]{2,1,0:T(8,128)(2,1)}, bf16[4,96,768]{2,1,0:T(8,128)(2,1)}, u32[]{:S(2)}, u32[]{:S(2)}) collective-permute-start(bf16[4,96,768]{2,1,0:T(8,128)(2,1)} %collective-permute-done.12.b1), channel_id=1, source_target_pairs={{0,2},{1,9},{2,0},{3,11},{4,6},{5,13},{6,4},{7,15},{8,10},{9,1},{1... | collective-permute-start | bytes 1769480 | tf_op jit(solution)/shard_map/ppermute | solution.py:481
  60.5 6.9 %shard_map.367 = (f32[16,768]{1,0:T(8,128)S(1)}, f32[4,1,768]{2,1,0:T(1,128)S(1)}, f32[416,768]{1,0:T(8,128)S(1)}, bf16[416,768]{1,0:T(8,128)(2,1)S(1)}, f32[4,1...) custom-call(s32[80]{0:T(128)S(1)} %get-tuple-element.202.tab, ...), custom_call_target="tpu_custom_call" | custom-call | flops 1 | bytes 1 | tf_op jit(solution)/shard_map/pallas_call | solution.py:445
  67.5 2.3 %collective-permute-start.22 = (bf16[4,96,768]{2,1,0:T(8,128)(2,1)S(1)}, bf16[4,96,768]{2,1,0:T(8,128)(2,1)S(1)}, u32[]{:S(2)}, u32[]{:S(2)}) collective-permute-start(bf16[4,96,768]{2,1,0:T(8,128)(2,1)S(1)} %pad_maximum_fusion.2.b0), channel_id=1, source_target_pairs={{0,8},{1,17},{2,10},{3,19},{4,12},{5,21},{6,14},{7,23},{8,0},{9,25... | collective-permute-start | bytes 1769480 | tf_op jit(solution)/shard_map/ppermute | solution.py:481
  70.4 6.3 %shard_map.369 = (bf16[2,768,768]{2,1,0:T(8,128)(2,1)S(1)}, bf16[2,416,576]{2,1,0:T(8,128)(2,1)S(1)}, f32[12,208,208]{2,1,0:T(8,128)S(1)}, bf16[2,416,192]{2,1,0...) custom-call(s32[80]{0:T(128)S(1)} %get-tuple-element.202.tab, ...), custom_call_target="tpu_custom_call" | custom-call | flops 1 | bytes 1 | tf_op jit(solution)/shard_map/pallas_call | solution.py:445
  77.0 4.6 %shard_map.370 = (bf16[2,768,768]{2,1,0:T(8,128)(2,1)S(1)}, bf16[2,416,768]{2,1,0:T(8,128)(2,1)S(1)}, f32[2,416,768]{2,1,0:T(8,128)S(1)}, bf16[416,768]{1,0:T(8,128)(2,1)S(1)}, bf16[16,96,768]{2,1,0:T(8,128)(2,1)S(1)}) custom-call(s32[80]{0:T(128)S(1)} %get-tuple-element.203.tab, bf16[416,768]{1,0:T(8,128)(2,1)S(1)} %get-tuple-element.118.normed_two, ...), custom_call_target="tpu_custom_call" | custom-call | flops 99999997952 | bytes 1 | tf_op jit(solution)/shard_map/pallas_call | solution.py:445
  86.3 3.8 %shard_map.371 = (bf16[2,768,768]{2,1,0:T(8,128)(2,1)S(1)}, bf16[2,416,768]{2,1,0:T(8,128)(2,1)S(1)}, f32[2,416,768]{2,1,0:T(8,128)S(1)}, bf16[16,96,768]{2,1,0:T(8,128)(2,1)S(1)}) custom-call(s32[80]{0:T(128)S(1)} %get-tuple-element.203.tab, bf16[416,768]{1,0:T(8,128)(2,1)S(1)} %get-tuple-element.118.normed_two, ...), custom_call_target="tpu_custom_call" | custom-call | flops 1 | bytes 1 | tf_op jit(solution)/shard_map/pallas_call | solution.py:445
  90.0 3.2 %collective-permute-done.26.b3 = bf16[4,96,768]{2,1,0:T(8,128)(2,1)S(1)} collective-permute-done((bf16[4,96,768]{2,1,0:T(8,128)(2,1)S(1)}, bf16[4,96,768]{2,1,0:T(8,128)(2,1)S(1)}, u32[]{:S(2)}, u32[]{:S(2)}) %collective-permute-start.26) | collective-permute-done | bytes 589856 | tf_op jit(solution)/shard_map/ppermute | solution.py:481
  95.7 3.6 %shard_map.372 = (bf16[2,768,768]{2,1,0:T(8,128)(2,1)S(1)}, bf16[2,416,768]{2,1,0:T(8,128)(2,1)S(1)}, f32[2,1,768]{2,1,0:T(1,128)S(1)}, bf16[16,96,768]{2,1,0:T(8,128)(2,1)S(1)}) custom-call(s32[80]{0:T(128)S(1)} %get-tuple-element.201.tab, bf16[416,768]{1,0:T(8,128)(2,1)S(1)} %get-tuple-element.118.normed_two, ...), custom_call_target="tpu_custom_call" | custom-call | flops 99999997952 | bytes 1 | tf_op jit(solution)/shard_map/pallas_call | solution.py:445
  101.4 3.7 %shard_map.373 = (bf16[2,768,768]{2,1,0:T(8,128)(2,1)S(1)}, bf16[2,416,768]{2,1,0:T(8,128)(2,1)S(1)}, f32[2,1,768]{2,1,0:T(1,128)S(1)}, bf16[16,96,768]{2,1,0:T(8,128)(2,1)S(1)}) custom-call(s32[80]{0:T(128)S(1)} %get-tuple-element.201.tab, bf16[416,768]{1,0:T(8,128)(2,1)S(1)} %get-tuple-element.118.normed_two, ...), custom_call_target="tpu_custom_call" | custom-call | flops 99999997952 | bytes 1 | tf_op jit(solution)/shard_map/pallas_call | solution.py:445
  105.1 2.4 %add_convert_fusion.1 = bf16[8,96,768]{2,1,0:T(8,128)(2,1)S(1)} fusion(bf16[16,96,768]{2,1,0:T(8,128)(2,1)} %collective-permute-done.29, bf16[16,96,768]{2,1,0:T(8,128)(2,1)S(1)} %get-tuple-element.141), kind=kLoop, calls=%fused_computation.1 | loop fusion | flops 2359296 | bytes 3538944 | tf_op jit(solution)/shard_map/convert_element_type | solution.py:545
  107.9 5.6 %shard_map.374 = (bf16[394,768]{1,0:T(8,128)(2,1)}, f32[416,768]{1,0:T(8,128)S(1)}, bf16[416,768]{1,0:T(8,128)(2,1)S(1)}, f32[16,768]{1,0:T(8,128)S(1)}) custom-call(bf16[2,416,768]{2,1,0:T(8,128)(2,1)S(1)} %get-tuple-element.122.act_sib, bf16[2,416,768]{2,1,0:T(8,128)(2,1)S(1)} %get-tuple-element.123.act_own, ...), custom_call_target="tpu_custom_call" | custom-call | flops 1 | bytes 1 | tf_op jit(solution)/shard_map/pallas_call | solution.py:445
  113.5 8.8 %shard_map.375 = (bf16[16,96,768]{2,1,0:T(8,128)(2,1)S(1)}, f32[416,768]{1,0:T(8,128)S(1)}, f32[2,2,192]{2,1,0:T(2,128)S(1)}) custom-call(s32[80]{0:T(128)S(1)} %get-tuple-element.202.tab, bf16[2,768,768]{2,1,0:T(8,128)(2,1)S(1)} %get-tuple-element.150.w1, bf16[416,768]{1,0:T(8,128)(2,1)S(1)} %copy-done.1, bf16[2,416,576]{2,1,0:T(8,128)(2,1)S(1)} %get-tuple-element.151.qkv, ...), custom_call_target="tpu_custom_call" | custom-call | flops 1 | bytes 1 | tf_op jit(solution)/shard_map/pallas_call | solution.py:445
  126.0 9.1 %shard_map.376 = (bf16[16,96,768]{2,1,0:T(8,128)(2,1)S(1)}, f32[416,768]{1,0:T(8,128)S(1)}, f32[2,2,192]{2,1,0:T(2,128)S(1)}) custom-call(s32[80]{0:T(128)S(1)} %get-tuple-element.202.tab, bf16[2,768,768]{2,1,0:T(8,128)(2,1)S(1)} %get-tuple-element.145.w1, bf16[416,768]{1,0:T(8,128)(2,1)S(1)} %copy-done.1, bf16[2,416,576]{2,1,0:T(8,128)(2,1)S(1)} %get-tuple-element.146.qkv, ...), custom_call_target="tpu_custom_call" | custom-call | flops 99999997952 | bytes 1 | tf_op jit(solution)/shard_map/pallas_call | solution.py:445
  136.8 2.7 %shard_map.377 = (bf16[394,768]{1,0:T(8,128)(2,1)}, f32[24,768]{1,0:T(8,128)S(1)}) custom-call(s32[80]{0:T(128)S(1)} %get-tuple-element.202.tab, bf16[416,768]{1,0:T(8,128)(2,1)S(1)} %shard_map.366.tok, f32[416,1]{1,0:T(8,128)S(1)} %copy-done.5, f32[16,768]{1,0:T(8,128)S(1)} %copy-done.14, f32[416,768]{1,0:T(8,128)S(1)} %get-tuple-element.162.grad_one, ...), custom_call_target="tpu_custom_call" | custom-call | flops 1 | bytes 1 | tf_op jit(solution)/shard_map/pallas_call | solution.py:445
  139.5 2.6 %add_convert_fusion.3 = bf16[4,96,768]{2,1,0:T(8,128)(2,1)} fusion(bf16[16,96,768]{2,1,0:T(8,128)(2,1)} %collective-permute-done.29, bf16[8,96,768]{2,1,0:T(8,128)(2,1)S(1)} %collective-permute-done.38, bf16[16,96,768]{2,1,0:T(8,128)(2,1)S(1)} %get-tuple-element.141), kind=kLoop, calls=%fused_computation.3 | loop fusion | flops 1769472 | bytes 2359296 | tf_op jit(solution)/shard_map/convert_element_type | solution.py:545
  145.0 6.0 %collective-permute-done.33 = bf16[8,96,768]{2,1,0:T(8,128)(2,1)S(1)} collective-permute-done((bf16[8,96,768]{2,1,0:T(8,128)(2,1)S(1)}, bf16[8,96,768]{2,1,0:T(8,128)(2,1)S(1)}, u32[]{:S(2)}, u32[]{:S(2)}) %collective-permute-start.33) | collective-permute-done | bytes 1179680 | tf_op jit(solution)/shard_map/ppermute | solution.py:546
  153.8 9.4 %collective-permute-done.45 = f32[24,768]{1,0:T(8,128)S(1)} collective-permute-done((f32[24,768]{1,0:T(8,128)S(1)}, f32[24,768]{1,0:T(8,128)S(1)}, u32[]{:S(2)}, u32[]{:S(2)}) %collective-permute-start.45) | collective-permute-done | bytes 73760 | tf_op jit(solution)/shard_map/ppermute | solution.py:466
  172.7 2.5 %collective-permute-done.40 = bf16[2,96,768]{2,1,0:T(8,128)(2,1)S(1)} collective-permute-done((bf16[2,96,768]{2,1,0:T(8,128)(2,1)S(1)}, bf16[2,96,768]{2,1,0:T(8,128)(2,1)S(1)}, u32[]{:S(2)}, u32[]{:S(2)}) %collective-permute-start.40) | collective-permute-done | bytes 294944 | tf_op jit(solution)/shard_map/ppermute | solution.py:546
  186.7 5.5 %collective-permute-done.36 = bf16[1,96,768]{2,1,0:T(8,128)(2,1)S(1)} collective-permute-done((bf16[1,96,768]{2,1,0:T(8,128)(2,1)S(1)}, bf16[1,96,768]{2,1,0:T(8,128)(2,1)S(1)}, u32[]{:S(2)}, u32[]{:S(2)}) %collective-permute-start.36) | collective-permute-done | bytes 147488 | tf_op jit(solution)/shard_map/ppermute | solution.py:554
  (223 shorter events, 66.5 us)
Async XLA Ops:
  6.3 12.8 %collective-permute-start.1 = (bf16[1,104,768]{2,1,0:T(8,128)(2,1)S(1)}, bf16[1,104,768]{2,1,0:T(8,128)(2,1)S(1)}, u32[]{:S(2)}, u32[]{:S(2)}) collective-permute-start(bf16[1,104,768]{2,1,0:T(8,128)(2,1)S(1)} %bitcast.33), channel_id=1, source_target_pairs={{0,8},{1,17},{2,10},{3,19},{4,12},{5,21},{6,14},{7,23},{8,0},{9,25... | collective-permute-start | bytes 479240 | tf_op jit(solution)/shard_map/ppermute | solution.py:488
  20.7 21.0 %collective-permute-start.5 = (bf16[4,104,768]{2,1,0:T(8,128)(2,1)S(1)}, bf16[4,104,768]{2,1,0:T(8,128)(2,1)}, u32[]{:S(2)}, u32[]{:S(2)}) collective-permute-start(bf16[4,104,768]{2,1,0:T(8,128)(2,1)S(1)} %pad_maximum_fusion.b0), channel_id=1, source_target_pairs={{0,4},{1,3},{2,6},{3,1},{4,0},{5,7},{6,2},{7,5},{8,12},{9,11},{10,... | collective-permute-start | bytes 1916936 | tf_op jit(solution)/shard_map/ppermute | solution.py:481
  22.1 29.3 %collective-permute-start.12 = (bf16[4,96,768]{2,1,0:T(8,128)(2,1)S(1)}, bf16[4,96,768]{2,1,0:T(8,128)(2,1)}, u32[]{:S(2)}, u32[]{:S(2)}) collective-permute-start(bf16[4,96,768]{2,1,0:T(8,128)(2,1)S(1)} %pad_maximum_fusion.1.b0), channel_id=1, source_target_pairs={{0,8},{1,17},{2,10},{3,19},{4,12},{5,21},{6,14},{7,23},{8,0},{9,25... | collective-permute-start | bytes 1769480 | tf_op jit(solution)/shard_map/ppermute | solution.py:481
  28.4 23.9 %collective-permute-start.13 = (bf16[4,96,768]{2,1,0:T(8,128)(2,1)S(1)}, bf16[4,96,768]{2,1,0:T(8,128)(2,1)S(1)}, u32[]{:S(2)}, u32[]{:S(2)}) collective-permute-start(bf16[4,96,768]{2,1,0:T(8,128)(2,1)S(1)} %pad_maximum_fusion.1.b0), channel_id=1, source_target_pairs={{0,2},{1,9},{2,0},{3,11},{4,6},{5,13},{6,4},{7,15},{8,10},{9,1},{1... | collective-permute-start | bytes 1769480 | tf_op jit(solution)/shard_map/ppermute | solution.py:481
  28.5 13.5 %collective-permute-start.14 = (bf16[2,96,768]{2,1,0:T(8,128)(2,1)S(1)}, bf16[2,96,768]{2,1,0:T(8,128)(2,1)S(1)}, u32[]{:S(2)}, u32[]{:S(2)}) collective-permute-start(bf16[2,96,768]{2,1,0:T(8,128)(2,1)S(1)} %pad_maximum_fusion.4), channel_id=1, source_target_pairs={{0,16},{1,3},{2,18},{3,1},{4,20},{5,7},{6,22},{7,5},{8,24},{9,11},... | collective-permute-start | bytes 884744 | tf_op jit(solution)/shard_map/ppermute | solution.py:481
  28.8 38.6 %collective-permute-start.9 = (bf16[4,104,768]{2,1,0:T(8,128)(2,1)S(1)}, bf16[4,104,768]{2,1,0:T(8,128)(2,1)S(1)}, u32[]{:S(2)}, u32[]{:S(2)}) collective-permute-start(bf16[4,104,768]{2,1,0:T(8,128)(2,1)S(1)} %pad_maximum_fusion.b0), channel_id=1, source_target_pairs={{0,1},{1,0},{2,3},{3,2},{4,5},{5,4},{6,7},{7,6},{8,9},{9,8},{10,11... | collective-permute-start | bytes 1916936 | tf_op jit(solution)/shard_map/ppermute | solution.py:522
  41.7 12.5 %collective-permute-start.8 = (bf16[4,104,768]{2,1,0:T(8,128)(2,1)}, bf16[4,104,768]{2,1,0:T(8,128)(2,1)}, u32[]{:S(2)}, u32[]{:S(2)}) collective-permute-start(bf16[4,104,768]{2,1,0:T(8,128)(2,1)} %collective-permute-done.4.b1), channel_id=1, source_target_pairs={{0,4},{1,3},{2,6},{3,1},{4,0},{5,7},{6,2},{7,5},{8,12},{9,11},{10,... | collective-permute-start | bytes 1916936 | tf_op jit(solution)/shard_map/ppermute | solution.py:481
  42.0 25.5 %collective-permute-start.10 = (bf16[4,104,768]{2,1,0:T(8,128)(2,1)}, bf16[4,104,768]{2,1,0:T(8,128)(2,1)S(1)}, u32[]{:S(2)}, u32[]{:S(2)}) collective-permute-start(bf16[4,104,768]{2,1,0:T(8,128)(2,1)} %collective-permute-done.4.b1), channel_id=1, source_target_pairs={{0,1},{1,0},{2,3},{3,2},{4,5},{5,4},{6,7},{7,6},{8,9},{9,8},{10,11... | collective-permute-start | bytes 1916936 | tf_op jit(solution)/shard_map/ppermute | solution.py:522
  51.5 18.4 %collective-permute-start.11 = (bf16[4,104,768]{2,1,0:T(8,128)(2,1)}, bf16[4,104,768]{2,1,0:T(8,128)(2,1)S(1)}, u32[]{:S(2)}, u32[]{:S(2)}) collective-permute-start(bf16[4,104,768]{2,1,0:T(8,128)(2,1)} %collective-permute-done.5.b2), channel_id=1, source_target_pairs={{0,1},{1,0},{2,3},{3,2},{4,5},{5,4},{6,7},{7,6},{8,9},{9,8},{10,11... | collective-permute-start | bytes 1916936 | tf_op jit(solution)/shard_map/ppermute | solution.py:522
  54.2 15.9 %collective-permute-start.15 = (bf16[4,104,768]{2,1,0:T(8,128)(2,1)}, bf16[4,104,768]{2,1,0:T(8,128)(2,1)}, u32[]{:S(2)}, u32[]{:S(2)}) collective-permute-start(bf16[4,104,768]{2,1,0:T(8,128)(2,1)} %collective-permute-done.8.b3), channel_id=1, source_target_pairs={{0,1},{1,0},{2,3},{3,2},{4,5},{5,4},{6,7},{7,6},{8,9},{9,8},{10,11... | collective-permute-start | bytes 1916936 | tf_op jit(solution)/shard_map/ppermute | solution.py:522
  54.2 22.6 %collective-permute-start.16 = (bf16[4,96,768]{2,1,0:T(8,128)(2,1)}, bf16[4,96,768]{2,1,0:T(8,128)(2,1)}, u32[]{:S(2)}, u32[]{:S(2)}) collective-permute-start(bf16[4,96,768]{2,1,0:T(8,128)(2,1)} %collective-permute-done.12.b1), channel_id=1, source_target_pairs={{0,2},{1,9},{2,0},{3,11},{4,6},{5,13},{6,4},{7,15},{8,10},{9,1},{1... | collective-permute-start | bytes 1769480 | tf_op jit(solution)/shard_map/ppermute | solution.py:481
  67.4 16.8 %collective-permute-start.17 = (bf16[4,96,768]{2,1,0:T(8,128)(2,1)S(1)}, bf16[4,96,768]{2,1,0:T(8,128)(2,1)S(1)}, u32[]{:S(2)}, u32[]{:S(2)}) collective-permute-start(bf16[4,96,768]{2,1,0:T(8,128)(2,1)S(1)} %copy-done.12), channel_id=1, source_target_pairs={{0,1},{1,0},{2,3},{3,2},{4,5},{5,4},{6,7},{7,6},{8,9},{9,8},{10,11... | collective-permute-start | bytes 1769480 | tf_op jit(solution)/shard_map/ppermute | solution.py:522
  67.5 15.3 %collective-permute-start.22 = (bf16[4,96,768]{2,1,0:T(8,128)(2,1)S(1)}, bf16[4,96,768]{2,1,0:T(8,128)(2,1)S(1)}, u32[]{:S(2)}, u32[]{:S(2)}) collective-permute-start(bf16[4,96,768]{2,1,0:T(8,128)(2,1)S(1)} %pad_maximum_fusion.2.b0), channel_id=1, source_target_pairs={{0,8},{1,17},{2,10},{3,19},{4,12},{5,21},{6,14},{7,23},{8,0},{9,25... | collective-permute-start | bytes 1769480 | tf_op jit(solution)/shard_map/ppermute | solution.py:481
  69.9 14.5 %collective-permute-start.24 = (bf16[4,96,768]{2,1,0:T(8,128)(2,1)S(1)}, bf16[4,96,768]{2,1,0:T(8,128)(2,1)S(1)}, u32[]{:S(2)}, u32[]{:S(2)}) collective-permute-start(bf16[4,96,768]{2,1,0:T(8,128)(2,1)S(1)} %pad_maximum_fusion.2.b0), channel_id=1, source_target_pairs={{0,2},{1,5},{2,0},{3,7},{4,6},{5,1},{6,4},{7,3},{8,10},{9,13},{10,... | collective-permute-start | bytes 1769480 | tf_op jit(solution)/shard_map/ppermute | solution.py:481
  70.1 15.7 %collective-permute-start.18 = (bf16[4,96,768]{2,1,0:T(8,128)(2,1)}, bf16[4,96,768]{2,1,0:T(8,128)(2,1)S(1)}, u32[]{:S(2)}, u32[]{:S(2)}) collective-permute-start(bf16[4,96,768]{2,1,0:T(8,128)(2,1)} %collective-permute-done.12.b1), channel_id=1, source_target_pairs={{0,1},{1,0},{2,3},{3,2},{4,5},{5,4},{6,7},{7,6},{8,9},{9,8},{10,11... | collective-permute-start | bytes 1769480 | tf_op jit(solution)/shard_map/ppermute | solution.py:522
  100.1 23.6 %collective-permute-start.30 = (bf16[8,96,768]{2,1,0:T(8,128)(2,1)S(1)}, bf16[8,96,768]{2,1,0:T(8,128)(2,1)}, u32[]{:S(2)}, u32[]{:S(2)}) collective-permute-start(bf16[8,96,768]{2,1,0:T(8,128)(2,1)S(1)} %add_convert_fusion.2), channel_id=1, source_target_pairs={{0,8},{1,3},{2,10},{3,1},{4,12},{5,7},{6,14},{7,5},{8,0},{9,11},{1... | collective-permute-start | bytes 3538952 | tf_op jit(solution)/shard_map/ppermute | solution.py:546
  107.6 31.9 %collective-permute-start.38 = (bf16[8,96,768]{2,1,0:T(8,128)(2,1)S(1)}, bf16[8,96,768]{2,1,0:T(8,128)(2,1)S(1)}, u32[]{:S(2)}, u32[]{:S(2)}) collective-permute-start(bf16[8,96,768]{2,1,0:T(8,128)(2,1)S(1)} %add_convert_fusion.1), channel_id=1, source_target_pairs={{0,4},{1,5},{2,6},{3,7},{4,0},{5,1},{6,2},{7,3},{8,12},{9,13},{10,... | collective-permute-start | bytes 3538952 | tf_op jit(solution)/shard_map/ppermute | solution.py:546
  122.3 12.8 %collective-permute-start.32 = (bf16[16,96,768]{2,1,0:T(8,128)(2,1)S(1)}, bf16[16,96,768]{2,1,0:T(8,128)(2,1)S(1)}, u32[]{:S(2)}, u32[]{:S(2)}) collective-permute-start(bf16[16,96,768]{2,1,0:T(8,128)(2,1)S(1)} %get-tuple-element.161), channel_id=1, source_target_pairs={{0,1},{1,0},{2,3},{3,2},{4,5},{5,4},{6,7},{7,6},{8,9},{9,8},{10,11... | collective-permute-start | bytes 7077896 | tf_op jit(solution)/shard_map/ppermute | solution.py:532
  135.5 15.5 %collective-permute-start.33 = (bf16[8,96,768]{2,1,0:T(8,128)(2,1)S(1)}, bf16[8,96,768]{2,1,0:T(8,128)(2,1)S(1)}, u32[]{:S(2)}, u32[]{:S(2)}) collective-permute-start(bf16[8,96,768]{2,1,0:T(8,128)(2,1)S(1)} %add_convert_fusion), channel_id=1, source_target_pairs={{0,2},{1,5},{2,0},{3,7},{4,6},{5,1},{6,4},{7,3},{8,10},{9,13},{10,... | collective-permute-start | bytes 3538952 | tf_op jit(solution)/shard_map/ppermute | solution.py:546
  139.5 12.8 %collective-permute-start.44 = (f32[24,768]{1,0:T(8,128)S(1)}, f32[24,768]{1,0:T(8,128)S(1)}, u32[]{:S(2)}, u32[]{:S(2)}) collective-permute-start(f32[24,768]{1,0:T(8,128)S(1)} %get-tuple-element.182), channel_id=1, source_target_pairs={{0,1},{1,0},{2,3},{3,2},{4,5},{5,4},{6,7},{7,6},{8,9},{9,8},{10,11... | collective-permute-start | bytes 221192 | tf_op jit(solution)/shard_map/ppermute | solution.py:466
  142.1 21.9 %collective-permute-start.39 = (bf16[4,96,768]{2,1,0:T(8,128)(2,1)}, bf16[4,96,768]{2,1,0:T(8,128)(2,1)}, u32[]{:S(2)}, u32[]{:S(2)}) collective-permute-start(bf16[4,96,768]{2,1,0:T(8,128)(2,1)} %add_convert_fusion.3), channel_id=1, source_target_pairs={{0,8},{1,9},{2,10},{3,11},{4,12},{5,13},{6,14},{7,15},{8,0},{9,1},... | collective-permute-start | bytes 1769480 | tf_op jit(solution)/shard_map/ppermute | solution.py:546
  144.1 19.9 %collective-permute-start.42 = (bf16[2,96,768]{2,1,0:T(8,128)(2,1)S(1)}, bf16[2,96,768]{2,1,0:T(8,128)(2,1)}, u32[]{:S(2)}, u32[]{:S(2)}) collective-permute-start(bf16[2,96,768]{2,1,0:T(8,128)(2,1)S(1)} %add_convert_fusion.6), channel_id=1, source_target_pairs={{0,16},{1,17},{2,18},{3,19},{4,20},{5,21},{6,22},{7,23},{8,24},{9,... | collective-permute-start | bytes 884744 | tf_op jit(solution)/shard_map/ppermute | solution.py:546
  152.2 17.4 %collective-permute-start.34 = (bf16[4,96,768]{2,1,0:T(8,128)(2,1)}, bf16[4,96,768]{2,1,0:T(8,128)(2,1)S(1)}, u32[]{:S(2)}, u32[]{:S(2)}) collective-permute-start(bf16[4,96,768]{2,1,0:T(8,128)(2,1)} %add_convert_fusion.4), channel_id=1, source_target_pairs={{0,4},{1,3},{2,6},{3,1},{4,0},{5,7},{6,2},{7,5},{8,12},{9,11},{10,... | collective-permute-start | bytes 1769480 | tf_op jit(solution)/shard_map/ppermute | solution.py:546
  179.5 12.8 %collective-permute-start.36 = (bf16[1,96,768]{2,1,0:T(8,128)(2,1)S(1)}, bf16[1,96,768]{2,1,0:T(8,128)(2,1)S(1)}, u32[]{:S(2)}, u32[]{:S(2)}) collective-permute-start(bf16[1,96,768]{2,1,0:T(8,128)(2,1)S(1)} %get-tuple-element.199), channel_id=1, source_target_pairs={{0,8},{1,17},{2,10},{3,19},{4,12},{5,21},{6,14},{7,23},{8,0},{9,25... | collective-permute-start | bytes 442376 | tf_op jit(solution)/shard_map/ppermute | solution.py:554
  (74 other events, 773.4 us)

commit v7 on v6

--- a/solution.py
+++ b/solution.py
@@ -703,7 +703,7 @@
             shape((16, D), F32), shape((GROUPS, 1, D), F32), row_f32, row_low,
             group_bias, group_bias, weights, *heads,
         ),
-        flops=SHORT,
+        flops=LONG,
     )
     w1_sib, *heads_sib, attn, mid, normed_two = call(
         functools.partial(attend_sib_kernel, imgs),

time: 197 us -> 205 us (1.041)
  waiting for transfers between devices: 33.1 us -> 52.1 us
  starting transfers between devices: 71.5 us -> 61.1 us
  local copies, waits for them, and re-layouts: 7.49 us -> 4.54 us
    ppermute x13, waiting for transfers between devices: 4.76 us -> 23.9 us  [send(): return lax.ppermute(values, AXES, pairs_of(self.orders, level))]
    ppermute x12, starting transfers between devices: 28 us -> 19 us  [sib(): return tuple((lax.ppermute(values, AXES, CORE_PAIRS) for values in own))]
    unnamed x98 -> x96, local copies, waits for them, and re-layouts: 5.82 us -> 3.45 us
    ppermute x10, starting transfers between devices: 9.3 us -> 7.1 us  [step(): lax.ppermute(sent, AXES, pairs_of(self.orders, self.level))]
  transfers between devices with their start and end apart: 49 -> 49, of which waited for: 9 -> 13; matrix products, arithmetic and copies ran while one was open for 13% -> 13% of each run, Pallas kernels for 29% -> 28%
where the time goes in v7:
time: 205 us; the launch traced here: 204 us
  starting transfers between devices  61.1 us (30%)
  Pallas kernels  57.2 us (28%)
  waiting for transfers between devices  52.1 us (25%)
  other arithmetic  27.5 us (13%)
  local copies, waits for them, and re-layouts  4.54 us (2%)
    pallas_call x14, Pallas kernels, call(): pl.pallas_call(kernel, out_shape=outs, in_specs=[SMEM] * table + [VMEM] *...  57.2 us
    ppermute x13, waiting for transfers between devices, send(): return lax.ppermute(values, AXES, pairs_of(self.orders, level))  23.9 us
    ppermute x12, starting transfers between devices, sib(): return tuple((lax.ppermute(values, AXES, CORE_PAIRS) for values in own))  19 us
    ppermute x13, starting transfers between devices, send(): return lax.ppermute(values, AXES, pairs_of(self.orders, level))  18.4 us
    convert_element_type x10, other arithmetic, step(): sent = self.total(size, 2 * size).astype(BF16)  12.6 us
    ppermute x5, waiting for transfers between devices, send_across(): return lax.ppermute(values, AXES, [(dev, dev ^ mask) for dev in range(32)])  8.82 us
    ppermute x10, waiting for transfers between devices, step(): lax.ppermute(sent, AXES, pairs_of(self.orders, self.level))  7.76 us
    ppermute x10, starting transfers between devices, step(): lax.ppermute(sent, AXES, pairs_of(self.orders, self.level))  7.1 us
  transfers between devices with their start and end apart: 49, of which 13 were waited for; matrix products, arithmetic and copies ran while one was open for 13% of the time, Pallas kernels for 28%

profile of v7, /device:TPU:1, one launch (start us, length us, event | category | flops | bytes accessed | tf_op | source)
XLA Modules:
  0.0 203.8 jit_solution(17225741339316158266)
XLA Ops:
  15.2 3.9 %collective-permute-done.1 = bf16[1,104,768]{2,1,0:T(8,128)(2,1)S(1)} collective-permute-done((bf16[1,104,768]{2,1,0:T(8,128)(2,1)S(1)}, bf16[1,104,768]{2,1,0:T(8,128)(2,1)S(1)}, u32[]{:S(2)}, u32[]{:S(2)}) %collective-permute-start.1) | collective-permute-done | bytes 159776 | tf_op jit(solution)/shard_map/ppermute | solution.py:488
  22.9 6.3 %collective-permute-start.12 = (bf16[4,96,768]{2,1,0:T(8,128)(2,1)S(1)}, bf16[4,96,768]{2,1,0:T(8,128)(2,1)}, u32[]{:S(2)}, u32[]{:S(2)}) collective-permute-start(bf16[4,96,768]{2,1,0:T(8,128)(2,1)S(1)} %pad_maximum_fusion.1.b0), channel_id=1, source_target_pairs={{0,8},{1,17},{2,10},{3,19},{4,12},{5,21},{6,14},{7,23},{8,0},{9,25... | collective-permute-start | bytes 1769480 | tf_op jit(solution)/shard_map/ppermute | solution.py:481
  29.7 7.8 %collective-permute-done.14 = bf16[2,96,768]{2,1,0:T(8,128)(2,1)S(1)} collective-permute-done((bf16[2,96,768]{2,1,0:T(8,128)(2,1)S(1)}, bf16[2,96,768]{2,1,0:T(8,128)(2,1)S(1)}, u32[]{:S(2)}, u32[]{:S(2)}) %collective-permute-start.14) | collective-permute-done | bytes 294944 | tf_op jit(solution)/shard_map/ppermute | solution.py:481
  37.5 14.8 %collective-permute-start.9 = (bf16[4,104,768]{2,1,0:T(8,128)(2,1)}, bf16[4,104,768]{2,1,0:T(8,128)(2,1)}, u32[]{:S(2)}, u32[]{:S(2)}) collective-permute-start(bf16[4,104,768]{2,1,0:T(8,128)(2,1)} %pad_maximum_fusion.b0), channel_id=1, source_target_pairs={{0,1},{1,0},{2,3},{3,2},{4,5},{5,4},{6,7},{7,6},{8,9},{9,8},{10,11... | collective-permute-start | bytes 1916936 | tf_op jit(solution)/shard_map/ppermute | solution.py:522
  54.0 2.7 %collective-permute-start.16 = (bf16[4,96,768]{2,1,0:T(8,128)(2,1)}, bf16[4,96,768]{2,1,0:T(8,128)(2,1)}, u32[]{:S(2)}, u32[]{:S(2)}) collective-permute-start(bf16[4,96,768]{2,1,0:T(8,128)(2,1)} %collective-permute-done.12.b1), channel_id=1, source_target_pairs={{0,2},{1,9},{2,0},{3,11},{4,6},{5,13},{6,4},{7,15},{8,10},{9,1},{1... | collective-permute-start | bytes 1769480 | tf_op jit(solution)/shard_map/ppermute | solution.py:481
  56.9 11.5 %collective-permute-done.8.b3 = bf16[4,104,768]{2,1,0:T(8,128)(2,1)S(1)} collective-permute-done((bf16[4,104,768]{2,1,0:T(8,128)(2,1)}, bf16[4,104,768]{2,1,0:T(8,128)(2,1)S(1)}, u32[]{:S(2)}, u32[]{:S(2)}) %collective-permute-start.8) | collective-permute-done | bytes 639008 | tf_op jit(solution)/shard_map/ppermute | solution.py:481
  68.4 7.0 %shard_map.367 = (f32[16,768]{1,0:T(8,128)S(1)}, f32[4,1,768]{2,1,0:T(1,128)S(1)}, f32[416,768]{1,0:T(8,128)S(1)}, bf16[416,768]{1,0:T(8,128)(2,1)S(1)}, f32[4,1...) custom-call(s32[80]{0:T(128)S(1)} %get-tuple-element.202.tab, ...), custom_call_target="tpu_custom_call" | custom-call | flops 99999997952 | bytes 1 | tf_op jit(solution)/shard_map/pallas_call | solution.py:445
  75.9 3.1 %collective-permute-start.22 = (bf16[4,96,768]{2,1,0:T(8,128)(2,1)S(1)}, bf16[4,96,768]{2,1,0:T(8,128)(2,1)S(1)}, u32[]{:S(2)}, u32[]{:S(2)}) collective-permute-start(bf16[4,96,768]{2,1,0:T(8,128)(2,1)S(1)} %copy-done.12), channel_id=1, source_target_pairs={{0,8},{1,17},{2,10},{3,19},{4,12},{5,21},{6,14},{7,23},{8,0},{9,25... | collective-permute-start | bytes 1769480 | tf_op jit(solution)/shard_map/ppermute | solution.py:481
  79.2 6.7 %shard_map.369 = (bf16[2,768,768]{2,1,0:T(8,128)(2,1)S(1)}, bf16[2,416,576]{2,1,0:T(8,128)(2,1)S(1)}, f32[12,208,208]{2,1,0:T(8,128)S(1)}, bf16[2,416,192]{2,1,0...) custom-call(s32[80]{0:T(128)S(1)} %get-tuple-element.202.tab, ...), custom_call_target="tpu_custom_call" | custom-call | flops 1 | bytes 1 | tf_op jit(solution)/shard_map/pallas_call | solution.py:445
  86.4 4.6 %shard_map.370 = (bf16[2,768,768]{2,1,0:T(8,128)(2,1)S(1)}, bf16[2,416,768]{2,1,0:T(8,128)(2,1)S(1)}, f32[2,416,768]{2,1,0:T(8,128)S(1)}, bf16[416,768]{1,0:T(8,128)(2,1)S(1)}, bf16[16,96,768]{2,1,0:T(8,128)(2,1)S(1)}) custom-call(s32[80]{0:T(128)S(1)} %get-tuple-element.203.tab, bf16[416,768]{1,0:T(8,128)(2,1)S(1)} %get-tuple-element.118.normed_two, ...), custom_call_target="tpu_custom_call" | custom-call | flops 99999997952 | bytes 1 | tf_op jit(solution)/shard_map/pallas_call | solution.py:445
  95.0 3.8 %shard_map.371 = (bf16[2,768,768]{2,1,0:T(8,128)(2,1)S(1)}, bf16[2,416,768]{2,1,0:T(8,128)(2,1)S(1)}, f32[2,416,768]{2,1,0:T(8,128)S(1)}, bf16[16,96,768]{2,1,0:T(8,128)(2,1)S(1)}) custom-call(s32[80]{0:T(128)S(1)} %get-tuple-element.203.tab, bf16[416,768]{1,0:T(8,128)(2,1)S(1)} %get-tuple-element.118.normed_two, ...), custom_call_target="tpu_custom_call" | custom-call | flops 1 | bytes 1 | tf_op jit(solution)/shard_map/pallas_call | solution.py:445
  98.8 3.4 %collective-permute-done.26.b3 = bf16[4,96,768]{2,1,0:T(8,128)(2,1)S(1)} collective-permute-done((bf16[4,96,768]{2,1,0:T(8,128)(2,1)S(1)}, bf16[4,96,768]{2,1,0:T(8,128)(2,1)S(1)}, u32[]{:S(2)}, u32[]{:S(2)}) %collective-permute-start.26) | collective-permute-done | bytes 589856 | tf_op jit(solution)/shard_map/ppermute | solution.py:481
  104.7 3.6 %shard_map.372 = (bf16[2,768,768]{2,1,0:T(8,128)(2,1)S(1)}, bf16[2,416,768]{2,1,0:T(8,128)(2,1)S(1)}, f32[2,1,768]{2,1,0:T(1,128)S(1)}, bf16[16,96,768]{2,1,0:T(8,128)(2,1)S(1)}) custom-call(s32[80]{0:T(128)S(1)} %get-tuple-element.201.tab, bf16[416,768]{1,0:T(8,128)(2,1)S(1)} %get-tuple-element.118.normed_two, ...), custom_call_target="tpu_custom_call" | custom-call | flops 99999997952 | bytes 1 | tf_op jit(solution)/shard_map/pallas_call | solution.py:445
  109.1 3.7 %shard_map.373 = (bf16[2,768,768]{2,1,0:T(8,128)(2,1)S(1)}, bf16[2,416,768]{2,1,0:T(8,128)(2,1)S(1)}, f32[2,1,768]{2,1,0:T(1,128)S(1)}, bf16[16,96,768]{2,1,0:T(8,128)(2,1)S(1)}) custom-call(s32[80]{0:T(128)S(1)} %get-tuple-element.201.tab, bf16[416,768]{1,0:T(8,128)(2,1)S(1)} %get-tuple-element.118.normed_two, ...), custom_call_target="tpu_custom_call" | custom-call | flops 99999997952 | bytes 1 | tf_op jit(solution)/shard_map/pallas_call | solution.py:445
  113.0 2.5 %add_convert_fusion.1 = bf16[8,96,768]{2,1,0:T(8,128)(2,1)S(1)} fusion(bf16[16,96,768]{2,1,0:T(8,128)(2,1)} %collective-permute-done.29, bf16[16,96,768]{2,1,0:T(8,128)(2,1)S(1)} %get-tuple-element.141), kind=kLoop, calls=%fused_computation.1 | loop fusion | flops 2359296 | bytes 3538944 | tf_op jit(solution)/shard_map/convert_element_type | solution.py:545
  115.6 5.7 %shard_map.374 = (bf16[394,768]{1,0:T(8,128)(2,1)}, f32[416,768]{1,0:T(8,128)S(1)}, bf16[416,768]{1,0:T(8,128)(2,1)S(1)}, f32[16,768]{1,0:T(8,128)S(1)}) custom-call(bf16[2,416,768]{2,1,0:T(8,128)(2,1)S(1)} %get-tuple-element.122.act_sib, bf16[2,416,768]{2,1,0:T(8,128)(2,1)S(1)} %get-tuple-element.123.act_own, ...), custom_call_target="tpu_custom_call" | custom-call | flops 1 | bytes 1 | tf_op jit(solution)/shard_map/pallas_call | solution.py:445
  121.4 8.8 %shard_map.375 = (bf16[16,96,768]{2,1,0:T(8,128)(2,1)S(1)}, f32[416,768]{1,0:T(8,128)S(1)}, f32[2,2,192]{2,1,0:T(2,128)S(1)}) custom-call(s32[80]{0:T(128)S(1)} %copy-done.26, bf16[2,768,768]{2,1,0:T(8,128)(2,1)S(1)} %get-tuple-element.150.w1, bf16[416,768]{1,0:T(8,128)(2,1)S(1)} %copy-done.1, bf16[2,416,576]{2,1,0:T(8,128)(2,1)S(1)} %get-tuple-element.151.qkv, ...), custom_call_target="tpu_custom_call" | custom-call | flops 1 | bytes 1 | tf_op jit(solution)/shard_map/pallas_call | solution.py:445
  132.7 9.1 %shard_map.376 = (bf16[16,96,768]{2,1,0:T(8,128)(2,1)S(1)}, f32[416,768]{1,0:T(8,128)S(1)}, f32[2,2,192]{2,1,0:T(2,128)S(1)}) custom-call(s32[80]{0:T(128)S(1)} %copy-done.26, bf16[2,768,768]{2,1,0:T(8,128)(2,1)S(1)} %get-tuple-element.145.w1, bf16[416,768]{1,0:T(8,128)(2,1)S(1)} %copy-done.1, bf16[2,416,576]{2,1,0:T(8,128)(2,1)S(1)} %get-tuple-element.146.qkv, ...), custom_call_target="tpu_custom_call" | custom-call | flops 99999997952 | bytes 1 | tf_op jit(solution)/shard_map/pallas_call | solution.py:445
  144.0 2.7 %shard_map.377 = (bf16[394,768]{1,0:T(8,128)(2,1)}, f32[24,768]{1,0:T(8,128)S(1)}) custom-call(s32[80]{0:T(128)S(1)} %copy-done.26, bf16[416,768]{1,0:T(8,128)(2,1)S(1)} %copy-done.9, f32[416,1]{1,0:T(8,128)S(1)} %copy-done.7, f32[16,768]{1,0:T(8,128)S(1)} %copy-done.16, f32[416,768]{1,0:T(8,128)S(1)} %get-tuple-element.162.grad_one, ...), custom_call_target="tpu_custom_call" | custom-call | flops 1 | bytes 1 | tf_op jit(solution)/shard_map/pallas_call | solution.py:445
  147.0 2.5 %add_convert_fusion.3 = bf16[4,96,768]{2,1,0:T(8,128)(2,1)} fusion(bf16[16,96,768]{2,1,0:T(8,128)(2,1)} %collective-permute-done.29, bf16[8,96,768]{2,1,0:T(8,128)(2,1)S(1)} %collective-permute-done.38, bf16[16,96,768]{2,1,0:T(8,128)(2,1)S(1)} %get-tuple-element.141), kind=kLoop, calls=%fused_computation.3 | loop fusion | flops 1769472 | bytes 2359296 | tf_op jit(solution)/shard_map/convert_element_type | solution.py:545
  153.1 4.8 %collective-permute-done.33 = bf16[8,96,768]{2,1,0:T(8,128)(2,1)S(1)} collective-permute-done((bf16[8,96,768]{2,1,0:T(8,128)(2,1)S(1)}, bf16[8,96,768]{2,1,0:T(8,128)(2,1)S(1)}, u32[]{:S(2)}, u32[]{:S(2)}) %collective-permute-start.33) | collective-permute-done | bytes 1179680 | tf_op jit(solution)/shard_map/ppermute | solution.py:546
  161.1 8.8 %collective-permute-done.45 = f32[24,768]{1,0:T(8,128)} collective-permute-done((f32[24,768]{1,0:T(8,128)}, f32[24,768]{1,0:T(8,128)}, u32[]{:S(2)}, u32[]{:S(2)}) %collective-permute-start.45) | collective-permute-done | bytes 73760 | tf_op jit(solution)/shard_map/ppermute | solution.py:466
  180.7 2.9 %collective-permute-done.40 = bf16[2,96,768]{2,1,0:T(8,128)(2,1)S(1)} collective-permute-done((bf16[2,96,768]{2,1,0:T(8,128)(2,1)S(1)}, bf16[2,96,768]{2,1,0:T(8,128)(2,1)S(1)}, u32[]{:S(2)}, u32[]{:S(2)}) %collective-permute-start.40) | collective-permute-done | bytes 294944 | tf_op jit(solution)/shard_map/ppermute | solution.py:546
  196.5 3.4 %collective-permute-done.36 = bf16[1,96,768]{2,1,0:T(8,128)(2,1)S(1)} collective-permute-done((bf16[1,96,768]{2,1,0:T(8,128)(2,1)S(1)}, bf16[1,96,768]{2,1,0:T(8,128)(2,1)S(1)}, u32[]{:S(2)}, u32[]{:S(2)}) %collective-permute-start.36) | collective-permute-done | bytes 147488 | tf_op jit(solution)/shard_map/ppermute | solution.py:554
  (221 shorter events, 68.2 us)
Async XLA Ops:
  6.3 12.8 %collective-permute-start.1 = (bf16[1,104,768]{2,1,0:T(8,128)(2,1)S(1)}, bf16[1,104,768]{2,1,0:T(8,128)(2,1)S(1)}, u32[]{:S(2)}, u32[]{:S(2)}) collective-permute-start(bf16[1,104,768]{2,1,0:T(8,128)(2,1)S(1)} %bitcast.33), channel_id=1, source_target_pairs={{0,8},{1,17},{2,10},{3,19},{4,12},{5,21},{6,14},{7,23},{8,0},{9,25... | collective-permute-start | bytes 479240 | tf_op jit(solution)/shard_map/ppermute | solution.py:488
  20.0 33.2 %collective-permute-start.4 = (bf16[4,104,768]{2,1,0:T(8,128)(2,1)}, bf16[4,104,768]{2,1,0:T(8,128)(2,1)}, u32[]{:S(2)}, u32[]{:S(2)}) collective-permute-start(bf16[4,104,768]{2,1,0:T(8,128)(2,1)} %pad_maximum_fusion.b0), channel_id=1, source_target_pairs={{0,2},{1,5},{2,0},{3,7},{4,6},{5,1},{6,4},{7,3},{8,10},{9,13},{10,... | collective-permute-start | bytes 1916936 | tf_op jit(solution)/shard_map/ppermute | solution.py:481
  21.5 31.7 %collective-permute-start.5 = (bf16[4,104,768]{2,1,0:T(8,128)(2,1)}, bf16[4,104,768]{2,1,0:T(8,128)(2,1)}, u32[]{:S(2)}, u32[]{:S(2)}) collective-permute-start(bf16[4,104,768]{2,1,0:T(8,128)(2,1)} %pad_maximum_fusion.b0), channel_id=1, source_target_pairs={{0,4},{1,3},{2,6},{3,1},{4,0},{5,7},{6,2},{7,5},{8,12},{9,11},{10,... | collective-permute-start | bytes 1916936 | tf_op jit(solution)/shard_map/ppermute | solution.py:481
  22.9 30.7 %collective-permute-start.12 = (bf16[4,96,768]{2,1,0:T(8,128)(2,1)S(1)}, bf16[4,96,768]{2,1,0:T(8,128)(2,1)}, u32[]{:S(2)}, u32[]{:S(2)}) collective-permute-start(bf16[4,96,768]{2,1,0:T(8,128)(2,1)S(1)} %pad_maximum_fusion.1.b0), channel_id=1, source_target_pairs={{0,8},{1,17},{2,10},{3,19},{4,12},{5,21},{6,14},{7,23},{8,0},{9,25... | collective-permute-start | bytes 1769480 | tf_op jit(solution)/shard_map/ppermute | solution.py:481
  29.2 24.8 %collective-permute-start.13 = (bf16[4,96,768]{2,1,0:T(8,128)(2,1)S(1)}, bf16[4,96,768]{2,1,0:T(8,128)(2,1)S(1)}, u32[]{:S(2)}, u32[]{:S(2)}) collective-permute-start(bf16[4,96,768]{2,1,0:T(8,128)(2,1)S(1)} %pad_maximum_fusion.1.b0), channel_id=1, source_target_pairs={{0,2},{1,9},{2,0},{3,11},{4,6},{5,13},{6,4},{7,15},{8,10},{9,1},{1... | collective-permute-start | bytes 1769480 | tf_op jit(solution)/shard_map/ppermute | solution.py:481
  37.5 37.9 %collective-permute-start.9 = (bf16[4,104,768]{2,1,0:T(8,128)(2,1)}, bf16[4,104,768]{2,1,0:T(8,128)(2,1)}, u32[]{:S(2)}, u32[]{:S(2)}) collective-permute-start(bf16[4,104,768]{2,1,0:T(8,128)(2,1)} %pad_maximum_fusion.b0), channel_id=1, source_target_pairs={{0,1},{1,0},{2,3},{3,2},{4,5},{5,4},{6,7},{7,6},{8,9},{9,8},{10,11... | collective-permute-start | bytes 1916936 | tf_op jit(solution)/shard_map/ppermute | solution.py:522
  53.2 15.2 %collective-permute-start.8 = (bf16[4,104,768]{2,1,0:T(8,128)(2,1)}, bf16[4,104,768]{2,1,0:T(8,128)(2,1)S(1)}, u32[]{:S(2)}, u32[]{:S(2)}) collective-permute-start(bf16[4,104,768]{2,1,0:T(8,128)(2,1)} %collective-permute-done.4.b1), channel_id=1, source_target_pairs={{0,4},{1,3},{2,6},{3,1},{4,0},{5,7},{6,2},{7,5},{8,12},{9,11},{10,... | collective-permute-start | bytes 1916936 | tf_op jit(solution)/shard_map/ppermute | solution.py:481
  53.4 22.5 %collective-permute-start.10 = (bf16[4,104,768]{2,1,0:T(8,128)(2,1)}, bf16[4,104,768]{2,1,0:T(8,128)(2,1)}, u32[]{:S(2)}, u32[]{:S(2)}) collective-permute-start(bf16[4,104,768]{2,1,0:T(8,128)(2,1)} %collective-permute-done.4.b1), channel_id=1, source_target_pairs={{0,1},{1,0},{2,3},{3,2},{4,5},{5,4},{6,7},{7,6},{8,9},{9,8},{10,11... | collective-permute-start | bytes 1916936 | tf_op jit(solution)/shard_map/ppermute | solution.py:522
  53.7 25.4 %collective-permute-start.11 = (bf16[4,104,768]{2,1,0:T(8,128)(2,1)}, bf16[4,104,768]{2,1,0:T(8,128)(2,1)}, u32[]{:S(2)}, u32[]{:S(2)}) collective-permute-start(bf16[4,104,768]{2,1,0:T(8,128)(2,1)} %collective-permute-done.5.b2), channel_id=1, source_target_pairs={{0,1},{1,0},{2,3},{3,2},{4,5},{5,4},{6,7},{7,6},{8,9},{9,8},{10,11... | collective-permute-start | bytes 1916936 | tf_op jit(solution)/shard_map/ppermute | solution.py:522
  54.0 31.9 %collective-permute-start.16 = (bf16[4,96,768]{2,1,0:T(8,128)(2,1)}, bf16[4,96,768]{2,1,0:T(8,128)(2,1)}, u32[]{:S(2)}, u32[]{:S(2)}) collective-permute-start(bf16[4,96,768]{2,1,0:T(8,128)(2,1)} %collective-permute-done.12.b1), channel_id=1, source_target_pairs={{0,2},{1,9},{2,0},{3,11},{4,6},{5,13},{6,4},{7,15},{8,10},{9,1},{1... | collective-permute-start | bytes 1769480 | tf_op jit(solution)/shard_map/ppermute | solution.py:481
  75.4 17.8 %collective-permute-start.17 = (bf16[4,96,768]{2,1,0:T(8,128)(2,1)S(1)}, bf16[4,96,768]{2,1,0:T(8,128)(2,1)S(1)}, u32[]{:S(2)}, u32[]{:S(2)}) collective-permute-start(bf16[4,96,768]{2,1,0:T(8,128)(2,1)S(1)} %copy-done.14), channel_id=1, source_target_pairs={{0,1},{1,0},{2,3},{3,2},{4,5},{5,4},{6,7},{7,6},{8,9},{9,8},{10,11... | collective-permute-start | bytes 1769480 | tf_op jit(solution)/shard_map/ppermute | solution.py:522
  75.9 16.1 %collective-permute-start.22 = (bf16[4,96,768]{2,1,0:T(8,128)(2,1)S(1)}, bf16[4,96,768]{2,1,0:T(8,128)(2,1)S(1)}, u32[]{:S(2)}, u32[]{:S(2)}) collective-permute-start(bf16[4,96,768]{2,1,0:T(8,128)(2,1)S(1)} %copy-done.12), channel_id=1, source_target_pairs={{0,8},{1,17},{2,10},{3,19},{4,12},{5,21},{6,14},{7,23},{8,0},{9,25... | collective-permute-start | bytes 1769480 | tf_op jit(solution)/shard_map/ppermute | solution.py:481
  79.1 14.2 %collective-permute-start.24 = (bf16[4,96,768]{2,1,0:T(8,128)(2,1)S(1)}, bf16[4,96,768]{2,1,0:T(8,128)(2,1)S(1)}, u32[]{:S(2)}, u32[]{:S(2)}) collective-permute-start(bf16[4,96,768]{2,1,0:T(8,128)(2,1)S(1)} %copy-done.12), channel_id=1, source_target_pairs={{0,2},{1,5},{2,0},{3,7},{4,6},{5,1},{6,4},{7,3},{8,10},{9,13},{10,... | collective-permute-start | bytes 1769480 | tf_op jit(solution)/shard_map/ppermute | solution.py:481
  79.1 14.2 %collective-permute-start.18 = (bf16[4,96,768]{2,1,0:T(8,128)(2,1)}, bf16[4,96,768]{2,1,0:T(8,128)(2,1)S(1)}, u32[]{:S(2)}, u32[]{:S(2)}) collective-permute-start(bf16[4,96,768]{2,1,0:T(8,128)(2,1)} %collective-permute-done.12.b1), channel_id=1, source_target_pairs={{0,1},{1,0},{2,3},{3,2},{4,5},{5,4},{6,7},{7,6},{8,9},{9,8},{10,11... | collective-permute-start | bytes 1769480 | tf_op jit(solution)/shard_map/ppermute | solution.py:522
  109.1 23.3 %collective-permute-start.30 = (bf16[8,96,768]{2,1,0:T(8,128)(2,1)S(1)}, bf16[8,96,768]{2,1,0:T(8,128)(2,1)S(1)}, u32[]{:S(2)}, u32[]{:S(2)}) collective-permute-start(bf16[8,96,768]{2,1,0:T(8,128)(2,1)S(1)} %add_convert_fusion.2), channel_id=1, source_target_pairs={{0,8},{1,3},{2,10},{3,1},{4,12},{5,7},{6,14},{7,5},{8,0},{9,11},{1... | collective-permute-start | bytes 3538952 | tf_op jit(solution)/shard_map/ppermute | solution.py:546
  115.5 31.5 %collective-permute-start.38 = (bf16[8,96,768]{2,1,0:T(8,128)(2,1)S(1)}, bf16[8,96,768]{2,1,0:T(8,128)(2,1)S(1)}, u32[]{:S(2)}, u32[]{:S(2)}) collective-permute-start(bf16[8,96,768]{2,1,0:T(8,128)(2,1)S(1)} %add_convert_fusion.1), channel_id=1, source_target_pairs={{0,4},{1,5},{2,6},{3,7},{4,0},{5,1},{6,2},{7,3},{8,12},{9,13},{10,... | collective-permute-start | bytes 3538952 | tf_op jit(solution)/shard_map/ppermute | solution.py:546
  130.2 11.6 %collective-permute-start.32 = (bf16[16,96,768]{2,1,0:T(8,128)(2,1)S(1)}, bf16[16,96,768]{2,1,0:T(8,128)(2,1)S(1)}, u32[]{:S(2)}, u32[]{:S(2)}) collective-permute-start(bf16[16,96,768]{2,1,0:T(8,128)(2,1)S(1)} %get-tuple-element.161), channel_id=1, source_target_pairs={{0,1},{1,0},{2,3},{3,2},{4,5},{5,4},{6,7},{7,6},{8,9},{9,8},{10,11... | collective-permute-start | bytes 7077896 | tf_op jit(solution)/shard_map/ppermute | solution.py:532
  142.2 15.8 %collective-permute-start.33 = (bf16[8,96,768]{2,1,0:T(8,128)(2,1)S(1)}, bf16[8,96,768]{2,1,0:T(8,128)(2,1)S(1)}, u32[]{:S(2)}, u32[]{:S(2)}) collective-permute-start(bf16[8,96,768]{2,1,0:T(8,128)(2,1)S(1)} %add_convert_fusion), channel_id=1, source_target_pairs={{0,2},{1,5},{2,0},{3,7},{4,6},{5,1},{6,4},{7,3},{8,10},{9,13},{10,... | collective-permute-start | bytes 3538952 | tf_op jit(solution)/shard_map/ppermute | solution.py:546
  146.7 13.2 %collective-permute-start.44 = (f32[24,768]{1,0:T(8,128)S(1)}, f32[24,768]{1,0:T(8,128)S(1)}, u32[]{:S(2)}, u32[]{:S(2)}) collective-permute-start(f32[24,768]{1,0:T(8,128)S(1)} %get-tuple-element.182), channel_id=1, source_target_pairs={{0,1},{1,0},{2,3},{3,2},{4,5},{5,4},{6,7},{7,6},{8,9},{9,8},{10,11... | collective-permute-start | bytes 221192 | tf_op jit(solution)/shard_map/ppermute | solution.py:466
  149.5 23.2 %collective-permute-start.39 = (bf16[4,96,768]{2,1,0:T(8,128)(2,1)}, bf16[4,96,768]{2,1,0:T(8,128)(2,1)}, u32[]{:S(2)}, u32[]{:S(2)}) collective-permute-start(bf16[4,96,768]{2,1,0:T(8,128)(2,1)} %add_convert_fusion.3), channel_id=1, source_target_pairs={{0,8},{1,9},{2,10},{3,11},{4,12},{5,13},{6,14},{7,15},{8,0},{9,1},... | collective-permute-start | bytes 1769480 | tf_op jit(solution)/shard_map/ppermute | solution.py:546
  152.6 20.1 %collective-permute-start.42 = (bf16[2,96,768]{2,1,0:T(8,128)(2,1)}, bf16[2,96,768]{2,1,0:T(8,128)(2,1)}, u32[]{:S(2)}, u32[]{:S(2)}) collective-permute-start(bf16[2,96,768]{2,1,0:T(8,128)(2,1)} %add_convert_fusion.6), channel_id=1, source_target_pairs={{0,16},{1,17},{2,18},{3,19},{4,20},{5,21},{6,22},{7,23},{8,24},{9,... | collective-permute-start | bytes 884744 | tf_op jit(solution)/shard_map/ppermute | solution.py:546
  159.0 18.5 %collective-permute-start.34 = (bf16[4,96,768]{2,1,0:T(8,128)(2,1)}, bf16[4,96,768]{2,1,0:T(8,128)(2,1)}, u32[]{:S(2)}, u32[]{:S(2)}) collective-permute-start(bf16[4,96,768]{2,1,0:T(8,128)(2,1)} %add_convert_fusion.4), channel_id=1, source_target_pairs={{0,4},{1,3},{2,6},{3,1},{4,0},{5,7},{6,2},{7,5},{8,12},{9,11},{10,... | collective-permute-start | bytes 1769480 | tf_op jit(solution)/shard_map/ppermute | solution.py:546
  179.2 12.0 %collective-permute-start.47 = (f32[24,768]{1,0:T(8,128)S(1)}, f32[24,768]{1,0:T(8,128)S(1)}, u32[]{:S(2)}, u32[]{:S(2)}) collective-permute-start(f32[24,768]{1,0:T(8,128)S(1)} %add.298), channel_id=1, source_target_pairs={{0,8},{1,9},{2,10},{3,11},{4,12},{5,13},{6,14},{7,15},{8,0},{9,1},... | collective-permute-start | bytes 221192 | tf_op jit(solution)/shard_map/ppermute | solution.py:466
  187.6 12.3 %collective-permute-start.36 = (bf16[1,96,768]{2,1,0:T(8,128)(2,1)S(1)}, bf16[1,96,768]{2,1,0:T(8,128)(2,1)S(1)}, u32[]{:S(2)}, u32[]{:S(2)}) collective-permute-start(bf16[1,96,768]{2,1,0:T(8,128)(2,1)S(1)} %get-tuple-element.199), channel_id=1, source_target_pairs={{0,8},{1,17},{2,10},{3,19},{4,12},{5,21},{6,14},{7,23},{8,0},{9,25... | collective-permute-start | bytes 442376 | tf_op jit(solution)/shard_map/ppermute | solution.py:554
  (73 other events, 924.9 us)
